TPU v7x, 32 devices: a whole 2x2x4 slice. The times are simulated.
32 devices in a mesh: img: 16 (over z, y, core), tok: 2 (over x).
Axes of the slice: x: 2, y: 2, z: 4, core: 2. Of those that a mesh axis runs over, the one named last changes fastest.
Arguments:
- tokens: bfloat16 [16, 256, 1280], P('img', 'tok'), may hold values from -6 to 6
- grad_out: bfloat16 [16, 256, 1280], P('img', 'tok'), may hold values from -6 to 6
- router: bfloat16 [1280, 8], replicated, may hold values from -0.15625 to 0.15625
- slot_scale: float32 [8], replicated, may hold values from 1 to 8
- w_in: bfloat16 [16, 1280, 2048], P('img', None, 'tok'), may hold values from -0.15625 to 0.15625
- w_out: bfloat16 [16, 2048, 1280], P('img', 'tok'), may hold values from -0.09375 to 0.09375
Outputs:
- combined: bfloat16 [16, 256, 1280], P('img', 'tok')
- grad_tokens: bfloat16 [16, 256, 1280], P('img', 'tok')
- grad_router: float32 [1280, 8], replicated
- grad_scale: float32 [8], replicated
- grad_w_in: bfloat16 [16, 1280, 2048], P('img', None, 'tok')
- grad_w_out: bfloat16 [16, 2048, 1280], P('img', 'tok')
All inputs are finite; a program needn't handle non-finite values.
Results may differ from a plain program's by a relative error of at most 0.015.
Values may be sent and summed in bfloat16 or wider, within the bound.
No kernel may reach another device: no remote copies, remote signals or barrier semaphores. Data moves between devices by JAX's collectives and lax.ppermute only.
A program may use at most 64 MiB of HBM per device.

v0:
```python
import jax
import jax.numpy as jnp
from jax import lax
from jax.sharding import PartitionSpec as P

EPSILON = 1e-06
ROOT_HALF = 0.7071067811865476
DENSITY = 0.3989422804014327


def gelu_value(values):
    return values * (0.5 * (1.0 + lax.erf(values * ROOT_HALF)))


def gelu_slope(values):
    return (
        0.5 * (1.0 + lax.erf(values * ROOT_HALF))
        + values * jnp.exp(-0.5 * values * values) * DENSITY
    )


def token_total(term):
    return lax.psum(term, "tok")


def route_rows(block):
    moved = lax.all_to_all(block, "img", split_axis=0, concat_axis=0, tiled=True)
    return moved


def token_stats(term):
    return lax.psum(term, "tok")


def contract_first(left, right):
    return lax.dot_general(
        left, right, (((0,), (0,)), ((), ())), preferred_element_type=jnp.float32
    )


def contract_last(left, right):
    return lax.dot_general(
        left, right, (((1,), (1,)), ((), ())), preferred_element_type=jnp.float32
    )


def to_experts(rows_bf):
    return route_rows(jnp.concatenate([rows_bf, rows_bf], 0))


def join_halves(term):
    summed = token_total(term).astype(jnp.bfloat16)
    back = route_rows(summed)
    experts = back.shape[0] // 2
    return (back[:experts].astype(jnp.float32) + back[experts:].astype(jnp.float32)).astype(
        jnp.bfloat16
    )


def shards(tokens, grad_out, router, slot_scale, w_in, w_out):
    single = jnp.float32
    half_type = jnp.bfloat16
    images_dev, tok_rows, model_width = tokens.shape
    flat_tokens = tokens.reshape(-1, model_width)
    grad_flat = grad_out.reshape(-1, model_width)
    weight_one = w_in[0]
    weight_two = w_out[0]
    router_f = router.astype(single)
    inv_p = lax.rsqrt(jnp.sum(router_f * router_f, 0) + EPSILON)
    column = inv_p * slot_scale
    tokens_f = flat_tokens.astype(single)
    inv_x = lax.rsqrt(jnp.sum(tokens_f * tokens_f, 1) + EPSILON)
    raw = jnp.dot(flat_tokens, router, preferred_element_type=single)
    logit = raw * inv_x[:, None] * column[None, :]
    expo = jnp.exp(logit)
    den = token_stats(jnp.sum(expo, 0))
    weights_b = expo.astype(half_type)
    numer = contract_first(weights_b, flat_tokens)
    slots = (token_total(numer) / den[:, None]).astype(half_type)
    rows = to_experts(slots)
    act = jnp.dot(rows, weight_one, preferred_element_type=single)
    hidden = gelu_value(act).astype(half_type)
    partial_out = jnp.dot(hidden, weight_two, preferred_element_type=single)
    ys = join_halves(partial_out)
    comb = expo / jnp.sum(expo, 1, keepdims=True)
    comb_b = comb.astype(half_type)
    combined = jnp.dot(comb_b, ys, preferred_element_type=single).astype(half_type)
    dys_part = contract_first(comb_b, grad_flat)
    dys = token_total(dys_part).astype(half_type)
    grad_rows = to_experts(dys)
    dcomb = contract_last(grad_flat, ys)
    dlc = comb * (dcomb - jnp.sum(comb * dcomb, 1, keepdims=True))
    grad_h = contract_last(grad_rows, weight_two)
    dact = (grad_h * gelu_slope(act)).astype(half_type)
    grad_w_in = contract_first(rows, dact).astype(half_type)[None]
    grad_w_out = contract_first(hidden, grad_rows).astype(half_type)[None]
    partial_in = contract_last(dact, weight_one)
    dxs = join_halves(partial_in)
    ddisp = contract_last(flat_tokens, dxs)
    disp_w = expo / den[None, :]
    corr = token_stats(jnp.sum(disp_w * ddisp, 0))
    grad_l = disp_w * (ddisp - corr[None, :]) + dlc
    product = grad_l * logit
    signal = jnp.sum(product, 1)
    grad_q = (grad_l * column[None, :] * inv_x[:, None]).astype(half_type)
    scaled = (dxs.astype(single) / den[:, None]).astype(half_type)
    grad_tokens = jnp.dot(weights_b, scaled, preferred_element_type=single)
    grad_tokens = grad_tokens + contract_last(grad_q, router)
    grad_tokens = grad_tokens - (inv_x * inv_x * signal)[:, None] * tokens_f
    outer = contract_first(flat_tokens, grad_q)
    total = jnp.sum(product, 0)
    outer, total = lax.psum((outer, total), ("img", "tok"))
    grad_router = outer - (inv_p * inv_p * total)[None, :] * router_f
    grad_scale = total / slot_scale
    grad_tokens = grad_tokens.astype(half_type).reshape(images_dev, tok_rows, model_width)
    combined = combined.reshape(images_dev, tok_rows, model_width)
    return (combined, grad_tokens, grad_router, grad_scale, grad_w_in, grad_w_out)


def solution(mesh):
    return jax.shard_map(
        shards,
        mesh=mesh,
        in_specs=(
            P("img", "tok", None),
            P("img", "tok", None),
            P(),
            P(),
            P("img", None, "tok"),
            P("img", "tok", None),
        ),
        out_specs=(
            P("img", "tok", None),
            P("img", "tok", None),
            P(),
            P(),
            P("img", None, "tok"),
            P("img", "tok", None),
        ),
        check_vma=False,
    )
```

profile of v0, /device:TPU:0, one launch (start us, length us, event | category | flops | bytes accessed | tf_op | source)
XLA Modules:
  0.0 127.4 jit_solution(9836334680248036418)
XLA Ops:
  0.6 1.0 fusion.34
  1.7 1.1 fusion.21
  3.5 1.3 %exponential_reduce_fusion.1 = (f32[128]{0:T(128)S(1)}, f32[8]{0:T(128)S(1)}, f32[128,8]{0,1:T(8,128)S(1)}) fusion(f32[8]{0:T(128)S(1)} %fusion.50, f32[128]{0:T(128)S(1)} %add_rsqrt_fusion.1, bf16[1280,8]{0,1:T(8,128)(2,1)} %param.8, bf16[1,128,1280]{2,1,0:T(8,128)(2,1)} %param.6), kind=kOutput, calls=%fused_computation.75 | convolution fusion | flops 2625400 | bytes 353344 | tf_op jit(solution)/shard_map/dot_general | solution.py:73
  4.8 1.1 fusion.27
  5.9 1.1 fusion.23
  7.0 10.7 %all-reduce.2 = (f32[8,1280]{1,0:T(8,128)S(1)}, f32[8]{0:T(128)S(1)}, bf16[8,1280]{1,0:T(8,128)(2,1)S(1)}) all-reduce(f32[8,1280]{1,0:T(8,128)S(1)} %fusion.27, f32[8]{0:T(128)S(1)} %get-tuple-element.11, f32[8,1280]{1,0:T(8,128)S(1)} %fusion.23), channel_id=1, replica_groups=mesh['img'=16,'tok'=2] {'tok'}, use_global_device_ids=true, to_apply=%region_3.0 | all-reduce | flops 20488 | bytes 143424 | tf_op jit(solution)/shard_map/psum | solution.py:23
  19.7 5.8 %all-to-all-start = ((bf16[16,2,640]{2,1,0:T(2,128)(2,1)}), bf16[16,2,640]{2,1,0:T(2,128)(2,1)S(1)}, u32[]{:S(2)}, u32[]{:S(2)}) async-start(bf16[16,2,640]{2,1,0:T(2,128)(2,1)} %reshape.69), calls=%async_computation | async-start | bytes 81920 | tf_op jit(solution)/shard_map/all_to_all | solution.py:27
  26.7 5.4 %all-to-all-done = bf16[16,2,640]{2,1,0:T(2,128)(2,1)S(1)} async-done(((bf16[16,2,640]{2,1,0:T(2,128)(2,1)}), bf16[16,2,640]{2,1,0:T(2,128)(2,1)S(1)}, u32[]{:S(2)}, u32[]{:S(2)}) %all-to-all-start) | async-done | bytes 40992 | tf_op jit(solution)/shard_map/all_to_all | solution.py:27
  32.1 3.5 %all-to-all-start.2 = ((bf16[16,2,640]{2,1,0:T(2,128)(2,1)}), bf16[16,2,640]{2,1,0:T(2,128)(2,1)S(1)}, u32[]{:S(2)}, u32[]{:S(2)}) async-start(bf16[16,2,640]{2,1,0:T(2,128)(2,1)} %reshape.73), calls=%async_computation.2 | async-start | bytes 81920 | tf_op jit(solution)/shard_map/all_to_all | solution.py:27
  35.7 2.2 %fusion.8 = f32[16,1024]{1,0:T(8,128)S(1)} fusion(bf16[1,1280,1024]{2,1,0:T(8,128)(2,1)} %param.10, bf16[16,1,1280]{2,1,0:T(2,128)(2,1)S(1)} %reshape.70), kind=kOutput, calls=%fused_computation.10 | convolution fusion | flops 41943040 | bytes 2727936 | tf_op jit(solution)/shard_map/dot_general | solution.py:81
  38.3 4.0 %all-to-all-done.2 = bf16[16,2,640]{2,1,0:T(2,128)(2,1)S(1)} async-done(((bf16[16,2,640]{2,1,0:T(2,128)(2,1)}), bf16[16,2,640]{2,1,0:T(2,128)(2,1)S(1)}, u32[]{:S(2)}, u32[]{:S(2)}) %all-to-all-start.2) | async-done | bytes 40992 | tf_op jit(solution)/shard_map/all_to_all | solution.py:27
  42.4 0.8 fusion.17
  43.1 2.4 %fusion.1 = bf16[1,1024,1280]{2,1,0:T(8,128)(2,1)} fusion(bf16[16,1,1280]{2,1,0:T(2,128)(2,1)S(1)} %reshape.74, f32[16,1024]{1,0:T(8,128)S(1)} %fusion.8), kind=kOutput, calls=%fused_computation.3 | convolution fusion | flops 43335680 | bytes 2727936 | tf_op jit(solution)/shard_map/dot_general | solution.py:36
  46.3 9.1 %all-reduce.4 = (bf16[16,1280]{1,0:T(8,128)(2,1)S(1)}, bf16[16,1280]{1,0:T(8,128)(2,1)S(1)}) all-reduce(f32[16,1280]{1,0:T(8,128)S(1)} %fusion.4, f32[16,1280]{1,0:T(8,128)S(1)} %fusion.6), channel_id=1, replica_groups=mesh['img'=16,'tok'=2] {'tok'}, use_global_device_ids=true, to_apply=%region_6.0 | all-reduce | flops 40960 | bytes 245760 | tf_op jit(solution)/shard_map/psum | solution.py:23
  58.1 3.5 %all-to-all-start.1 = ((bf16[16,2,640]{2,1,0:T(2,128)(2,1)}), bf16[16,2,640]{2,1,0:T(2,128)(2,1)S(1)}, u32[]{:S(2)}, u32[]{:S(2)}) async-start(bf16[16,2,640]{2,1,0:T(2,128)(2,1)} %reshape.71), calls=%async_computation.1 | async-start | bytes 81920 | tf_op jit(solution)/shard_map/all_to_all | solution.py:27
  61.6 2.4 %fusion = bf16[1,1280,1024]{2,1,0:T(8,128)(2,1)} fusion(bf16[16,1024]{1,0:T(8,128)(2,1)S(1)} %fusion.17, bf16[16,1,1280]{2,1,0:T(2,128)(2,1)S(1)} %reshape.70), kind=kOutput, calls=%fused_computation.2 | convolution fusion | flops 43253760 | bytes 2695168 | tf_op jit(solution)/shard_map/dot_general | solution.py:36
  64.0 4.3 %all-to-all-done.1 = bf16[16,2,640]{2,1,0:T(2,128)(2,1)S(1)} async-done(((bf16[16,2,640]{2,1,0:T(2,128)(2,1)}), bf16[16,2,640]{2,1,0:T(2,128)(2,1)S(1)}, u32[]{:S(2)}, u32[]{:S(2)}) %all-to-all-start.1) | async-done | bytes 40992 | tf_op jit(solution)/shard_map/all_to_all | solution.py:27
  68.2 3.5 %all-to-all-start.3 = ((bf16[16,2,640]{2,1,0:T(2,128)(2,1)}), bf16[16,2,640]{2,1,0:T(2,128)(2,1)S(1)}, u32[]{:S(2)}, u32[]{:S(2)}) async-start(bf16[16,2,640]{2,1,0:T(2,128)(2,1)} %reshape.75), calls=%async_computation.3 | async-start | bytes 81920 | tf_op jit(solution)/shard_map/all_to_all | solution.py:27
  72.0 1.1 fusion.13
  73.1 5.3 %all-to-all-done.3 = bf16[16,2,640]{2,1,0:T(2,128)(2,1)S(1)} async-done(((bf16[16,2,640]{2,1,0:T(2,128)(2,1)}), bf16[16,2,640]{2,1,0:T(2,128)(2,1)S(1)}, u32[]{:S(2)}, u32[]{:S(2)}) %all-to-all-start.3) | async-done | bytes 40992 | tf_op jit(solution)/shard_map/all_to_all | solution.py:27
  78.5 1.2 fusion.40
  80.0 4.9 %psum.61 = f32[8]{0:T(128)S(1)} all-reduce(f32[8]{0:T(128)S(1)} %get-tuple-element.8), channel_id=1, replica_groups=mesh['img'=16,'tok'=2] {'tok'}, use_global_device_ids=true, to_apply=%region_10.0 | all-reduce | flops 8 | bytes 64 | tf_op jit(solution)/shard_map/psum | solution.py:32
  85.4 38.6 %all-reduce = (f32[1280,8]{0,1:T(8,128)S(1)}, f32[8]{0:T(128)S(1)}) all-reduce(f32[1280,8]{0,1:T(8,128)S(1)} %convolution_bitcast_fusion, f32[8]{0:T(128)S(1)} %get-tuple-element.6), channel_id=1, replica_groups=mesh['img'=16,'tok'=2] {'img','tok'}, use_global_device_ids=true, to_apply=%region_13.0 | all-reduce | flops 10248 | bytes 81984 | tf_op jit(solution)/shard_map/psum | solution.py:112
  125.2 2.2 %fusion.12 = bf16[1,128,1280]{2,1,0:T(8,128)(2,1)} fusion(f32[128,1280]{1,0:T(8,128)} %fusion.40, bf16[1280,8]{0,1:T(8,128)(2,1)S(1)} %copy-done.4, bf16[1,128,1280]{2,1,0:T(8,128)(2,1)S(1)} %copy-done.2, f32[128]{0:T(128)S(1)} %multiply_multiply_fusion.2, f32[128,8]{0,1:T(8,128)S(1)} %get-tuple-element.19, f32[8]{0:T(128)S(1)} %fusion.50, ...), kind=kOutput, calls=%fused_computation.16 | convolution fusion | flops 3443712 | bytes 1336352 | tf_op jit(solution)/shard_map/dot_general | solution.py:42
  (49 shorter events, 10.2 us)
Async XLA Ops:
  0.6 37.2 %copy-start = (bf16[1,1024,1280]{2,1,0:T(8,128)(2,1)S(1)}, bf16[1,1024,1280]{2,1,0:T(8,128)(2,1)}, u32[]{:S(2)}) copy-start(bf16[1,1024,1280]{2,1,0:T(8,128)(2,1)} %param.11) | copy-start | bytes 7864324
  1.6 5.4 %copy-start.5 = (f32[8]{0:T(128)}, f32[8]{0:T(128)S(1)}, u32[]{:S(2)}) copy-start(f32[8]{0:T(128)S(1)} %fusion.34) | copy-start | bytes 100
  2.8 4.3 %copy-start.7 = (f32[128]{0:T(128)}, f32[128]{0:T(128)S(1)}, u32[]{:S(2)}) copy-start(f32[128]{0:T(128)S(1)} %fusion.21) | copy-start | bytes 1540
  19.7 12.5 %all-to-all-start = ((bf16[16,2,640]{2,1,0:T(2,128)(2,1)}), bf16[16,2,640]{2,1,0:T(2,128)(2,1)S(1)}, u32[]{:S(2)}, u32[]{:S(2)}) async-start(bf16[16,2,640]{2,1,0:T(2,128)(2,1)} %reshape.69), calls=%async_computation | async-start | bytes 81920 | tf_op jit(solution)/shard_map/all_to_all | solution.py:27
  32.1 10.2 %all-to-all-start.2 = ((bf16[16,2,640]{2,1,0:T(2,128)(2,1)}), bf16[16,2,640]{2,1,0:T(2,128)(2,1)S(1)}, u32[]{:S(2)}, u32[]{:S(2)}) async-start(bf16[16,2,640]{2,1,0:T(2,128)(2,1)} %reshape.73), calls=%async_computation.2 | async-start | bytes 81920 | tf_op jit(solution)/shard_map/all_to_all | solution.py:27
  42.3 3.2 %copy-start.1 = (bf16[1,1280,1024]{2,1,0:T(8,128)(2,1)S(1)}, bf16[1,1280,1024]{2,1,0:T(8,128)(2,1)}, u32[]{:S(2)}) copy-start(bf16[1,1280,1024]{2,1,0:T(8,128)(2,1)} %param.10) | copy-start | bytes 7864324
  45.5 26.3 %copy-start.3 = (bf16[1,128,1280]{2,1,0:T(8,128)(2,1)S(1)}, bf16[1,128,1280]{2,1,0:T(8,128)(2,1)}, u32[]{:S(2)}) copy-start(bf16[1,128,1280]{2,1,0:T(8,128)(2,1)} %param.7) | copy-start | bytes 983044
  55.4 24.3 %copy-start.2 = (bf16[1,128,1280]{2,1,0:T(8,128)(2,1)S(1)}, bf16[1,128,1280]{2,1,0:T(8,128)(2,1)}, u32[]{:S(2)}) copy-start(bf16[1,128,1280]{2,1,0:T(8,128)(2,1)} %param.6) | copy-start | bytes 983044
  58.1 10.2 %all-to-all-start.1 = ((bf16[16,2,640]{2,1,0:T(2,128)(2,1)}), bf16[16,2,640]{2,1,0:T(2,128)(2,1)S(1)}, u32[]{:S(2)}, u32[]{:S(2)}) async-start(bf16[16,2,640]{2,1,0:T(2,128)(2,1)} %reshape.71), calls=%async_computation.1 | async-start | bytes 81920 | tf_op jit(solution)/shard_map/all_to_all | solution.py:27
  61.6 23.6 %copy-start.8 = (f32[128]{0:T(128)S(1)}, f32[128]{0:T(128)}, u32[]{:S(2)}) copy-start(f32[128]{0:T(128)} %copy-done.7) | copy-start | bytes 1540
  61.6 62.4 %copy-start.6 = (f32[8]{0:T(128)S(1)}, f32[8]{0:T(128)}, u32[]{:S(2)}) copy-start(f32[8]{0:T(128)} %copy-done.5) | copy-start | bytes 100
  61.6 62.4 %copy-start.9 = (f32[8]{0:T(128)S(1)}, f32[8]{0:T(128)}, u32[]{:S(2)}) copy-start(f32[8]{0:T(128)} %param.9) | copy-start | bytes 100
  61.6 62.9 %copy-start.4 = (bf16[1280,8]{0,1:T(8,128)(2,1)S(1)}, bf16[1280,8]{0,1:T(8,128)(2,1)}, u32[]{:S(2)}) copy-start(bf16[1280,8]{0,1:T(8,128)(2,1)} %param.8) | copy-start | bytes 61444
  68.2 10.2 %all-to-all-start.3 = ((bf16[16,2,640]{2,1,0:T(2,128)(2,1)}), bf16[16,2,640]{2,1,0:T(2,128)(2,1)S(1)}, u32[]{:S(2)}, u32[]{:S(2)}) async-start(bf16[16,2,640]{2,1,0:T(2,128)(2,1)} %reshape.75), calls=%async_computation.3 | async-start | bytes 81920 | tf_op jit(solution)/shard_map/all_to_all | solution.py:27
where the time goes:
time: 128 us; the launch traced here: 127 us
  blocking collectives  63.3 us (49%)
  waiting for transfers between devices  18.9 us (15%)
  matrix products  17.7 us (14%)
  starting transfers between devices  16.3 us (13%)
  other arithmetic  6.95 us (5%)
  local copies, waits for them, and re-layouts  3.42 us (3%)
    psum x1, blocking collectives, shards(): outer, total = lax.psum((outer, total), ('img', 'tok'))  38.6 us
    psum x2, blocking collectives, token_total(): return lax.psum(term, 'tok')  19.8 us
    all_to_all x4, waiting for transfers between devices, route_rows(): lax.all_to_all(block, 'img', split_axis=0, concat_axis=0, tiled=True)  18.9 us
    all_to_all x4, starting transfers between devices, route_rows(): lax.all_to_all(block, 'img', split_axis=0, concat_axis=0, tiled=True)  16.3 us
    dot_general x5, matrix products, contract_first(): lax.dot_general(left, right, (((0,), (0,)), ((), ())), preferred_element_...  7.23 us
    psum x1, blocking collectives, token_stats(): return lax.psum(term, 'tok')  4.94 us
    dot_general x5, matrix products, contract_last(): lax.dot_general(left, right, (((1,), (1,)), ((), ())), preferred_element_...  4.21 us
    unnamed x28, local copies, waits for them, and re-layouts  2.73 us
  transfers between devices with their start and end apart: 4, of which 4 were waited for; matrix products, arithmetic and copies ran while one was open for 6% of the time, Pallas kernels for 0%

commit v1 on v0

v1 whole, which is shorter than its diff:
```python
import functools

import jax
import jax.numpy as jnp
from jax import lax
from jax.experimental import pallas as pl
from jax.experimental.pallas import tpu as pltpu
from jax.sharding import PartitionSpec as P

EPSILON = 1e-06
ROOT_HALF = 0.7071067811865476
DENSITY = 0.3989422804014327
BF = jnp.bfloat16
F32 = jnp.float32
BOTH = ("img", "tok")
LANES = 128


def dot(left, right, dims):
    return lax.dot_general(left, right, (dims, ((), ())), preferred_element_type=F32)


def log2(size):
    assert size & (size - 1) == 0
    return size.bit_length() - 1


def iota(shape, axis):
    return lax.broadcasted_iota(jnp.int32, shape, axis)


def selection(shape, row_key, column_key):
    hit = row_key(iota(shape, 0)) == column_key(iota(shape, 1))
    return jnp.where(hit, 1.0, 0.0).astype(BF)


def stacked_key(count):
    return lambda row: row


def by_image(images, halves):
    return lambda row: (row & 1) * images + (row >> (1 + log2(halves)))


def by_expert(experts, halves):
    return lambda row: (row & 1) * experts + ((row >> (1 + log2(halves))) & (experts - 1))


def as_column(row):
    size = row.shape[1]
    eye = iota((size, size), 0) == iota((size, size), 1)
    return jnp.sum(jnp.where(eye, row, 0.0), 1, keepdims=True)


def row_of(column):
    return jnp.transpose(jnp.broadcast_to(column, (column.shape[0], LANES)))[:1]


def stack_rows(first, second, extras):
    lane = iota((first.shape[0], LANES), 1)
    high = jnp.zeros(lane.shape, F32)
    low = jnp.zeros(lane.shape, F32)
    for place, value in enumerate(extras):
        top = value.astype(BF).astype(F32)
        high = jnp.where(lane == place, top, high)
        low = jnp.where(lane == place, value - top, low)
    return jnp.concatenate(
        [jnp.concatenate([first, high], 1), jnp.concatenate([second, low], 1)], 0
    ).astype(BF)


def slot_column(router_ref, scale_ref):
    router_f = router_ref[...].astype(F32)
    inv_p = lax.rsqrt(jnp.sum(router_f * router_f, 1, keepdims=True) + EPSILON)
    scale = as_column(scale_ref[...])
    return router_f, inv_p, scale


def softmax(logit):
    expo = jnp.exp(logit)
    return expo, expo / jnp.sum(expo, 0, keepdims=True)


def front_kernel(halves, tok_ref, grad_ref, router_ref, scale_ref, sent_ref, logit_ref, inv_ref):
    experts = router_ref.shape[0]
    tok = tok_ref[0]
    tok_f = tok.astype(F32)
    inv_x = row_of(lax.rsqrt(jnp.sum(tok_f * tok_f, 1, keepdims=True) + EPSILON))
    _, inv_p, scale = slot_column(router_ref, scale_ref)
    raw = dot(router_ref[...], tok, ((1,), (1,)))
    logit = raw * inv_x * (inv_p * scale)
    expo, comb = softmax(logit)
    numer = dot(expo.astype(BF), tok, ((1,), (0,)))
    dys = dot(comb.astype(BF), grad_ref[0], ((1,), (0,)))
    rows = stack_rows(numer, dys, [jnp.sum(expo, 1, keepdims=True)])
    spread = selection(
        (sent_ref.shape[0], 2 * experts), by_expert(experts, halves), stacked_key(experts)
    )
    sent_ref[...] = dot(spread, rows, ((1,), (0,))).astype(BF)
    logit_ref[...] = logit
    inv_ref[...] = inv_x


def expert_kernel(
    images, halves, got_ref, one_ref, two_ref, back_ref, rows_ref, grad_rows_ref, hidden_ref, dact_ref
):
    width = one_ref.shape[1]
    gather = selection(
        (2 * images, got_ref.shape[0]), stacked_key(images), by_image(images, halves)
    )
    sums = dot(gather, got_ref[...], ((1,), (0,)))
    den = sums[:images, width : width + 1] + sums[images:, width : width + 1]
    rows = (sums[:images, :width] / den).astype(BF)
    grad_rows = sums[images:, :width].astype(BF)
    act = dot(rows, one_ref[0], ((1,), (0,)))
    grad_h = dot(grad_rows, two_ref[0], ((1,), (1,)))
    phi = 0.5 * (1.0 + lax.erf(act * ROOT_HALF))
    hidden = (act * phi).astype(BF)
    dact = (grad_h * (phi + act * jnp.exp(-0.5 * act * act) * DENSITY)).astype(BF)
    out_part = dot(hidden, two_ref[0], ((1,), (0,)))
    in_part = dot(dact, one_ref[0], ((1,), (1,)))
    corr = jnp.sum(dact.astype(F32) * act, 1, keepdims=True)
    spread = selection(
        (back_ref.shape[0], 2 * images), by_image(images, halves), stacked_key(images)
    )
    packed = stack_rows(out_part, in_part, [den, corr])
    back_ref[...] = dot(spread, packed, ((1,), (0,))).astype(BF)
    rows_ref[...] = rows
    grad_rows_ref[...] = grad_rows
    hidden_ref[...] = hidden
    dact_ref[...] = dact


def middle_kernel(
    halves, copies, back_ref, tok_ref, grad_ref, logit_ref, inv_ref, router_ref, scale_ref,
    sums_ref, outs_ref, coef_ref, mix_ref, signal_ref,
):
    experts, width = router_ref.shape
    gather = selection(
        (2 * experts, back_ref.shape[0]), stacked_key(experts), by_expert(experts, halves)
    )
    sums = dot(gather, back_ref[...], ((1,), (0,)))
    extras = sums[:experts, width:] + sums[experts:, width:]
    den = extras[:, :1] * (1.0 / (copies * halves))
    corr = extras[:, 1:2]
    ys = sums[:experts, :width].astype(BF)
    dxs = sums[experts:, :width].astype(BF)
    router_f, inv_p, scale = slot_column(router_ref, scale_ref)
    tok = tok_ref[0]
    logit = logit_ref[...]
    inv_x = inv_ref[...]
    expo, comb = softmax(logit)
    dcomb = dot(ys, grad_ref[0], ((1,), (1,)))
    ddisp = dot(dxs, tok, ((1,), (1,)))
    dlc = comb * (dcomb - jnp.sum(comb * dcomb, 0, keepdims=True))
    grad_l = expo / den * (ddisp - corr) + dlc
    product = grad_l * logit
    grad_q = (grad_l * inv_x * (inv_p * scale)).astype(BF)
    outer = dot(grad_q, tok, ((1,), (0,)))
    total = jnp.sum(product, 1, keepdims=True)
    local = outer - inv_p * inv_p * total * router_f
    lane = iota((experts, LANES), 1)
    sums_ref[...] = jnp.concatenate([local, jnp.where(lane == 0, total / scale, 0.0)], 1)
    outs_ref[...] = ys
    coef_ref[...] = jnp.concatenate([expo, grad_q.astype(F32)], 0).astype(BF)
    mix_ref[...] = jnp.concatenate([dxs.astype(F32) / den, router_f], 0).astype(BF)
    signal_ref[...] = inv_x * inv_x * jnp.sum(product, 0, keepdims=True)


def tail_kernel(tok_ref, logit_ref, outs_ref, coef_ref, mix_ref, signal_ref, combined_ref, grads_ref):
    _, comb = softmax(logit_ref[...])
    combined_ref[0] = dot(comb.astype(BF), outs_ref[...], ((0,), (0,))).astype(BF)
    signal = signal_ref[...]
    column = jnp.transpose(jnp.broadcast_to(signal, (LANES, signal.shape[1])))[:, :1]
    grads = dot(coef_ref[...], mix_ref[...], ((0,), (0,)))
    grads_ref[0] = (grads - column * tok_ref[0].astype(F32)).astype(BF)


def call(kernel, outs, *args, flops=10**7, room=24 * 2**20):
    return pl.pallas_call(
        kernel,
        out_shape=[jax.ShapeDtypeStruct(shape, dtype) for shape, dtype in outs],
        in_specs=[pl.BlockSpec(memory_space=pltpu.VMEM)] * len(args),
        out_specs=[pl.BlockSpec(memory_space=pltpu.VMEM)] * len(outs),
        compiler_params=pltpu.CompilerParams(vmem_limit_bytes=room),
        cost_estimate=pl.CostEstimate(
            flops=flops, bytes_accessed=sum(a.size * a.dtype.itemsize for a in args), transcendentals=0
        ),
    )(*args)


def exchange(block, devices):
    moved = lax.all_to_all(
        block.reshape(devices, 2, block.shape[1]), BOTH, split_axis=0, concat_axis=0, tiled=True
    )
    return moved.reshape(block.shape)


def pair(term, mask, devices):
    return lax.ppermute(term, BOTH, [(d, d ^ mask) for d in range(devices)])


def sum_everywhere(term, devices):
    bits = [1 << place for place in range(log2(devices))]
    chip_bits = [bits[0]] + bits[2:]
    term = term + pair(term, bits[1], devices)
    for place in range(0, len(chip_bits), 2):
        group = chip_bits[place : place + 2]
        sent = term.astype(BF)
        near = sent.astype(F32) + pair(sent, group[0], devices).astype(F32)
        if len(group) == 2:
            far = pair(sent, group[1], devices).astype(F32)
            far = far + pair(sent, group[0] ^ group[1], devices).astype(F32)
            near = near + far
        term = near
    return term


def shards(images, halves, tokens, grad_out, router, slot_scale, w_in, w_out):
    devices = images * halves
    tok_rows, width = tokens.shape[1:]
    experts = router.shape[1]
    copies = images // experts
    hidden_dev = w_in.shape[2]
    long = width + LANES
    router_t = router.T
    scale_row = slot_scale.reshape(1, experts)
    sent, logit, inv_x = call(
        functools.partial(front_kernel, halves),
        [((2 * devices, long), BF), ((experts, tok_rows), F32), ((1, tok_rows), F32)],
        tokens, grad_out, router_t, scale_row,
    )
    got = exchange(sent, devices)
    back, rows, grad_rows, hidden, dact = call(
        functools.partial(expert_kernel, images, halves),
        [((2 * devices, long), BF), ((images, width), BF), ((images, width), BF),
         ((images, hidden_dev), BF), ((images, hidden_dev), BF)],
        got, w_in, w_out,
    )
    back = exchange(back, devices)
    grad_w_in = dot(rows, dact, ((0,), (0,))).astype(BF)[None]
    grad_w_out = dot(hidden, grad_rows, ((0,), (0,))).astype(BF)[None]
    sums, ys, coef, mix, signal = call(
        functools.partial(middle_kernel, halves, copies),
        [((experts, long), F32), ((experts, width), BF), ((2 * experts, tok_rows), BF),
         ((2 * experts, width), BF), ((1, tok_rows), F32)],
        back, tokens, grad_out, logit, inv_x, router_t, scale_row,
    )
    combined, grad_tokens = call(
        tail_kernel,
        [(tokens.shape, BF), (tokens.shape, BF)],
        tokens, logit, ys, coef, mix, signal,
    )
    sums = sum_everywhere(sums, devices)
    return (combined, grad_tokens, sums[:, :width].T, sums[:, width], grad_w_in, grad_w_out)


def solution(mesh):
    images, halves = mesh.shape["img"], mesh.shape["tok"]

    def body(*args):
        return shards(images, halves, *args)

    return jax.shard_map(
        body,
        mesh=mesh,
        in_specs=(
            P("img", "tok", None),
            P("img", "tok", None),
            P(),
            P(),
            P("img", None, "tok"),
            P("img", "tok", None),
        ),
        out_specs=(
            P("img", "tok", None),
            P("img", "tok", None),
            P(),
            P(),
            P("img", None, "tok"),
            P("img", "tok", None),
        ),
        check_vma=False,
    )
```

time: 128 us -> 56 us (0.44)
  blocking collectives: 63.3 us -> 27.6 us
  waiting for transfers between devices: 18.9 us -> 1.23 us
  matrix products: 17.7 us -> 4.73 us
  starting transfers between devices: 16.3 us -> 8.03 us
  other arithmetic: 6.95 us -> 0.04 us
  local copies, waits for them, and re-layouts: 3.42 us -> 8.34 us
  Pallas kernels: 0 us -> 4.9 us
    psum x4 -> x0, blocking collectives: 63.3 us -> none  [the longest x1 38.6 us: shards(): outer, total = lax.psum((outer, total), ('img', 'tok'))]
    all_to_all x0 -> x2, blocking collectives: none -> 27.6 us  [exchange(): lax.all_to_all(block.reshape(devices, 2, block.shape[1]), BOTH, split_axi...]
    all_to_all x4 -> x0, waiting for transfers between devices: 18.9 us -> none  [route_rows(): lax.all_to_all(block, 'img', split_axis=0, concat_axis=0, tiled=True)]
    all_to_all x4 -> x0, starting transfers between devices: 16.3 us -> none  [route_rows(): lax.all_to_all(block, 'img', split_axis=0, concat_axis=0, tiled=True)]
    dot_general x15 -> x2, matrix products: 17.7 us -> 4.73 us  [dot(): lax.dot_general(left, right, (dims, ((), ())), preferred_element_type=F32)]
    ppermute x0 -> x7, starting transfers between devices: none -> 8.03 us  [pair(): return lax.ppermute(term, BOTH, [(d, d ^ mask) for d in range(devices)])]
    pallas_call x0 -> x4, Pallas kernels: none -> 4.9 us  [call(): pl.pallas_call(kernel, out_shape=[jax.ShapeDtypeStruct(shape, dtype) for...]
    unnamed x28 -> x20, local copies, waits for them, and re-layouts: 2.73 us -> 6.81 us
  transfers between devices with their start and end apart: 4 -> 7, of which waited for: 4 -> 1; matrix products, arithmetic and copies ran while one was open for 6% -> 9% of each run, Pallas kernels for 0% -> 2%
where the time goes in v1:
time: 56 us; the launch traced here: 55.6 us
  blocking collectives  27.6 us (49%)
  local copies, waits for them, and re-layouts  8.34 us (15%)
  starting transfers between devices  8.03 us (14%)
  Pallas kernels  4.9 us (9%)
  matrix products  4.73 us (8%)
  waiting for transfers between devices  1.23 us (2%)
  between operations  0.76 us (1%)
    all_to_all x2, blocking collectives, exchange(): lax.all_to_all(block.reshape(devices, 2, block.shape[1]), BOTH, split_axi...  27.6 us
    ppermute x7, starting transfers between devices, pair(): return lax.ppermute(term, BOTH, [(d, d ^ mask) for d in range(devices)])  8.03 us
    unnamed x20, local copies, waits for them, and re-layouts  6.81 us
    pallas_call x4, Pallas kernels, call(): pl.pallas_call(kernel, out_shape=[jax.ShapeDtypeStruct(shape, dtype) for...  4.9 us
    dot_general x2, matrix products, dot(): lax.dot_general(left, right, (dims, ((), ())), preferred_element_type=F32)  4.73 us
    ppermute x7, waiting for transfers between devices, pair(): return lax.ppermute(term, BOTH, [(d, d ^ mask) for d in range(devices)])  1.23 us
  transfers between devices with their start and end apart: 7, of which 1 were waited for; matrix products, arithmetic and copies ran while one was open for 9% of the time, Pallas kernels for 2%

profile of v1, /device:TPU:0, one launch (start us, length us, event | category | flops | bytes accessed | tf_op | source)
XLA Modules:
  0.0 55.6 jit_solution(2649274529669994806)
XLA Ops:
  0.6 1.0 %copy-done = bf16[1,128,1280]{2,1,0:T(8,128)(2,1)S(1)} copy-done((bf16[1,128,1280]{2,1,0:T(8,128)(2,1)S(1)}, bf16[1,128,1280]{2,1,0:T(8,128)(2,1)}, u32[]{:S(2)}) %copy-start) | copy-done | bytes 327704
  1.6 1.0 %copy-done.4 = bf16[1,128,1280]{2,1,0:T(8,128)(2,1)S(1)} copy-done((bf16[1,128,1280]{2,1,0:T(8,128)(2,1)S(1)}, bf16[1,128,1280]{2,1,0:T(8,128)(2,1)}, u32[]{:S(2)}) %copy-start.4) | copy-done | bytes 327704
  2.6 0.7 %copy-done.6 = bf16[1280,8]{0,1:T(8,128)(2,1)S(1)} copy-done((bf16[1280,8]{0,1:T(8,128)(2,1)S(1)}, bf16[1280,8]{0,1:T(8,128)(2,1)}, u32[]{:S(2)}) %copy-start.6) | copy-done | bytes 20504
  3.3 0.7 %copy-done.8 = f32[8]{0:T(128)S(1)} copy-done((f32[8]{0:T(128)S(1)}, f32[8]{0:T(128)}, u32[]{:S(2)}) %copy-start.8) | copy-done | bytes 56
  4.0 0.7 %shard_map.109 = (bf16[64,1408]{1,0:T(8,128)(2,1)S(1)}, f32[8,128]{1,0:T(8,128)S(1)}, f32[1,128]{1,0:T(1,128)S(1)}) custom-call(bf16[1,128,1280]{2,1,0:T(8,128)(2,1)S(1)} %copy-done, bf16[1,128,1280]{2,1,0:T(8,128)(2,1)S(1)} %copy-done.4, bf16[8,1280]{1,0:T(8,128)(2,1)S(1)} %bitcast.12, f32[1,8]{1,0:T(1,128)S(1)} %bitcast.14), custom_call_target="tpu_custom_call" | custom-call | flops 10000000 | bytes 675872 | tf_op jit(solution)/shard_map/pallas_call | solution.py:180
  4.7 0.1 reshape.28
  4.7 16.5 %all_to_all.10 = bf16[32,2,1408]{2,1,0:T(2,128)(2,1)S(1)} all-to-all(bf16[32,2,1408]{2,1,0:T(2,128)(2,1)S(1)} %reshape.28), channel_id=1, replica_groups=mesh['img'=16,'tok'=2] {'img','tok'}, dimensions={0} | all-to-all | bytes 360448 | tf_op jit(solution)/shard_map/all_to_all | solution.py:193
  21.3 1.7 %copy-done.2 = bf16[1,1280,1024]{2,1,0:T(8,128)(2,1)S(1)} copy-done((bf16[1,1280,1024]{2,1,0:T(8,128)(2,1)S(1)}, bf16[1,1280,1024]{2,1,0:T(8,128)(2,1)}, u32[]{:S(2)}) %copy-start.2) | copy-done | bytes 2621464
  23.1 1.7 %copy-done.3 = bf16[1,1024,1280]{2,1,0:T(8,128)(2,1)S(1)} copy-done((bf16[1,1024,1280]{2,1,0:T(8,128)(2,1)S(1)}, bf16[1,1024,1280]{2,1,0:T(8,128)(2,1)}, u32[]{:S(2)}) %copy-start.3) | copy-done | bytes 2621464
  24.8 2.5 %shard_map.110 = (bf16[64,1408]{1,0:T(8,128)(2,1)S(1)}, bf16[16,1280]{1,0:T(8,128)(2,1)S(1)}, bf16[16,1280]{1,0:T(8,128)(2,1)S(1)}, bf16[16,1024]{1,0:T(8,128)(2,1)S(1)}, bf16[16,1024]{1,0:T(8,128)(2,1)S(1)}) custom-call(bf16[64,1408]{1,0:T(8,128)(2,1)S(1)} %reshape.29.got_ref, bf16[1,1280,1024]{2,1,0:T(8,128)(2,1)S(1)} %copy-done.2, ...), custom_call_target="tpu_custom_call" | custom-call | flops 10000000 | bytes 5423104 | tf_op jit(solution)/shard_map/pallas_call | solution.py:180
  27.4 11.1 %all_to_all.11 = bf16[32,2,1408]{2,1,0:T(2,128)(2,1)S(1)} all-to-all(bf16[32,2,1408]{2,1,0:T(2,128)(2,1)S(1)} %reshape.30), channel_id=1, replica_groups=mesh['img'=16,'tok'=2] {'img','tok'}, dimensions={0} | all-to-all | bytes 360448 | tf_op jit(solution)/shard_map/all_to_all | solution.py:193
  38.6 0.5 shard_map.111
  39.2 1.2 %collective-permute-done = f32[8,1408]{1,0:T(8,128)S(1)} collective-permute-done((f32[8,1408]{1,0:T(8,128)S(1)}, f32[8,1408]{1,0:T(8,128)S(1)}, u32[]{:S(2)}, u32[]{:S(2)}) %collective-permute-start) | collective-permute-done | bytes 45088 | tf_op jit(solution)/shard_map/ppermute | solution.py:200
  40.4 0.6 %collective-permute-start.3 = (bf16[8,1408]{1,0:T(8,128)(2,1)S(1)}, bf16[8,1408]{1,0:T(8,128)(2,1)S(1)}, u32[]{:S(2)}, u32[]{:S(2)}) collective-permute-start(bf16[8,1408]{1,0:T(8,128)(2,1)S(1)} %add_convert_fusion.1), channel_id=1, source_target_pairs={{0,5},{1,4},{2,7},{3,6},{4,1},{5,0},{6,3},{7,2},{8,13},{9,12},{10,... | collective-permute-start | bytes 67592 | tf_op jit(solution)/shard_map/ppermute | solution.py:200
  41.0 1.2 %collective-permute-start.2 = (bf16[8,1408]{1,0:T(8,128)(2,1)S(1)}, bf16[8,1408]{1,0:T(8,128)(2,1)S(1)}, u32[]{:S(2)}, u32[]{:S(2)}) collective-permute-start(bf16[8,1408]{1,0:T(8,128)(2,1)S(1)} %add_convert_fusion.1), channel_id=1, source_target_pairs={{0,4},{1,5},{2,6},{3,7},{4,0},{5,1},{6,2},{7,3},{8,12},{9,13},{10,... | collective-permute-start | bytes 67592 | tf_op jit(solution)/shard_map/ppermute | solution.py:200
  42.2 1.8 %collective-permute-start.1 = (bf16[8,1408]{1,0:T(8,128)(2,1)S(1)}, bf16[8,1408]{1,0:T(8,128)(2,1)S(1)}, u32[]{:S(2)}, u32[]{:S(2)}) collective-permute-start(bf16[8,1408]{1,0:T(8,128)(2,1)S(1)} %add_convert_fusion.1), channel_id=1, source_target_pairs={{0,1},{1,0},{2,3},{3,2},{4,5},{5,4},{6,7},{7,6},{8,9},{9,8},{10,11... | collective-permute-start | bytes 67592 | tf_op jit(solution)/shard_map/ppermute | solution.py:200
  44.0 2.4 %fusion = bf16[1,1280,1024]{2,1,0:T(8,128)(2,1)} fusion(bf16[16,1280]{1,0:T(8,128)(2,1)S(1)} %get-tuple-element.32, bf16[16,1024]{1,0:T(8,128)(2,1)S(1)} %get-tuple-element.33), kind=kOutput, calls=%fused_computation.2 | convolution fusion | flops 43253760 | bytes 2695168 | tf_op jit(solution)/shard_map/dot_general | solution.py:20
  46.4 1.4 %collective-permute-start.6 = (bf16[8,1408]{1,0:T(8,128)(2,1)S(1)}, bf16[8,1408]{1,0:T(8,128)(2,1)S(1)}, u32[]{:S(2)}, u32[]{:S(2)}) collective-permute-start(bf16[8,1408]{1,0:T(8,128)(2,1)S(1)} %add_convert_fusion), channel_id=1, source_target_pairs={{0,24},{1,25},{2,26},{3,27},{4,28},{5,29},{6,30},{7,31},{8,16},{9,... | collective-permute-start | bytes 67592 | tf_op jit(solution)/shard_map/ppermute | solution.py:200
  47.7 0.6 %collective-permute-start.5 = (bf16[8,1408]{1,0:T(8,128)(2,1)S(1)}, bf16[8,1408]{1,0:T(8,128)(2,1)S(1)}, u32[]{:S(2)}, u32[]{:S(2)}) collective-permute-start(bf16[8,1408]{1,0:T(8,128)(2,1)S(1)} %add_convert_fusion), channel_id=1, source_target_pairs={{0,16},{1,17},{2,18},{3,19},{4,20},{5,21},{6,22},{7,23},{8,24},{9,... | collective-permute-start | bytes 67592 | tf_op jit(solution)/shard_map/ppermute | solution.py:200
  48.3 2.5 %collective-permute-start.4 = (bf16[8,1408]{1,0:T(8,128)(2,1)S(1)}, bf16[8,1408]{1,0:T(8,128)(2,1)S(1)}, u32[]{:S(2)}, u32[]{:S(2)}) collective-permute-start(bf16[8,1408]{1,0:T(8,128)(2,1)S(1)} %add_convert_fusion), channel_id=1, source_target_pairs={{0,8},{1,9},{2,10},{3,11},{4,12},{5,13},{6,14},{7,15},{8,0},{9,1},... | collective-permute-start | bytes 67592 | tf_op jit(solution)/shard_map/ppermute | solution.py:200
  50.8 2.4 %fusion.1 = bf16[1,1024,1280]{2,1,0:T(8,128)(2,1)} fusion(bf16[16,1024]{1,0:T(8,128)(2,1)S(1)} %get-tuple-element.34, bf16[16,1280]{1,0:T(8,128)(2,1)S(1)} %get-tuple-element.35), kind=kOutput, calls=%fused_computation.3 | convolution fusion | flops 43253760 | bytes 2695168 | tf_op jit(solution)/shard_map/dot_general | solution.py:20
  53.2 1.1 %shard_map.112 = (bf16[1,128,1280]{2,1,0:T(8,128)(2,1)}, bf16[1,128,1280]{2,1,0:T(8,128)(2,1)}) custom-call(bf16[1,128,1280]{2,1,0:T(8,128)(2,1)S(1)} %copy-done.1, f32[8,128]{1,0:T(8,128)S(1)} %get-tuple-element.21.logit_ref, bf16[8,1280]{1,0:T(8,128)(2,1)S(1)} %get-tuple-element.25.outs_ref, bf16[16,128]{1,0:T(8,128)(2,1)S(1)} %get-tuple-element.26.coef_ref, ...), custom_call_target="tpu_custom_call" | custom-call | flops 10000000 | bytes 397824 | tf_op jit(solution)/shard_map/pallas_call | solution.py:180
  54.4 0.6 %slice_reduce_fusion = f32[8]{0:T(128)} fusion(f32[8,1408]{1,0:T(8,128)S(1)} %add_add_fusion), kind=kLoop, calls=%fused_computation.8 | loop fusion | bytes 64 | tf_op jit(solution)/shard_map/slice | solution.py:255
  55.0 0.6 %slice_bitcast_fusion = f32[1280,8]{0,1:T(8,128)} fusion(f32[8,1408]{1,0:T(8,128)S(1)} %add_add_fusion), kind=kLoop, calls=%fused_computation.7 | loop fusion | bytes 81920 | tf_op jit(solution)/shard_map/transpose | solution.py:255
  (27 shorter events, 0.3 us)
Async XLA Ops:
  0.6 1.0 %copy-start = (bf16[1,128,1280]{2,1,0:T(8,128)(2,1)S(1)}, bf16[1,128,1280]{2,1,0:T(8,128)(2,1)}, u32[]{:S(2)}) copy-start(bf16[1,128,1280]{2,1,0:T(8,128)(2,1)} %tok_ref.5) | copy-start | bytes 983044
  1.6 1.0 %copy-start.4 = (bf16[1,128,1280]{2,1,0:T(8,128)(2,1)S(1)}, bf16[1,128,1280]{2,1,0:T(8,128)(2,1)}, u32[]{:S(2)}) copy-start(bf16[1,128,1280]{2,1,0:T(8,128)(2,1)} %grad_ref.3) | copy-start | bytes 983044
  2.6 0.7 %copy-start.6 = (bf16[1280,8]{0,1:T(8,128)(2,1)S(1)}, bf16[1280,8]{0,1:T(8,128)(2,1)}, u32[]{:S(2)}) copy-start(bf16[1280,8]{0,1:T(8,128)(2,1)} %param.8) | copy-start | bytes 61444
  3.3 0.7 %copy-start.8 = (f32[8]{0:T(128)S(1)}, f32[8]{0:T(128)}, u32[]{:S(2)}) copy-start(f32[8]{0:T(128)} %param.9) | copy-start | bytes 100
  21.3 1.7 %copy-start.2 = (bf16[1,1280,1024]{2,1,0:T(8,128)(2,1)S(1)}, bf16[1,1280,1024]{2,1,0:T(8,128)(2,1)}, u32[]{:S(2)}) copy-start(bf16[1,1280,1024]{2,1,0:T(8,128)(2,1)} %one_ref.1) | copy-start | bytes 7864324
  23.1 1.7 %copy-start.3 = (bf16[1,1024,1280]{2,1,0:T(8,128)(2,1)S(1)}, bf16[1,1024,1280]{2,1,0:T(8,128)(2,1)}, u32[]{:S(2)}) copy-start(bf16[1,1024,1280]{2,1,0:T(8,128)(2,1)} %two_ref.1) | copy-start | bytes 7864324
  24.8 13.8 %copy-start.1 = (bf16[1,128,1280]{2,1,0:T(8,128)(2,1)S(1)}, bf16[1,128,1280]{2,1,0:T(8,128)(2,1)}, u32[]{:S(2)}) copy-start(bf16[1,128,1280]{2,1,0:T(8,128)(2,1)} %tok_ref.5) | copy-start | bytes 983044
  24.8 13.8 %copy-start.5 = (bf16[1,128,1280]{2,1,0:T(8,128)(2,1)S(1)}, bf16[1,128,1280]{2,1,0:T(8,128)(2,1)}, u32[]{:S(2)}) copy-start(bf16[1,128,1280]{2,1,0:T(8,128)(2,1)} %grad_ref.3) | copy-start | bytes 983044
  24.8 13.8 %copy-start.7 = (bf16[1280,8]{0,1:T(8,128)(2,1)S(1)}, bf16[1280,8]{0,1:T(8,128)(2,1)}, u32[]{:S(2)}) copy-start(bf16[1280,8]{0,1:T(8,128)(2,1)} %param.8) | copy-start | bytes 61444
  24.8 13.8 %copy-start.9 = (f32[8]{0:T(128)S(1)}, f32[8]{0:T(128)}, u32[]{:S(2)}) copy-start(f32[8]{0:T(128)} %param.9) | copy-start | bytes 100
  39.2 1.2 %collective-permute-start = (f32[8,1408]{1,0:T(8,128)S(1)}, f32[8,1408]{1,0:T(8,128)S(1)}, u32[]{:S(2)}, u32[]{:S(2)}) collective-permute-start(f32[8,1408]{1,0:T(8,128)S(1)} %get-tuple-element.31), channel_id=1, source_target_pairs={{0,2},{1,3},{2,0},{3,1},{4,6},{5,7},{6,4},{7,5},{8,10},{9,11},{10,... | collective-permute-start | bytes 135176 | tf_op jit(solution)/shard_map/ppermute | solution.py:200
  40.4 5.9 %collective-permute-start.3 = (bf16[8,1408]{1,0:T(8,128)(2,1)S(1)}, bf16[8,1408]{1,0:T(8,128)(2,1)S(1)}, u32[]{:S(2)}, u32[]{:S(2)}) collective-permute-start(bf16[8,1408]{1,0:T(8,128)(2,1)S(1)} %add_convert_fusion.1), channel_id=1, source_target_pairs={{0,5},{1,4},{2,7},{3,6},{4,1},{5,0},{6,3},{7,2},{8,13},{9,12},{10,... | collective-permute-start | bytes 67592 | tf_op jit(solution)/shard_map/ppermute | solution.py:200
  41.0 5.4 %collective-permute-start.2 = (bf16[8,1408]{1,0:T(8,128)(2,1)S(1)}, bf16[8,1408]{1,0:T(8,128)(2,1)S(1)}, u32[]{:S(2)}, u32[]{:S(2)}) collective-permute-start(bf16[8,1408]{1,0:T(8,128)(2,1)S(1)} %add_convert_fusion.1), channel_id=1, source_target_pairs={{0,4},{1,5},{2,6},{3,7},{4,0},{5,1},{6,2},{7,3},{8,12},{9,13},{10,... | collective-permute-start | bytes 67592 | tf_op jit(solution)/shard_map/ppermute | solution.py:200
  42.2 4.1 %collective-permute-start.1 = (bf16[8,1408]{1,0:T(8,128)(2,1)S(1)}, bf16[8,1408]{1,0:T(8,128)(2,1)S(1)}, u32[]{:S(2)}, u32[]{:S(2)}) collective-permute-start(bf16[8,1408]{1,0:T(8,128)(2,1)S(1)} %add_convert_fusion.1), channel_id=1, source_target_pairs={{0,1},{1,0},{2,3},{3,2},{4,5},{5,4},{6,7},{7,6},{8,9},{9,8},{10,11... | collective-permute-start | bytes 67592 | tf_op jit(solution)/shard_map/ppermute | solution.py:200
  46.4 8.0 %collective-permute-start.6 = (bf16[8,1408]{1,0:T(8,128)(2,1)S(1)}, bf16[8,1408]{1,0:T(8,128)(2,1)S(1)}, u32[]{:S(2)}, u32[]{:S(2)}) collective-permute-start(bf16[8,1408]{1,0:T(8,128)(2,1)S(1)} %add_convert_fusion), channel_id=1, source_target_pairs={{0,24},{1,25},{2,26},{3,27},{4,28},{5,29},{6,30},{7,31},{8,16},{9,... | collective-permute-start | bytes 67592 | tf_op jit(solution)/shard_map/ppermute | solution.py:200
  47.7 6.6 %collective-permute-start.5 = (bf16[8,1408]{1,0:T(8,128)(2,1)S(1)}, bf16[8,1408]{1,0:T(8,128)(2,1)S(1)}, u32[]{:S(2)}, u32[]{:S(2)}) collective-permute-start(bf16[8,1408]{1,0:T(8,128)(2,1)S(1)} %add_convert_fusion), channel_id=1, source_target_pairs={{0,16},{1,17},{2,18},{3,19},{4,20},{5,21},{6,22},{7,23},{8,24},{9,... | collective-permute-start | bytes 67592 | tf_op jit(solution)/shard_map/ppermute | solution.py:200
  48.3 6.1 %collective-permute-start.4 = (bf16[8,1408]{1,0:T(8,128)(2,1)S(1)}, bf16[8,1408]{1,0:T(8,128)(2,1)S(1)}, u32[]{:S(2)}, u32[]{:S(2)}) collective-permute-start(bf16[8,1408]{1,0:T(8,128)(2,1)S(1)} %add_convert_fusion), channel_id=1, source_target_pairs={{0,8},{1,9},{2,10},{3,11},{4,12},{5,13},{6,14},{7,15},{8,0},{9,1},... | collective-permute-start | bytes 67592 | tf_op jit(solution)/shard_map/ppermute | solution.py:200

commit v2 on v1

--- a/solution.py
+++ b/solution.py
@@ -14,6 +14,7 @@
 F32 = jnp.float32
 BOTH = ("img", "tok")
 LANES = 128
+FRONT = 4 * 10**9
 
 
 def dot(left, right, dims):
@@ -29,21 +30,25 @@
     return lax.broadcasted_iota(jnp.int32, shape, axis)
 
 
+def digits(row, sizes):
+    out = []
+    for size in reversed(sizes):
+        out.append(row & (size - 1))
+        row = row >> log2(size)
+    return out[::-1]
+
+
 def selection(shape, row_key, column_key):
     hit = row_key(iota(shape, 0)) == column_key(iota(shape, 1))
     return jnp.where(hit, 1.0, 0.0).astype(BF)
 
 
-def stacked_key(count):
-    return lambda row: row
-
-
-def by_image(images, halves):
-    return lambda row: (row & 1) * images + (row >> (1 + log2(halves)))
-
-
-def by_expert(experts, halves):
-    return lambda row: (row & 1) * experts + ((row >> (1 + log2(halves))) & (experts - 1))
+def pick(left_key, left_size, right, right_key):
+    return dot(selection((left_size, right.shape[0]), left_key, right_key), right, ((1,), (0,)))
+
+
+def itself(row):
+    return row
 
 
 def as_column(row):
@@ -81,8 +86,43 @@
     return expo, expo / jnp.sum(expo, 0, keepdims=True)
 
 
-def front_kernel(halves, tok_ref, grad_ref, router_ref, scale_ref, sent_ref, logit_ref, inv_ref):
-    experts = router_ref.shape[0]
+def fetch(sources, targets, sems):
+    copies = [
+        pltpu.make_async_copy(source, target, sems.at[place])
+        for place, (source, target) in enumerate(zip(sources, targets))
+    ]
+    for copy in copies:
+        copy.start()
+    return copies
+
+
+def expert_rows(plan, experts):
+    copies, halves = plan
+
+    def key(row):
+        _, place, _, kind = digits(row, (copies, experts, halves, 2))
+        return kind * experts + place
+
+    return key
+
+
+def image_rows(images, halves):
+    def key(row):
+        place, _, kind = digits(row, (images, halves, 2))
+        return kind * images + place
+
+    return key
+
+
+def front_kernel(
+    plan, tok_hbm, grad_hbm, router_hbm, scale_hbm, sent_ref, logit_ref, inv_ref,
+    tok_ref, grad_ref, router_ref, scale_ref, sems,
+):
+    arrived = fetch(
+        [tok_hbm, router_hbm, scale_hbm, grad_hbm], [tok_ref, router_ref, scale_ref, grad_ref], sems
+    )
+    for copy in arrived[:3]:
+        copy.wait()
     tok = tok_ref[0]
     tok_f = tok.astype(F32)
     inv_x = row_of(lax.rsqrt(jnp.sum(tok_f * tok_f, 1, keepdims=True) + EPSILON))
@@ -91,12 +131,10 @@
     logit = raw * inv_x * (inv_p * scale)
     expo, comb = softmax(logit)
     numer = dot(expo.astype(BF), tok, ((1,), (0,)))
+    arrived[3].wait()
     dys = dot(comb.astype(BF), grad_ref[0], ((1,), (0,)))
     rows = stack_rows(numer, dys, [jnp.sum(expo, 1, keepdims=True)])
-    spread = selection(
-        (sent_ref.shape[0], 2 * experts), by_expert(experts, halves), stacked_key(experts)
-    )
-    sent_ref[...] = dot(spread, rows, ((1,), (0,))).astype(BF)
+    sent_ref[...] = pick(expert_rows(plan, router_ref.shape[0]), sent_ref.shape[0], rows, itself).astype(BF)
     logit_ref[...] = logit
     inv_ref[...] = inv_x
 
@@ -105,10 +143,8 @@
     images, halves, got_ref, one_ref, two_ref, back_ref, rows_ref, grad_rows_ref, hidden_ref, dact_ref
 ):
     width = one_ref.shape[1]
-    gather = selection(
-        (2 * images, got_ref.shape[0]), stacked_key(images), by_image(images, halves)
-    )
-    sums = dot(gather, got_ref[...], ((1,), (0,)))
+    key = image_rows(images, halves)
+    sums = pick(itself, 2 * images, got_ref[...], key)
     den = sums[:images, width : width + 1] + sums[images:, width : width + 1]
     rows = (sums[:images, :width] / den).astype(BF)
     grad_rows = sums[images:, :width].astype(BF)
@@ -120,28 +156,37 @@
     out_part = dot(hidden, two_ref[0], ((1,), (0,)))
     in_part = dot(dact, one_ref[0], ((1,), (1,)))
     corr = jnp.sum(dact.astype(F32) * act, 1, keepdims=True)
-    spread = selection(
-        (back_ref.shape[0], 2 * images), by_image(images, halves), stacked_key(images)
-    )
     packed = stack_rows(out_part, in_part, [den, corr])
-    back_ref[...] = dot(spread, packed, ((1,), (0,))).astype(BF)
+    back_ref[...] = pick(key, back_ref.shape[0], packed, itself).astype(BF)
     rows_ref[...] = rows
     grad_rows_ref[...] = grad_rows
     hidden_ref[...] = hidden
     dact_ref[...] = dact
 
 
+def outer_kernel(size, left_ref, right_ref, out_hbm, out_ref, sems):
+    copies = []
+    for place in range(left_ref.shape[1] // size):
+        part = slice(place * size, (place + 1) * size)
+        out_ref[0, part] = dot(left_ref[:, part], right_ref[...], ((0,), (0,))).astype(BF)
+        copy = pltpu.make_async_copy(
+            out_ref.at[:, pl.ds(place * size, size)], out_hbm.at[:, pl.ds(place * size, size)],
+            sems.at[place],
+        )
+        copy.start()
+        copies.append(copy)
+    for copy in copies:
+        copy.wait()
+
+
 def middle_kernel(
-    halves, copies, back_ref, tok_ref, grad_ref, logit_ref, inv_ref, router_ref, scale_ref,
+    plan, back_ref, tok_ref, grad_ref, logit_ref, inv_ref, router_ref, scale_ref,
     sums_ref, outs_ref, coef_ref, mix_ref, signal_ref,
 ):
     experts, width = router_ref.shape
-    gather = selection(
-        (2 * experts, back_ref.shape[0]), stacked_key(experts), by_expert(experts, halves)
-    )
-    sums = dot(gather, back_ref[...], ((1,), (0,)))
+    sums = pick(itself, 2 * experts, back_ref[...], expert_rows(plan, router_ref.shape[0]))
     extras = sums[:experts, width:] + sums[experts:, width:]
-    den = extras[:, :1] * (1.0 / (copies * halves))
+    den = extras[:, :1] * (1.0 / (plan[0] * plan[1]))
     corr = extras[:, 1:2]
     ys = sums[:experts, :width].astype(BF)
     dxs = sums[experts:, :width].astype(BF)
@@ -176,12 +221,26 @@
     grads_ref[0] = (grads - column * tok_ref[0].astype(F32)).astype(BF)
 
 
-def call(kernel, outs, *args, flops=10**7, room=24 * 2**20):
+def last_kernel(own_ref, other_ref, router_ref, scale_ref):
+    sums = own_ref[...].astype(F32) + other_ref[...].astype(F32)
+    experts, width = router_ref.shape
+    router_ref[...] = sums[:, :width]
+    eye = iota((experts, experts), 0) == iota((experts, experts), 1)
+    scale_ref[...] = jnp.sum(jnp.where(eye, sums[:, width : width + 1], 0.0), 0, keepdims=True)
+
+
+def call(kernel, outs, *args, stays=(), buffers=(), flops=10**7, room=24 * 2**20, home=pltpu.VMEM):
+    specs = [pl.BlockSpec(memory_space=pltpu.VMEM)] * len(args)
+    args = list(args)
+    for place in stays:
+        specs[place] = pl.BlockSpec(memory_space=pltpu.HBM)
+        args[place] = pltpu.with_memory_space_constraint(args[place], pltpu.HBM)
     return pl.pallas_call(
         kernel,
         out_shape=[jax.ShapeDtypeStruct(shape, dtype) for shape, dtype in outs],
-        in_specs=[pl.BlockSpec(memory_space=pltpu.VMEM)] * len(args),
-        out_specs=[pl.BlockSpec(memory_space=pltpu.VMEM)] * len(outs),
+        in_specs=specs,
+        out_specs=[pl.BlockSpec(memory_space=home)] * len(outs),
+        scratch_shapes=buffers,
         compiler_params=pltpu.CompilerParams(vmem_limit_bytes=room),
         cost_estimate=pl.CostEstimate(
             flops=flops, bytes_accessed=sum(a.size * a.dtype.itemsize for a in args), transcendentals=0
@@ -189,6 +248,17 @@
     )(*args)
 
 
+def weight_grad(left, right):
+    size = 256
+    shape = (1, left.shape[1], right.shape[1])
+    (out,) = call(
+        functools.partial(outer_kernel, size), [(shape, BF)], left, right,
+        buffers=[pltpu.VMEM(shape, BF), pltpu.SemaphoreType.DMA((shape[1] // size,))],
+        flops=10**9, home=pltpu.HBM,
+    )
+    return out
+
+
 def exchange(block, devices):
     moved = lax.all_to_all(
         block.reshape(devices, 2, block.shape[1]), BOTH, split_axis=0, concat_axis=0, tiled=True
@@ -196,39 +266,42 @@
     return moved.reshape(block.shape)
 
 
-def pair(term, mask, devices):
-    return lax.ppermute(term, BOTH, [(d, d ^ mask) for d in range(devices)])
-
-
-def sum_everywhere(term, devices):
-    bits = [1 << place for place in range(log2(devices))]
-    chip_bits = [bits[0]] + bits[2:]
-    term = term + pair(term, bits[1], devices)
-    for place in range(0, len(chip_bits), 2):
-        group = chip_bits[place : place + 2]
-        sent = term.astype(BF)
-        near = sent.astype(F32) + pair(sent, group[0], devices).astype(F32)
-        if len(group) == 2:
-            far = pair(sent, group[1], devices).astype(F32)
-            far = far + pair(sent, group[0] ^ group[1], devices).astype(F32)
-            near = near + far
-        term = near
-    return term
+def pair(term, place, devices):
+    return lax.ppermute(term, BOTH, [(d, d ^ (1 << place)) for d in range(devices)])
+
+
+def sum_everywhere(term, devices, beside):
+    order = [1, 0] + list(range(2, log2(devices)))
+    done = []
+    term = term + pair(term, order[0], devices)
+    for place in order[1:]:
+        own = term.astype(BF)
+        other = pair(own, place, devices)
+        if beside:
+            other, ready = lax.optimization_barrier((other, beside[0]))
+            beside = beside[1:]
+            done.append(ready)
+        term = own.astype(F32) + other.astype(F32)
+    return own, other, done + list(beside)
 
 
 def shards(images, halves, tokens, grad_out, router, slot_scale, w_in, w_out):
     devices = images * halves
     tok_rows, width = tokens.shape[1:]
     experts = router.shape[1]
-    copies = images // experts
+    plan = (images // experts, halves)
     hidden_dev = w_in.shape[2]
     long = width + LANES
     router_t = router.T
     scale_row = slot_scale.reshape(1, experts)
+    inputs = (tokens, grad_out, router_t, scale_row)
     sent, logit, inv_x = call(
-        functools.partial(front_kernel, halves),
+        functools.partial(front_kernel, plan),
         [((2 * devices, long), BF), ((experts, tok_rows), F32), ((1, tok_rows), F32)],
-        tokens, grad_out, router_t, scale_row,
+        *inputs,
+        stays=range(4),
+        buffers=[pltpu.VMEM(a.shape, a.dtype) for a in inputs] + [pltpu.SemaphoreType.DMA((4,))],
+        flops=FRONT,
     )
     got = exchange(sent, devices)
     back, rows, grad_rows, hidden, dact = call(
@@ -236,12 +309,13 @@
         [((2 * devices, long), BF), ((images, width), BF), ((images, width), BF),
          ((images, hidden_dev), BF), ((images, hidden_dev), BF)],
         got, w_in, w_out,
+        flops=10**9,
     )
     back = exchange(back, devices)
-    grad_w_in = dot(rows, dact, ((0,), (0,))).astype(BF)[None]
-    grad_w_out = dot(hidden, grad_rows, ((0,), (0,))).astype(BF)[None]
+    grad_w_in = weight_grad(rows, dact)
+    grad_w_out = weight_grad(hidden, grad_rows)
     sums, ys, coef, mix, signal = call(
-        functools.partial(middle_kernel, halves, copies),
+        functools.partial(middle_kernel, plan),
         [((experts, long), F32), ((experts, width), BF), ((2 * experts, tok_rows), BF),
          ((2 * experts, width), BF), ((1, tok_rows), F32)],
         back, tokens, grad_out, logit, inv_x, router_t, scale_row,
@@ -251,8 +325,13 @@
         [(tokens.shape, BF), (tokens.shape, BF)],
         tokens, logit, ys, coef, mix, signal,
     )
-    sums = sum_everywhere(sums, devices)
-    return (combined, grad_tokens, sums[:, :width].T, sums[:, width], grad_w_in, grad_w_out)
+    own, other, (grad_w_in, grad_w_out, (combined, grad_tokens)) = sum_everywhere(
+        sums, devices, [grad_w_in, grad_w_out, (combined, grad_tokens)]
+    )
+    grad_router, grad_scale = call(
+        last_kernel, [((experts, width), F32), ((1, experts), F32)], own, other
+    )
+    return (combined, grad_tokens, grad_router.T, grad_scale[0], grad_w_in, grad_w_out)
 
 
 def solution(mesh):

time: 56 us -> 57.7 us (1.030)
  waiting for transfers between devices: 1.23 us -> 8.92 us
  Pallas kernels: 4.9 us -> 10.6 us
  starting transfers between devices: 8.03 us -> 2.49 us
  matrix products: 4.73 us -> 0 us
  local copies, waits for them, and re-layouts: 8.34 us -> 7 us
    ppermute x7 -> x5, waiting for transfers between devices: 1.23 us -> 8.92 us  [pair(): lax.ppermute(term, BOTH, [(d, d ^ 1 << place) for d in range(devices)])]
    pallas_call x4 -> x7, Pallas kernels: 4.9 us -> 10.6 us  [call(): pl.pallas_call(kernel, out_shape=[jax.ShapeDtypeStruct(shape, dtype) for...]
    ppermute x7 -> x5, starting transfers between devices: 8.03 us -> 2.49 us  [pair(): lax.ppermute(term, BOTH, [(d, d ^ 1 << place) for d in range(devices)])]
    dot_general x2 -> x0, matrix products: 4.73 us -> none  [dot(): lax.dot_general(left, right, (dims, ((), ())), preferred_element_type=F32)]
    unnamed x20 -> x26, local copies, waits for them, and re-layouts: 6.81 us -> 5.8 us
    reshape x2, local copies, waits for them, and re-layouts: 0.14 us -> 1.06 us  [exchange(): block.reshape(devices, 2, block.shape[1])]
    slice x1 -> x0, local copies, waits for them, and re-layouts: 0.63 us -> none  [shards(): sums[:, width]]
    transpose x1 -> x0, local copies, waits for them, and re-layouts: 0.62 us -> none  [shards(): sums[:, :width]]
  transfers between devices with their start and end apart: 7 -> 5, of which waited for: 1 -> 5; matrix products, arithmetic and copies ran while one was open for 9% -> 0% of each run, Pallas kernels for 2% -> 9%
where the time goes in v2:
time: 57.7 us; the launch traced here: 57.4 us
  blocking collectives  27.6 us (48%)
  Pallas kernels  10.6 us (18%)
  waiting for transfers between devices  8.92 us (15%)
  local copies, waits for them, and re-layouts  7 us (12%)
  starting transfers between devices  2.49 us (4%)
  between operations  0.78 us (1%)
    all_to_all x2, blocking collectives, exchange(): lax.all_to_all(block.reshape(devices, 2, block.shape[1]), BOTH, split_axi...  27.6 us
    pallas_call x7, Pallas kernels, call(): pl.pallas_call(kernel, out_shape=[jax.ShapeDtypeStruct(shape, dtype) for...  10.6 us
    ppermute x5, waiting for transfers between devices, pair(): lax.ppermute(term, BOTH, [(d, d ^ 1 << place) for d in range(devices)])  8.92 us
    unnamed x26, local copies, waits for them, and re-layouts  5.8 us
    ppermute x5, starting transfers between devices, pair(): lax.ppermute(term, BOTH, [(d, d ^ 1 << place) for d in range(devices)])  2.49 us
  transfers between devices with their start and end apart: 5, of which 5 were waited for; matrix products, arithmetic and copies ran while one was open for 0% of the time, Pallas kernels for 9%

profile of v2, /device:TPU:0, one launch (start us, length us, event | category | flops | bytes accessed | tf_op | source)
XLA Modules:
  0.0 57.4 jit_solution(618217060074853029)
XLA Ops:
  0.6 2.0 %shard_map.109 = (bf16[64,1408]{1,0:T(8,128)(2,1)S(1)}, f32[8,128]{1,0:T(8,128)S(1)}, f32[1,128]{1,0:T(1,128)S(1)}) custom-call(bf16[1,128,1280]{2,1,0:T(8,128)(2,1)} %tok_ref.3, bf16[1,128,1280]{2,1,0:T(8,128)(2,1)} %grad_ref.1, bf16[8,1280]{1,0:T(8,128)(2,1)} %bitcast.4, f32[1,8]{1,0:T(1,128)} %bitcast.6), custom_call_target="tpu_custom_call" | custom-call | flops 4000000000 | bytes 675872 | tf_op jit(solution)/shard_map/pallas_call | solution.py:238
  2.7 16.5 %all_to_all.10 = bf16[32,2,1408]{2,1,0:T(2,128)(2,1)S(1)} all-to-all(bf16[32,2,1408]{2,1,0:T(2,128)(2,1)S(1)} %reshape.28), channel_id=1, replica_groups=mesh['img'=16,'tok'=2] {'img','tok'}, dimensions={0} | all-to-all | bytes 360448 | tf_op jit(solution)/shard_map/all_to_all | solution.py:263
  19.3 1.7 %copy-done.1 = bf16[1,1024,1280]{2,1,0:T(8,128)(2,1)S(1)} copy-done((bf16[1,1024,1280]{2,1,0:T(8,128)(2,1)S(1)}, bf16[1,1024,1280]{2,1,0:T(8,128)(2,1)}, u32[]{:S(2)}) %copy-start.1) | copy-done | bytes 2621464
  21.0 2.5 %shard_map.110 = (bf16[64,1408]{1,0:T(8,128)(2,1)S(1)}, bf16[16,1280]{1,0:T(8,128)(2,1)S(1)}, bf16[16,1280]{1,0:T(8,128)(2,1)S(1)}, bf16[16,1024]{1,0:T(8,128)(2,1)S(1)}, bf16[16,1024]{1,0:T(8,128)(2,1)S(1)}) custom-call(bf16[64,1408]{1,0:T(8,128)(2,1)S(1)} %reshape.29.got_ref, bf16[1,1280,1024]{2,1,0:T(8,128)(2,1)S(1)} %copy-done, ...), custom_call_target="tpu_custom_call" | custom-call | flops 1000000000 | bytes 5423104 | tf_op jit(solution)/shard_map/pallas_call | solution.py:238
  23.6 0.7 %copy-done.4 = bf16[64,1408]{1,0:T(8,128)(2,1)} copy-done((bf16[64,1408]{1,0:T(8,128)(2,1)}, bf16[64,1408]{1,0:T(8,128)(2,1)S(1)}, u32[]{:S(2)}) %copy-start.4) | copy-done | bytes 180248
  24.3 0.6 %copy-done.7 = bf16[16,1280]{1,0:T(8,128)(2,1)} copy-done((bf16[16,1280]{1,0:T(8,128)(2,1)}, bf16[16,1280]{1,0:T(8,128)(2,1)S(1)}, u32[]{:S(2)}) %copy-start.7) | copy-done | bytes 40984
  24.9 0.6 %copy-done.9 = bf16[16,1024]{1,0:T(8,128)(2,1)} copy-done((bf16[16,1024]{1,0:T(8,128)(2,1)}, bf16[16,1024]{1,0:T(8,128)(2,1)S(1)}, u32[]{:S(2)}) %copy-start.9) | copy-done | bytes 32792
  25.5 0.6 %copy-done.11 = bf16[16,1024]{1,0:T(8,128)(2,1)} copy-done((bf16[16,1024]{1,0:T(8,128)(2,1)}, bf16[16,1024]{1,0:T(8,128)(2,1)S(1)}, u32[]{:S(2)}) %copy-start.11) | copy-done | bytes 32792
  26.1 1.0 %reshape.30 = bf16[32,2,1408]{2,1,0:T(2,128)(2,1)S(1)} reshape(bf16[64,1408]{1,0:T(8,128)(2,1)} %copy-done.4) | data formatting | bytes 360448 | tf_op jit(solution)/shard_map/reshape | solution.py:264
  27.1 11.1 %all_to_all.11 = bf16[32,2,1408]{2,1,0:T(2,128)(2,1)S(1)} all-to-all(bf16[32,2,1408]{2,1,0:T(2,128)(2,1)S(1)} %reshape.30), channel_id=1, replica_groups=mesh['img'=16,'tok'=2] {'img','tok'}, dimensions={0} | all-to-all | bytes 360448 | tf_op jit(solution)/shard_map/all_to_all | solution.py:263
  38.3 0.5 shard_map.111
  38.9 1.2 %collective-permute-done = f32[8,1408]{1,0:T(8,128)S(1)} collective-permute-done((f32[8,1408]{1,0:T(8,128)S(1)}, f32[8,1408]{1,0:T(8,128)S(1)}, u32[]{:S(2)}, u32[]{:S(2)}) %collective-permute-start) | collective-permute-done | bytes 45088 | tf_op jit(solution)/shard_map/ppermute | solution.py:270
  40.4 0.8 %copy-done.8 = bf16[16,1280]{1,0:T(8,128)(2,1)S(1)} copy-done((bf16[16,1280]{1,0:T(8,128)(2,1)S(1)}, bf16[16,1280]{1,0:T(8,128)(2,1)}, u32[]{:S(2)}) %copy-start.8) | copy-done | bytes 40984
  41.2 0.8 %copy-done.12 = bf16[16,1024]{1,0:T(8,128)(2,1)S(1)} copy-done((bf16[16,1024]{1,0:T(8,128)(2,1)S(1)}, bf16[16,1024]{1,0:T(8,128)(2,1)}, u32[]{:S(2)}) %copy-start.12) | copy-done | bytes 32792
  42.0 1.8 %shard_map.112 = bf16[1,1280,1024]{2,1,0:T(8,128)(2,1)} custom-call(bf16[16,1280]{1,0:T(8,128)(2,1)S(1)} %copy-done.8, bf16[16,1024]{1,0:T(8,128)(2,1)S(1)} %copy-done.12), custom_call_target="tpu_custom_call" | custom-call | flops 1000000000 | bytes 73728 | tf_op jit(solution)/shard_map/pallas_call | solution.py:238
  44.0 0.7 %collective-permute-start.2 = (bf16[8,1408]{1,0:T(8,128)(2,1)S(1)}, bf16[8,1408]{1,0:T(8,128)(2,1)S(1)}, u32[]{:S(2)}, u32[]{:S(2)}) collective-permute-start(bf16[8,1408]{1,0:T(8,128)(2,1)S(1)} %add_convert_fusion.2), channel_id=1, source_target_pairs={{0,4},{1,5},{2,6},{3,7},{4,0},{5,1},{6,2},{7,3},{8,12},{9,13},{10,... | collective-permute-start | bytes 67592 | tf_op jit(solution)/shard_map/ppermute | solution.py:270
  44.7 1.9 %shard_map.113 = bf16[1,1024,1280]{2,1,0:T(8,128)(2,1)} custom-call(bf16[16,1024]{1,0:T(8,128)(2,1)S(1)} %copy-done.10, bf16[16,1280]{1,0:T(8,128)(2,1)S(1)} %get-tuple-element.39.right_ref), custom_call_target="tpu_custom_call" | custom-call | flops 1000000000 | bytes 73728 | tf_op jit(solution)/shard_map/pallas_call | solution.py:238
  46.6 1.2 %collective-permute-done.2 = bf16[8,1408]{1,0:T(8,128)(2,1)S(1)} collective-permute-done((bf16[8,1408]{1,0:T(8,128)(2,1)S(1)}, bf16[8,1408]{1,0:T(8,128)(2,1)S(1)}, u32[]{:S(2)}, u32[]{:S(2)}) %collective-permute-start.2) | collective-permute-done | bytes 22560 | tf_op jit(solution)/shard_map/ppermute | solution.py:270
  47.9 0.7 %collective-permute-start.3 = (bf16[8,1408]{1,0:T(8,128)(2,1)S(1)}, bf16[8,1408]{1,0:T(8,128)(2,1)S(1)}, u32[]{:S(2)}, u32[]{:S(2)}) collective-permute-start(bf16[8,1408]{1,0:T(8,128)(2,1)S(1)} %add_convert_fusion.1), channel_id=1, source_target_pairs={{0,8},{1,9},{2,10},{3,11},{4,12},{5,13},{6,14},{7,15},{8,0},{9,1},... | collective-permute-start | bytes 67592 | tf_op jit(solution)/shard_map/ppermute | solution.py:270
  48.5 1.1 %shard_map.114 = (bf16[1,128,1280]{2,1,0:T(8,128)(2,1)}, bf16[1,128,1280]{2,1,0:T(8,128)(2,1)}) custom-call(bf16[1,128,1280]{2,1,0:T(8,128)(2,1)S(1)} %copy-done.2, f32[8,128]{1,0:T(8,128)S(1)} %get-tuple-element.32.logit_ref, bf16[8,1280]{1,0:T(8,128)(2,1)S(1)} %get-tuple-element.41.outs_ref, bf16[16,128]{1,0:T(8,128)(2,1)S(1)} %get-tuple-element.42.coef_ref, ...), custom_call_target="tpu_custom_call" | custom-call | flops 10000000 | bytes 397824 | tf_op jit(solution)/shard_map/pallas_call | solution.py:238
  49.7 2.1 %collective-permute-done.3 = bf16[8,1408]{1,0:T(8,128)(2,1)S(1)} collective-permute-done((bf16[8,1408]{1,0:T(8,128)(2,1)S(1)}, bf16[8,1408]{1,0:T(8,128)(2,1)S(1)}, u32[]{:S(2)}, u32[]{:S(2)}) %collective-permute-start.3) | collective-permute-done | bytes 22560 | tf_op jit(solution)/shard_map/ppermute | solution.py:270
  51.8 0.8 %collective-permute-start.4 = (bf16[8,1408]{1,0:T(8,128)(2,1)S(1)}, bf16[8,1408]{1,0:T(8,128)(2,1)S(1)}, u32[]{:S(2)}, u32[]{:S(2)}) collective-permute-start(bf16[8,1408]{1,0:T(8,128)(2,1)S(1)} %add_convert_fusion.own_ref), channel_id=1, source_target_pairs={{0,16},{1,17},{2,18},{3,19},{4,20},{5,21},{6,22},{7,23},{8,24},{9,... | collective-permute-start | bytes 67592 | tf_op jit(solution)/shard_map/ppermute | solution.py:270
  52.5 4.2 %collective-permute-done.4.other_ref = bf16[8,1408]{1,0:T(8,128)(2,1)S(1)} collective-permute-done((bf16[8,1408]{1,0:T(8,128)(2,1)S(1)}, bf16[8,1408]{1,0:T(8,128)(2,1)S(1)}, u32[]{:S(2)}, u32[]{:S(2)}) %collective-permute-start.4) | collective-permute-done | bytes 22560 | tf_op jit(solution)/shard_map/ppermute | solution.py:270
  56.8 0.6 %shard_map.115 = (f32[8,1280]{1,0:T(8,128)}, f32[1,8]{1,0:T(1,128)}) custom-call(bf16[8,1408]{1,0:T(8,128)(2,1)S(1)} %add_convert_fusion.own_ref, bf16[8,1408]{1,0:T(8,128)(2,1)S(1)} %collective-permute-done.4.other_ref), custom_call_target="tpu_custom_call" | custom-call | flops 10000000 | bytes 45056 | tf_op jit(solution)/shard_map/pallas_call | solution.py:238
  (29 shorter events, 0.8 us)
Async XLA Ops:
  0.6 18.7 %copy-start = (bf16[1,1280,1024]{2,1,0:T(8,128)(2,1)S(1)}, bf16[1,1280,1024]{2,1,0:T(8,128)(2,1)}, u32[]{:S(2)}) copy-start(bf16[1,1280,1024]{2,1,0:T(8,128)(2,1)} %one_ref.1) | copy-start | bytes 7864324
  19.3 1.7 %copy-start.1 = (bf16[1,1024,1280]{2,1,0:T(8,128)(2,1)S(1)}, bf16[1,1024,1280]{2,1,0:T(8,128)(2,1)}, u32[]{:S(2)}) copy-start(bf16[1,1024,1280]{2,1,0:T(8,128)(2,1)} %two_ref.1) | copy-start | bytes 7864324
  21.0 17.3 %copy-start.2 = (bf16[1,128,1280]{2,1,0:T(8,128)(2,1)S(1)}, bf16[1,128,1280]{2,1,0:T(8,128)(2,1)}, u32[]{:S(2)}) copy-start(bf16[1,128,1280]{2,1,0:T(8,128)(2,1)} %tok_ref.3) | copy-start | bytes 983044
  21.0 17.3 %copy-start.3 = (bf16[1,128,1280]{2,1,0:T(8,128)(2,1)S(1)}, bf16[1,128,1280]{2,1,0:T(8,128)(2,1)}, u32[]{:S(2)}) copy-start(bf16[1,128,1280]{2,1,0:T(8,128)(2,1)} %grad_ref.1) | copy-start | bytes 983044
  21.0 17.3 %copy-start.5 = (bf16[1280,8]{0,1:T(8,128)(2,1)S(1)}, bf16[1280,8]{0,1:T(8,128)(2,1)}, u32[]{:S(2)}) copy-start(bf16[1280,8]{0,1:T(8,128)(2,1)} %param.8) | copy-start | bytes 61444
  21.0 17.3 %copy-start.6 = (f32[8]{0:T(128)S(1)}, f32[8]{0:T(128)}, u32[]{:S(2)}) copy-start(f32[8]{0:T(128)} %param.9) | copy-start | bytes 100
  23.6 0.7 %copy-start.4 = (bf16[64,1408]{1,0:T(8,128)(2,1)}, bf16[64,1408]{1,0:T(8,128)(2,1)S(1)}, u32[]{:S(2)}) copy-start(bf16[64,1408]{1,0:T(8,128)(2,1)S(1)} %get-tuple-element.31) | copy-start | bytes 540676
  24.3 0.6 %copy-start.7 = (bf16[16,1280]{1,0:T(8,128)(2,1)}, bf16[16,1280]{1,0:T(8,128)(2,1)S(1)}, u32[]{:S(2)}) copy-start(bf16[16,1280]{1,0:T(8,128)(2,1)S(1)} %get-tuple-element.35.left_ref) | copy-start | bytes 122884
  24.9 0.6 %copy-start.9 = (bf16[16,1024]{1,0:T(8,128)(2,1)}, bf16[16,1024]{1,0:T(8,128)(2,1)S(1)}, u32[]{:S(2)}) copy-start(bf16[16,1024]{1,0:T(8,128)(2,1)S(1)} %get-tuple-element.38.left_ref) | copy-start | bytes 98308
  25.5 0.6 %copy-start.11 = (bf16[16,1024]{1,0:T(8,128)(2,1)}, bf16[16,1024]{1,0:T(8,128)(2,1)S(1)}, u32[]{:S(2)}) copy-start(bf16[16,1024]{1,0:T(8,128)(2,1)S(1)} %get-tuple-element.36.right_ref) | copy-start | bytes 98308
  38.2 6.5 %copy-start.10 = (bf16[16,1024]{1,0:T(8,128)(2,1)S(1)}, bf16[16,1024]{1,0:T(8,128)(2,1)}, u32[]{:S(2)}) copy-start(bf16[16,1024]{1,0:T(8,128)(2,1)} %copy-done.9) | copy-start | bytes 98308
  38.9 1.2 %collective-permute-start = (f32[8,1408]{1,0:T(8,128)S(1)}, f32[8,1408]{1,0:T(8,128)S(1)}, u32[]{:S(2)}, u32[]{:S(2)}) collective-permute-start(f32[8,1408]{1,0:T(8,128)S(1)} %get-tuple-element.34), channel_id=1, source_target_pairs={{0,2},{1,3},{2,0},{3,1},{4,6},{5,7},{6,4},{7,5},{8,10},{9,11},{10,... | collective-permute-start | bytes 135176 | tf_op jit(solution)/shard_map/ppermute | solution.py:270
  40.1 3.9 %collective-permute-start.1 = (bf16[8,1408]{1,0:T(8,128)(2,1)S(1)}, bf16[8,1408]{1,0:T(8,128)(2,1)S(1)}, u32[]{:S(2)}, u32[]{:S(2)}) collective-permute-start(bf16[8,1408]{1,0:T(8,128)(2,1)S(1)} %add_convert_fusion.3), channel_id=1, source_target_pairs={{0,1},{1,0},{2,3},{3,2},{4,5},{5,4},{6,7},{7,6},{8,9},{9,8},{10,11... | collective-permute-start | bytes 67592 | tf_op jit(solution)/shard_map/ppermute | solution.py:270
  40.4 0.8 %copy-start.8 = (bf16[16,1280]{1,0:T(8,128)(2,1)S(1)}, bf16[16,1280]{1,0:T(8,128)(2,1)}, u32[]{:S(2)}) copy-start(bf16[16,1280]{1,0:T(8,128)(2,1)} %copy-done.7) | copy-start | bytes 122884
  41.2 0.8 %copy-start.12 = (bf16[16,1024]{1,0:T(8,128)(2,1)S(1)}, bf16[16,1024]{1,0:T(8,128)(2,1)}, u32[]{:S(2)}) copy-start(bf16[16,1024]{1,0:T(8,128)(2,1)} %copy-done.11) | copy-start | bytes 98308
  44.0 3.9 %collective-permute-start.2 = (bf16[8,1408]{1,0:T(8,128)(2,1)S(1)}, bf16[8,1408]{1,0:T(8,128)(2,1)S(1)}, u32[]{:S(2)}, u32[]{:S(2)}) collective-permute-start(bf16[8,1408]{1,0:T(8,128)(2,1)S(1)} %add_convert_fusion.2), channel_id=1, source_target_pairs={{0,4},{1,5},{2,6},{3,7},{4,0},{5,1},{6,2},{7,3},{8,12},{9,13},{10,... | collective-permute-start | bytes 67592 | tf_op jit(solution)/shard_map/ppermute | solution.py:270
  47.9 3.9 %collective-permute-start.3 = (bf16[8,1408]{1,0:T(8,128)(2,1)S(1)}, bf16[8,1408]{1,0:T(8,128)(2,1)S(1)}, u32[]{:S(2)}, u32[]{:S(2)}) collective-permute-start(bf16[8,1408]{1,0:T(8,128)(2,1)S(1)} %add_convert_fusion.1), channel_id=1, source_target_pairs={{0,8},{1,9},{2,10},{3,11},{4,12},{5,13},{6,14},{7,15},{8,0},{9,1},... | collective-permute-start | bytes 67592 | tf_op jit(solution)/shard_map/ppermute | solution.py:270
  51.8 5.0 %collective-permute-start.4 = (bf16[8,1408]{1,0:T(8,128)(2,1)S(1)}, bf16[8,1408]{1,0:T(8,128)(2,1)S(1)}, u32[]{:S(2)}, u32[]{:S(2)}) collective-permute-start(bf16[8,1408]{1,0:T(8,128)(2,1)S(1)} %add_convert_fusion.own_ref), channel_id=1, source_target_pairs={{0,16},{1,17},{2,18},{3,19},{4,20},{5,21},{6,22},{7,23},{8,24},{9,... | collective-permute-start | bytes 67592 | tf_op jit(solution)/shard_map/ppermute | solution.py:270

commit v3 on v2

--- a/solution.py
+++ b/solution.py
@@ -45,6 +45,14 @@
 
 def pick(left_key, left_size, right, right_key):
     return dot(selection((left_size, right.shape[0]), left_key, right_key), right, ((1,), (0,)))
+
+
+def store_blocks(ref, rows):
+    ref[...] = rows.astype(BF).reshape(ref.shape)
+
+
+def load_blocks(ref):
+    return ref[...].reshape(2 * ref.shape[0], ref.shape[2])
 
 
 def itself(row):
@@ -134,7 +142,7 @@
     arrived[3].wait()
     dys = dot(comb.astype(BF), grad_ref[0], ((1,), (0,)))
     rows = stack_rows(numer, dys, [jnp.sum(expo, 1, keepdims=True)])
-    sent_ref[...] = pick(expert_rows(plan, router_ref.shape[0]), sent_ref.shape[0], rows, itself).astype(BF)
+    store_blocks(sent_ref, pick(expert_rows(plan, router_ref.shape[0]), 2 * sent_ref.shape[0], rows, itself))
     logit_ref[...] = logit
     inv_ref[...] = inv_x
 
@@ -144,7 +152,7 @@
 ):
     width = one_ref.shape[1]
     key = image_rows(images, halves)
-    sums = pick(itself, 2 * images, got_ref[...], key)
+    sums = pick(itself, 2 * images, load_blocks(got_ref), key)
     den = sums[:images, width : width + 1] + sums[images:, width : width + 1]
     rows = (sums[:images, :width] / den).astype(BF)
     grad_rows = sums[images:, :width].astype(BF)
@@ -157,7 +165,7 @@
     in_part = dot(dact, one_ref[0], ((1,), (1,)))
     corr = jnp.sum(dact.astype(F32) * act, 1, keepdims=True)
     packed = stack_rows(out_part, in_part, [den, corr])
-    back_ref[...] = pick(key, back_ref.shape[0], packed, itself).astype(BF)
+    store_blocks(back_ref, pick(key, 2 * back_ref.shape[0], packed, itself))
     rows_ref[...] = rows
     grad_rows_ref[...] = grad_rows
     hidden_ref[...] = hidden
@@ -184,7 +192,7 @@
     sums_ref, outs_ref, coef_ref, mix_ref, signal_ref,
 ):
     experts, width = router_ref.shape
-    sums = pick(itself, 2 * experts, back_ref[...], expert_rows(plan, router_ref.shape[0]))
+    sums = pick(itself, 2 * experts, load_blocks(back_ref), expert_rows(plan, router_ref.shape[0]))
     extras = sums[:experts, width:] + sums[experts:, width:]
     den = extras[:, :1] * (1.0 / (plan[0] * plan[1]))
     corr = extras[:, 1:2]
@@ -221,8 +229,11 @@
     grads_ref[0] = (grads - column * tok_ref[0].astype(F32)).astype(BF)
 
 
-def last_kernel(own_ref, other_ref, router_ref, scale_ref):
+def last_kernel(own_ref, other_ref, *refs):
+    *more, router_ref, scale_ref = refs
     sums = own_ref[...].astype(F32) + other_ref[...].astype(F32)
+    if more:
+        sums = sums + (more[0][...].astype(F32) + more[1][...].astype(F32))
     experts, width = router_ref.shape
     router_ref[...] = sums[:, :width]
     eye = iota((experts, experts), 0) == iota((experts, experts), 1)
@@ -259,30 +270,33 @@
     return out
 
 
-def exchange(block, devices):
-    moved = lax.all_to_all(
-        block.reshape(devices, 2, block.shape[1]), BOTH, split_axis=0, concat_axis=0, tiled=True
-    )
-    return moved.reshape(block.shape)
-
-
-def pair(term, place, devices):
-    return lax.ppermute(term, BOTH, [(d, d ^ (1 << place)) for d in range(devices)])
+def exchange(block):
+    return lax.all_to_all(block, BOTH, split_axis=0, concat_axis=0, tiled=True)
+
+
+def pair(term, mask, devices):
+    return lax.ppermute(term, BOTH, [(d, d ^ mask) for d in range(devices)])
 
 
 def sum_everywhere(term, devices, beside):
-    order = [1, 0] + list(range(2, log2(devices)))
+    term = term + pair(term, 2, devices)
+    masks = [1] + [1 << place for place in range(2, log2(devices))]
+    rounds = [masks[place : place + 2] for place in range(0, len(masks), 2)]
     done = []
-    term = term + pair(term, order[0], devices)
-    for place in order[1:]:
+    for group in rounds:
+        if group is not rounds[0]:
+            term = (terms[0].astype(F32) + terms[1].astype(F32)) + (
+                terms[2].astype(F32) + terms[3].astype(F32)
+            )
         own = term.astype(BF)
-        other = pair(own, place, devices)
+        terms = [own, pair(own, group[0], devices)]
+        if len(group) == 2:
+            terms += [pair(own, group[1], devices), pair(own, group[0] ^ group[1], devices)]
         if beside:
-            other, ready = lax.optimization_barrier((other, beside[0]))
+            terms[1], ready = lax.optimization_barrier((terms[1], beside[0]))
             beside = beside[1:]
             done.append(ready)
-        term = own.astype(F32) + other.astype(F32)
-    return own, other, done + list(beside)
+    return terms, done + list(beside)
 
 
 def shards(images, halves, tokens, grad_out, router, slot_scale, w_in, w_out):
@@ -297,21 +311,21 @@
     inputs = (tokens, grad_out, router_t, scale_row)
     sent, logit, inv_x = call(
         functools.partial(front_kernel, plan),
-        [((2 * devices, long), BF), ((experts, tok_rows), F32), ((1, tok_rows), F32)],
+        [((devices, 2, long), BF), ((experts, tok_rows), F32), ((1, tok_rows), F32)],
         *inputs,
         stays=range(4),
         buffers=[pltpu.VMEM(a.shape, a.dtype) for a in inputs] + [pltpu.SemaphoreType.DMA((4,))],
         flops=FRONT,
     )
-    got = exchange(sent, devices)
+    got = exchange(sent)
     back, rows, grad_rows, hidden, dact = call(
         functools.partial(expert_kernel, images, halves),
-        [((2 * devices, long), BF), ((images, width), BF), ((images, width), BF),
+        [((devices, 2, long), BF), ((images, width), BF), ((images, width), BF),
          ((images, hidden_dev), BF), ((images, hidden_dev), BF)],
         got, w_in, w_out,
         flops=10**9,
     )
-    back = exchange(back, devices)
+    back = exchange(back)
     grad_w_in = weight_grad(rows, dact)
     grad_w_out = weight_grad(hidden, grad_rows)
     sums, ys, coef, mix, signal = call(
@@ -325,11 +339,11 @@
         [(tokens.shape, BF), (tokens.shape, BF)],
         tokens, logit, ys, coef, mix, signal,
     )
-    own, other, (grad_w_in, grad_w_out, (combined, grad_tokens)) = sum_everywhere(
-        sums, devices, [grad_w_in, grad_w_out, (combined, grad_tokens)]
+    terms, (grad_w_in, (grad_w_out, combined, grad_tokens)) = sum_everywhere(
+        sums, devices, [grad_w_in, (grad_w_out, combined, grad_tokens)]
     )
     grad_router, grad_scale = call(
-        last_kernel, [((experts, width), F32), ((1, experts), F32)], own, other
+        last_kernel, [((experts, width), F32), ((1, experts), F32)], *terms
     )
     return (combined, grad_tokens, grad_router.T, grad_scale[0], grad_w_in, grad_w_out)
 

time: 57.7 us -> 49.1 us (0.85)
  waiting for transfers between devices: 8.92 us -> 1.85 us
  local copies, waits for them, and re-layouts: 7 us -> 0.03 us
  starting transfers between devices: 2.49 us -> 8.03 us
    ppermute x5 -> x7, waiting for transfers between devices: 8.92 us -> 1.85 us  [pair(): return lax.ppermute(term, BOTH, [(d, d ^ mask) for d in range(devices)])]
    unnamed x26 -> x12, local copies, waits for them, and re-layouts: 5.8 us -> 0.03 us
    ppermute x5 -> x7, starting transfers between devices: 2.49 us -> 8.03 us  [pair(): return lax.ppermute(term, BOTH, [(d, d ^ mask) for d in range(devices)])]
    reshape x4 -> x0, local copies, waits for them, and re-layouts: 1.2 us -> none  [the longest x2 1.06 us: exchange(): block.reshape(devices, 2, block.shape[1])]
  transfers between devices with their start and end apart: 5 -> 7, of which waited for: 5 -> 3; matrix products, arithmetic and copies ran while one was open for 0% -> 0% of each run, Pallas kernels for 9% -> 10%
where the time goes in v3:
time: 49.1 us; the launch traced here: 48.9 us
  blocking collectives  27.6 us (56%)
  Pallas kernels  10.6 us (22%)
  starting transfers between devices  8.03 us (16%)
  waiting for transfers between devices  1.85 us (4%)
  between operations  0.75 us (2%)
    all_to_all x2, blocking collectives, exchange(): return lax.all_to_all(block, BOTH, split_axis=0, concat_axis=0, tiled=True)  27.6 us
    pallas_call x7, Pallas kernels, call(): pl.pallas_call(kernel, out_shape=[jax.ShapeDtypeStruct(shape, dtype) for...  10.6 us
    ppermute x7, starting transfers between devices, pair(): return lax.ppermute(term, BOTH, [(d, d ^ mask) for d in range(devices)])  8.03 us
    ppermute x7, waiting for transfers between devices, pair(): return lax.ppermute(term, BOTH, [(d, d ^ mask) for d in range(devices)])  1.85 us
  transfers between devices with their start and end apart: 7, of which 3 were waited for; matrix products, arithmetic and copies ran while one was open for 0% of the time, Pallas kernels for 10%

profile of v3, /device:TPU:0, one launch (start us, length us, event | category | flops | bytes accessed | tf_op | source)
XLA Modules:
  0.0 48.9 jit_solution(2853705896232479663)
XLA Ops:
  0.7 2.0 %shard_map.109 = (bf16[32,2,1408]{2,1,0:T(2,128)(2,1)S(1)}, f32[8,128]{1,0:T(8,128)S(1)}, f32[1,128]{1,0:T(1,128)S(1)}) custom-call(bf16[1,128,1280]{2,1,0:T(8,128)(2,1)} %tok_ref.3, bf16[1,128,1280]{2,1,0:T(8,128)(2,1)} %grad_ref.1, bf16[8,1280]{1,0:T(8,128)(2,1)} %bitcast.4, f32[1,8]{1,0:T(1,128)} %bitcast.6), custom_call_target="tpu_custom_call" | custom-call | flops 4000000000 | bytes 675872 | tf_op jit(solution)/shard_map/pallas_call | solution.py:249
  2.6 16.5 %all_to_all.10.got_ref = bf16[32,2,1408]{2,1,0:T(2,128)(2,1)S(1)} all-to-all(bf16[32,2,1408]{2,1,0:T(2,128)(2,1)S(1)} %get-tuple-element.29), channel_id=1, replica_groups=mesh['img'=16,'tok'=2] {'img','tok'}, dimensions={0} | all-to-all | bytes 360448 | tf_op jit(solution)/shard_map/all_to_all | solution.py:274
  19.2 0.0 copy-start.4
  19.2 0.0 copy-start.5
  19.2 2.6 %shard_map.110 = (bf16[32,2,1408]{2,1,0:T(2,128)(2,1)S(1)}, bf16[16,1280]{1,0:T(8,128)(2,1)S(1)}, bf16[16,1280]{1,0:T(8,128)(2,1)S(1)}, bf16[16,1024]{1,0:T(8,128)(2,1)S(1)}, bf16[16,1024]{1,0:T(8,128)(2,1)S(1)}) custom-call(bf16[32,2,1408]{2,1,0:T(2,128)(2,1)S(1)} %all_to_all.10.got_ref, bf16[1,1280,1024]{2,1,0:T(8,128)(2,1)S(1)} %copy-done, ...), custom_call_target="tpu_custom_call" | custom-call | flops 1000000000 | bytes 5423104 | tf_op jit(solution)/shard_map/pallas_call | solution.py:249
  21.7 11.1 %all_to_all.11.back_ref = bf16[32,2,1408]{2,1,0:T(2,128)(2,1)S(1)} all-to-all(bf16[32,2,1408]{2,1,0:T(2,128)(2,1)S(1)} %get-tuple-element.30), channel_id=1, replica_groups=mesh['img'=16,'tok'=2] {'img','tok'}, dimensions={0} | all-to-all | bytes 360448 | tf_op jit(solution)/shard_map/all_to_all | solution.py:274
  32.9 0.5 %shard_map.111 = (f32[8,1408]{1,0:T(8,128)S(1)}, bf16[8,1280]{1,0:T(8,128)(2,1)S(1)}, bf16[16,128]{1,0:T(8,128)(2,1)S(1)}, bf16[16,1280]{1,0:T(8,128)(2,1)S(1)}, f32[1,128]{1,0:T(1,128)S(1)}) custom-call(bf16[32,2,1408]{2,1,0:T(2,128)(2,1)S(1)} %all_to_all.11.back_ref, bf16[1,128,1280]{2,1,0:T(8,128)(2,1)S(1)} %copy-done.2, ...), custom_call_target="tpu_custom_call" | custom-call | flops 10000000 | bytes 860704 | tf_op jit(solution)/shard_map/pallas_call | solution.py:249
  33.4 0.0 collective-permute-start
  33.4 1.2 %collective-permute-done = f32[8,1408]{1,0:T(8,128)S(1)} collective-permute-done((f32[8,1408]{1,0:T(8,128)S(1)}, f32[8,1408]{1,0:T(8,128)S(1)}, u32[]{:S(2)}, u32[]{:S(2)}) %collective-permute-start) | collective-permute-done | bytes 45088 | tf_op jit(solution)/shard_map/ppermute | solution.py:278
  34.7 0.3 collective-permute-start.1
  35.0 0.8 %collective-permute-start.2 = (bf16[8,1408]{1,0:T(8,128)(2,1)S(1)}, bf16[8,1408]{1,0:T(8,128)(2,1)S(1)}, u32[]{:S(2)}, u32[]{:S(2)}) collective-permute-start(bf16[8,1408]{1,0:T(8,128)(2,1)S(1)} %add_convert_fusion.1), channel_id=1, source_target_pairs={{0,4},{1,5},{2,6},{3,7},{4,0},{5,1},{6,2},{7,3},{8,12},{9,13},{10,... | collective-permute-start | bytes 67592 | tf_op jit(solution)/shard_map/ppermute | solution.py:278
  35.8 2.4 %collective-permute-start.3 = (bf16[8,1408]{1,0:T(8,128)(2,1)S(1)}, bf16[8,1408]{1,0:T(8,128)(2,1)S(1)}, u32[]{:S(2)}, u32[]{:S(2)}) collective-permute-start(bf16[8,1408]{1,0:T(8,128)(2,1)S(1)} %add_convert_fusion.1), channel_id=1, source_target_pairs={{0,5},{1,4},{2,7},{3,6},{4,1},{5,0},{6,3},{7,2},{8,13},{9,12},{10,... | collective-permute-start | bytes 67592 | tf_op jit(solution)/shard_map/ppermute | solution.py:278
  38.2 1.8 %shard_map.112 = bf16[1,1280,1024]{2,1,0:T(8,128)(2,1)} custom-call(bf16[16,1280]{1,0:T(8,128)(2,1)S(1)} %get-tuple-element.34.left_ref, bf16[16,1024]{1,0:T(8,128)(2,1)S(1)} %get-tuple-element.35.right_ref), custom_call_target="tpu_custom_call" | custom-call | flops 1000000000 | bytes 73728 | tf_op jit(solution)/shard_map/pallas_call | solution.py:249
  40.1 0.0 collective-permute-done.1
  40.1 0.0 collective-permute-done.2
  40.1 0.4 collective-permute-done.3
  40.5 0.8 %collective-permute-start.4 = (bf16[8,1408]{1,0:T(8,128)(2,1)S(1)}, bf16[8,1408]{1,0:T(8,128)(2,1)S(1)}, u32[]{:S(2)}, u32[]{:S(2)}) collective-permute-start(bf16[8,1408]{1,0:T(8,128)(2,1)S(1)} %add_convert_fusion.own_ref), channel_id=1, source_target_pairs={{0,8},{1,9},{2,10},{3,11},{4,12},{5,13},{6,14},{7,15},{8,0},{9,1},... | collective-permute-start | bytes 67592 | tf_op jit(solution)/shard_map/ppermute | solution.py:278
  41.3 1.4 %collective-permute-start.5 = (bf16[8,1408]{1,0:T(8,128)(2,1)S(1)}, bf16[8,1408]{1,0:T(8,128)(2,1)S(1)}, u32[]{:S(2)}, u32[]{:S(2)}) collective-permute-start(bf16[8,1408]{1,0:T(8,128)(2,1)S(1)} %add_convert_fusion.own_ref), channel_id=1, source_target_pairs={{0,16},{1,17},{2,18},{3,19},{4,20},{5,21},{6,22},{7,23},{8,24},{9,... | collective-permute-start | bytes 67592 | tf_op jit(solution)/shard_map/ppermute | solution.py:278
  42.6 2.3 %collective-permute-start.6 = (bf16[8,1408]{1,0:T(8,128)(2,1)S(1)}, bf16[8,1408]{1,0:T(8,128)(2,1)S(1)}, u32[]{:S(2)}, u32[]{:S(2)}) collective-permute-start(bf16[8,1408]{1,0:T(8,128)(2,1)S(1)} %add_convert_fusion.own_ref), channel_id=1, source_target_pairs={{0,24},{1,25},{2,26},{3,27},{4,28},{5,29},{6,30},{7,31},{8,16},{9,... | collective-permute-start | bytes 67592 | tf_op jit(solution)/shard_map/ppermute | solution.py:278
  45.0 1.9 %shard_map.113 = bf16[1,1024,1280]{2,1,0:T(8,128)(2,1)} custom-call(bf16[16,1024]{1,0:T(8,128)(2,1)S(1)} %get-tuple-element.37.left_ref, bf16[16,1280]{1,0:T(8,128)(2,1)S(1)} %get-tuple-element.38.right_ref), custom_call_target="tpu_custom_call" | custom-call | flops 1000000000 | bytes 73728 | tf_op jit(solution)/shard_map/pallas_call | solution.py:249
  46.9 1.1 %shard_map.114 = (bf16[1,128,1280]{2,1,0:T(8,128)(2,1)}, bf16[1,128,1280]{2,1,0:T(8,128)(2,1)}) custom-call(bf16[1,128,1280]{2,1,0:T(8,128)(2,1)S(1)} %copy-done.2, f32[8,128]{1,0:T(8,128)S(1)} %get-tuple-element.31.logit_ref, bf16[8,1280]{1,0:T(8,128)(2,1)S(1)} %get-tuple-element.39.outs_ref, bf16[16,128]{1,0:T(8,128)(2,1)S(1)} %get-tuple-element.40.coef_ref, ...), custom_call_target="tpu_custom_call" | custom-call | flops 10000000 | bytes 397824 | tf_op jit(solution)/shard_map/pallas_call | solution.py:249
  48.0 0.0 collective-permute-done.4.other_ref
  48.0 0.2 collective-permute-done.6.refs_1_
  48.2 0.6 %shard_map.115 = (f32[8,1280]{1,0:T(8,128)}, f32[1,8]{1,0:T(1,128)}) custom-call(bf16[8,1408]{1,0:T(8,128)(2,1)S(1)} %add_convert_fusion.own_ref, bf16[8,1408]{1,0:T(8,128)(2,1)S(1)} %collective-permute-done.4.other_ref, bf16[8,1408]{1,0:T(8,128)(2,1)S(1)} %collective-permute-done.5.refs_0_, bf16[8,1408]{1,0:T(8,128)(2,1)S(1)} %collective-permute-done.6.refs_1_), custom_call_target="tpu_custom_call" | custom-call | flops 10000000 | bytes 90112 | tf_op jit(solution)/shard_map/pallas_call | solution.py:249
  (13 shorter events, 0.0 us)
Async XLA Ops:
  0.6 18.5 %copy-start = (bf16[1,1280,1024]{2,1,0:T(8,128)(2,1)S(1)}, bf16[1,1280,1024]{2,1,0:T(8,128)(2,1)}, u32[]{:S(2)}) copy-start(bf16[1,1280,1024]{2,1,0:T(8,128)(2,1)} %one_ref.1) | copy-start | bytes 7864324
  0.6 18.5 %copy-start.1 = (bf16[1,1024,1280]{2,1,0:T(8,128)(2,1)S(1)}, bf16[1,1024,1280]{2,1,0:T(8,128)(2,1)}, u32[]{:S(2)}) copy-start(bf16[1,1024,1280]{2,1,0:T(8,128)(2,1)} %two_ref.1) | copy-start | bytes 7864324
  19.2 13.7 %copy-start.2 = (bf16[1,128,1280]{2,1,0:T(8,128)(2,1)S(1)}, bf16[1,128,1280]{2,1,0:T(8,128)(2,1)}, u32[]{:S(2)}) copy-start(bf16[1,128,1280]{2,1,0:T(8,128)(2,1)} %tok_ref.3) | copy-start | bytes 983044
  19.2 13.7 %copy-start.3 = (bf16[1,128,1280]{2,1,0:T(8,128)(2,1)S(1)}, bf16[1,128,1280]{2,1,0:T(8,128)(2,1)}, u32[]{:S(2)}) copy-start(bf16[1,128,1280]{2,1,0:T(8,128)(2,1)} %grad_ref.1) | copy-start | bytes 983044
  19.2 13.7 %copy-start.4 = (bf16[1280,8]{0,1:T(8,128)(2,1)S(1)}, bf16[1280,8]{0,1:T(8,128)(2,1)}, u32[]{:S(2)}) copy-start(bf16[1280,8]{0,1:T(8,128)(2,1)} %param.8) | copy-start | bytes 61444
  19.2 13.7 %copy-start.5 = (f32[8]{0:T(128)S(1)}, f32[8]{0:T(128)}, u32[]{:S(2)}) copy-start(f32[8]{0:T(128)} %param.9) | copy-start | bytes 100
  33.4 1.2 %collective-permute-start = (f32[8,1408]{1,0:T(8,128)S(1)}, f32[8,1408]{1,0:T(8,128)S(1)}, u32[]{:S(2)}, u32[]{:S(2)}) collective-permute-start(f32[8,1408]{1,0:T(8,128)S(1)} %get-tuple-element.33), channel_id=1, source_target_pairs={{0,2},{1,3},{2,0},{3,1},{4,6},{5,7},{6,4},{7,5},{8,10},{9,11},{10,... | collective-permute-start | bytes 135176 | tf_op jit(solution)/shard_map/ppermute | solution.py:278
  34.7 5.4 %collective-permute-start.1 = (bf16[8,1408]{1,0:T(8,128)(2,1)S(1)}, bf16[8,1408]{1,0:T(8,128)(2,1)S(1)}, u32[]{:S(2)}, u32[]{:S(2)}) collective-permute-start(bf16[8,1408]{1,0:T(8,128)(2,1)S(1)} %add_convert_fusion.1), channel_id=1, source_target_pairs={{0,1},{1,0},{2,3},{3,2},{4,5},{5,4},{6,7},{7,6},{8,9},{9,8},{10,11... | collective-permute-start | bytes 67592 | tf_op jit(solution)/shard_map/ppermute | solution.py:278
  35.0 5.1 %collective-permute-start.2 = (bf16[8,1408]{1,0:T(8,128)(2,1)S(1)}, bf16[8,1408]{1,0:T(8,128)(2,1)S(1)}, u32[]{:S(2)}, u32[]{:S(2)}) collective-permute-start(bf16[8,1408]{1,0:T(8,128)(2,1)S(1)} %add_convert_fusion.1), channel_id=1, source_target_pairs={{0,4},{1,5},{2,6},{3,7},{4,0},{5,1},{6,2},{7,3},{8,12},{9,13},{10,... | collective-permute-start | bytes 67592 | tf_op jit(solution)/shard_map/ppermute | solution.py:278
  35.8 4.7 %collective-permute-start.3 = (bf16[8,1408]{1,0:T(8,128)(2,1)S(1)}, bf16[8,1408]{1,0:T(8,128)(2,1)S(1)}, u32[]{:S(2)}, u32[]{:S(2)}) collective-permute-start(bf16[8,1408]{1,0:T(8,128)(2,1)S(1)} %add_convert_fusion.1), channel_id=1, source_target_pairs={{0,5},{1,4},{2,7},{3,6},{4,1},{5,0},{6,3},{7,2},{8,13},{9,12},{10,... | collective-permute-start | bytes 67592 | tf_op jit(solution)/shard_map/ppermute | solution.py:278
  40.5 7.5 %collective-permute-start.4 = (bf16[8,1408]{1,0:T(8,128)(2,1)S(1)}, bf16[8,1408]{1,0:T(8,128)(2,1)S(1)}, u32[]{:S(2)}, u32[]{:S(2)}) collective-permute-start(bf16[8,1408]{1,0:T(8,128)(2,1)S(1)} %add_convert_fusion.own_ref), channel_id=1, source_target_pairs={{0,8},{1,9},{2,10},{3,11},{4,12},{5,13},{6,14},{7,15},{8,0},{9,1},... | collective-permute-start | bytes 67592 | tf_op jit(solution)/shard_map/ppermute | solution.py:278
  41.3 6.8 %collective-permute-start.5 = (bf16[8,1408]{1,0:T(8,128)(2,1)S(1)}, bf16[8,1408]{1,0:T(8,128)(2,1)S(1)}, u32[]{:S(2)}, u32[]{:S(2)}) collective-permute-start(bf16[8,1408]{1,0:T(8,128)(2,1)S(1)} %add_convert_fusion.own_ref), channel_id=1, source_target_pairs={{0,16},{1,17},{2,18},{3,19},{4,20},{5,21},{6,22},{7,23},{8,24},{9,... | collective-permute-start | bytes 67592 | tf_op jit(solution)/shard_map/ppermute | solution.py:278
  42.6 5.6 %collective-permute-start.6 = (bf16[8,1408]{1,0:T(8,128)(2,1)S(1)}, bf16[8,1408]{1,0:T(8,128)(2,1)S(1)}, u32[]{:S(2)}, u32[]{:S(2)}) collective-permute-start(bf16[8,1408]{1,0:T(8,128)(2,1)S(1)} %add_convert_fusion.own_ref), channel_id=1, source_target_pairs={{0,24},{1,25},{2,26},{3,27},{4,28},{5,29},{6,30},{7,31},{8,16},{9,... | collective-permute-start | bytes 67592 | tf_op jit(solution)/shard_map/ppermute | solution.py:278

commit v4 on v3

--- a/solution.py
+++ b/solution.py
@@ -14,7 +14,7 @@
 F32 = jnp.float32
 BOTH = ("img", "tok")
 LANES = 128
-FRONT = 4 * 10**9
+FRONT = 2 * 10**10
 
 
 def dot(left, right, dims):
@@ -122,6 +122,11 @@
     return key
 
 
+def scores(tok, tok_f, router, column):
+    inv_x = row_of(lax.rsqrt(jnp.sum(tok_f * tok_f, 1, keepdims=True) + EPSILON))
+    return dot(router, tok, ((1,), (1,))) * inv_x * column, inv_x
+
+
 def front_kernel(
     plan, tok_hbm, grad_hbm, router_hbm, scale_hbm, sent_ref, logit_ref, inv_ref,
     tok_ref, grad_ref, router_ref, scale_ref, sems,
@@ -133,10 +138,8 @@
         copy.wait()
     tok = tok_ref[0]
     tok_f = tok.astype(F32)
-    inv_x = row_of(lax.rsqrt(jnp.sum(tok_f * tok_f, 1, keepdims=True) + EPSILON))
     _, inv_p, scale = slot_column(router_ref, scale_ref)
-    raw = dot(router_ref[...], tok, ((1,), (1,)))
-    logit = raw * inv_x * (inv_p * scale)
+    logit, inv_x = scores(tok, tok_f, router_ref[...], inv_p * scale)
     expo, comb = softmax(logit)
     numer = dot(expo.astype(BF), tok, ((1,), (0,)))
     arrived[3].wait()
@@ -187,37 +190,43 @@
         copy.wait()
 
 
-def middle_kernel(
-    plan, back_ref, tok_ref, grad_ref, logit_ref, inv_ref, router_ref, scale_ref,
-    sums_ref, outs_ref, coef_ref, mix_ref, signal_ref,
-):
+def middle_kernel(plan, halves, *refs):
+    back_ref, logit_ref, inv_ref, router_ref, scale_ref = refs[:5]
+    tok_refs, grad_refs = refs[5 : 5 + halves], refs[5 + halves : 5 + 2 * halves]
+    sums_ref, outs_ref, coef_ref, mix_ref, signal_ref = refs[5 + 2 * halves :]
     experts, width = router_ref.shape
-    sums = pick(itself, 2 * experts, load_blocks(back_ref), expert_rows(plan, router_ref.shape[0]))
+    sums = pick(itself, 2 * experts, load_blocks(back_ref), expert_rows(plan, experts))
     extras = sums[:experts, width:] + sums[experts:, width:]
     den = extras[:, :1] * (1.0 / (plan[0] * plan[1]))
     corr = extras[:, 1:2]
     ys = sums[:experts, :width].astype(BF)
     dxs = sums[experts:, :width].astype(BF)
     router_f, inv_p, scale = slot_column(router_ref, scale_ref)
-    tok = tok_ref[0]
-    logit = logit_ref[...]
-    inv_x = inv_ref[...]
-    expo, comb = softmax(logit)
-    dcomb = dot(ys, grad_ref[0], ((1,), (1,)))
-    ddisp = dot(dxs, tok, ((1,), (1,)))
-    dlc = comb * (dcomb - jnp.sum(comb * dcomb, 0, keepdims=True))
-    grad_l = expo / den * (ddisp - corr) + dlc
-    product = grad_l * logit
-    grad_q = (grad_l * inv_x * (inv_p * scale)).astype(BF)
-    outer = dot(grad_q, tok, ((1,), (0,)))
-    total = jnp.sum(product, 1, keepdims=True)
+    column = inv_p * scale
+    outer = total = 0.0
+    for half, (tok_ref, grad_ref) in enumerate(zip(tok_refs, grad_refs)):
+        tok = tok_ref[0]
+        if half == 0:
+            logit, inv_x = logit_ref[...], inv_ref[...]
+        else:
+            logit, inv_x = scores(tok, tok.astype(F32), router_ref[...], column)
+        expo, comb = softmax(logit)
+        dcomb = dot(ys, grad_ref[0], ((1,), (1,)))
+        ddisp = dot(dxs, tok, ((1,), (1,)))
+        dlc = comb * (dcomb - jnp.sum(comb * dcomb, 0, keepdims=True))
+        grad_l = expo / den * (ddisp - corr) + dlc
+        product = grad_l * logit
+        grad_q = (grad_l * inv_x * column).astype(BF)
+        outer += dot(grad_q, tok, ((1,), (0,)))
+        total += jnp.sum(product, 1, keepdims=True)
+        if half == 0:
+            coef_ref[...] = jnp.concatenate([expo, grad_q.astype(F32)], 0).astype(BF)
+            signal_ref[...] = inv_x * inv_x * jnp.sum(product, 0, keepdims=True)
     local = outer - inv_p * inv_p * total * router_f
     lane = iota((experts, LANES), 1)
     sums_ref[...] = jnp.concatenate([local, jnp.where(lane == 0, total / scale, 0.0)], 1)
     outs_ref[...] = ys
-    coef_ref[...] = jnp.concatenate([expo, grad_q.astype(F32)], 0).astype(BF)
     mix_ref[...] = jnp.concatenate([dxs.astype(F32) / den, router_f], 0).astype(BF)
-    signal_ref[...] = inv_x * inv_x * jnp.sum(product, 0, keepdims=True)
 
 
 def tail_kernel(tok_ref, logit_ref, outs_ref, coef_ref, mix_ref, signal_ref, combined_ref, grads_ref):
@@ -274,14 +283,14 @@
     return lax.all_to_all(block, BOTH, split_axis=0, concat_axis=0, tiled=True)
 
 
-def pair(term, mask, devices):
-    return lax.ppermute(term, BOTH, [(d, d ^ mask) for d in range(devices)])
-
-
-def sum_everywhere(term, devices, beside):
-    term = term + pair(term, 2, devices)
-    masks = [1] + [1 << place for place in range(2, log2(devices))]
-    rounds = [masks[place : place + 2] for place in range(0, len(masks), 2)]
+def pair(term, mask, axis, size):
+    return lax.ppermute(term, axis, [(d, d ^ mask) for d in range(size)])
+
+
+def sum_images(term, images, beside):
+    masks = [1 << place for place in range(log2(images))]
+    term = term + pair(term, masks[0], "img", images)
+    rounds = [masks[place : place + 2] for place in range(1, len(masks), 2)]
     done = []
     for group in rounds:
         if group is not rounds[0]:
@@ -289,9 +298,10 @@
                 terms[2].astype(F32) + terms[3].astype(F32)
             )
         own = term.astype(BF)
-        terms = [own, pair(own, group[0], devices)]
+        terms = [own, pair(own, group[0], "img", images)]
         if len(group) == 2:
-            terms += [pair(own, group[1], devices), pair(own, group[0] ^ group[1], devices)]
+            terms.append(pair(own, group[1], "img", images))
+            terms.append(pair(own, group[0] ^ group[1], "img", images))
         if beside:
             terms[1], ready = lax.optimization_barrier((terms[1], beside[0]))
             beside = beside[1:]
@@ -317,7 +327,9 @@
         buffers=[pltpu.VMEM(a.shape, a.dtype) for a in inputs] + [pltpu.SemaphoreType.DMA((4,))],
         flops=FRONT,
     )
-    got = exchange(sent)
+    toks = [pair(tokens, mask, "tok", halves) for mask in range(1, halves)]
+    grads = [pair(grad_out, mask, "tok", halves) for mask in range(1, halves)]
+    got, toks, grads = lax.optimization_barrier((exchange(sent), toks, grads))
     back, rows, grad_rows, hidden, dact = call(
         functools.partial(expert_kernel, images, halves),
         [((devices, 2, long), BF), ((images, width), BF), ((images, width), BF),
@@ -329,18 +341,18 @@
     grad_w_in = weight_grad(rows, dact)
     grad_w_out = weight_grad(hidden, grad_rows)
     sums, ys, coef, mix, signal = call(
-        functools.partial(middle_kernel, plan),
+        functools.partial(middle_kernel, plan, halves),
         [((experts, long), F32), ((experts, width), BF), ((2 * experts, tok_rows), BF),
          ((2 * experts, width), BF), ((1, tok_rows), F32)],
-        back, tokens, grad_out, logit, inv_x, router_t, scale_row,
+        back, logit, inv_x, router_t, scale_row, tokens, *toks, grad_out, *grads,
     )
     combined, grad_tokens = call(
         tail_kernel,
         [(tokens.shape, BF), (tokens.shape, BF)],
         tokens, logit, ys, coef, mix, signal,
     )
-    terms, (grad_w_in, (grad_w_out, combined, grad_tokens)) = sum_everywhere(
-        sums, devices, [grad_w_in, (grad_w_out, combined, grad_tokens)]
+    terms, (grad_w_in, (grad_w_out, combined, grad_tokens)) = sum_images(
+        sums, images, [grad_w_in, (grad_w_out, combined, grad_tokens)]
     )
     grad_router, grad_scale = call(
         last_kernel, [((experts, width), F32), ((1, experts), F32)], *terms

time: 49.1 us -> 62 us (1.26)
  waiting for transfers between devices: 1.85 us -> 18.5 us
  blocking collectives: 27.6 us -> 13.9 us
  starting transfers between devices: 8.03 us -> 13.6 us
  local copies, waits for them, and re-layouts: 0.03 us -> 3.88 us
    ppermute x7, waiting for transfers between devices: 1.85 us -> 18.5 us  [pair(): return lax.ppermute(term, axis, [(d, d ^ mask) for d in range(size)])]
    all_to_all x2 -> x1, blocking collectives: 27.6 us -> 13.9 us  [exchange(): return lax.all_to_all(block, BOTH, split_axis=0, concat_axis=0, tiled=True)]
    all_to_all x0 -> x1, starting transfers between devices: none -> 7.3 us  [exchange(): return lax.all_to_all(block, BOTH, split_axis=0, concat_axis=0, tiled=True)]
    unnamed x12 -> x22, local copies, waits for them, and re-layouts: 0.03 us -> 3.88 us
    ppermute x7, starting transfers between devices: 8.03 us -> 6.34 us  [pair(): return lax.ppermute(term, axis, [(d, d ^ mask) for d in range(size)])]
  transfers between devices with their start and end apart: 7 -> 8, of which waited for: 3 -> 4; matrix products, arithmetic and copies ran while one was open for 0% -> 0% of each run, Pallas kernels for 10% -> 8%
where the time goes in v4:
time: 62 us; the launch traced here: 61.8 us
  waiting for transfers between devices  18.5 us (30%)
  blocking collectives  13.9 us (22%)
  starting transfers between devices  13.6 us (22%)
  Pallas kernels  11 us (18%)
  local copies, waits for them, and re-layouts  3.88 us (6%)
  between operations  0.78 us (1%)
    ppermute x7, waiting for transfers between devices, pair(): return lax.ppermute(term, axis, [(d, d ^ mask) for d in range(size)])  18.5 us
    all_to_all x1, blocking collectives, exchange(): return lax.all_to_all(block, BOTH, split_axis=0, concat_axis=0, tiled=True)  13.9 us
    pallas_call x7, Pallas kernels, call(): pl.pallas_call(kernel, out_shape=[jax.ShapeDtypeStruct(shape, dtype) for...  11 us
    all_to_all x1, starting transfers between devices, exchange(): return lax.all_to_all(block, BOTH, split_axis=0, concat_axis=0, tiled=True)  7.3 us
    ppermute x7, starting transfers between devices, pair(): return lax.ppermute(term, axis, [(d, d ^ mask) for d in range(size)])  6.34 us
    unnamed x22, local copies, waits for them, and re-layouts  3.88 us
  transfers between devices with their start and end apart: 8, of which 4 were waited for; matrix products, arithmetic and copies ran while one was open for 0% of the time, Pallas kernels for 8%

profile of v4, /device:TPU:0, one launch (start us, length us, event | category | flops | bytes accessed | tf_op | source)
XLA Modules:
  0.0 61.8 jit_solution(10973765965636202647)
XLA Ops:
  0.7 2.0 %shard_map.109 = (bf16[32,2,1408]{2,1,0:T(2,128)(2,1)S(1)}, f32[8,128]{1,0:T(8,128)S(1)}, f32[1,128]{1,0:T(1,128)S(1)}) custom-call(bf16[1,128,1280]{2,1,0:T(8,128)(2,1)} %tok_ref.1, bf16[1,128,1280]{2,1,0:T(8,128)(2,1)} %refs_7_.1, bf16[8,1280]{1,0:T(8,128)(2,1)} %bitcast.4, f32[1,8]{1,0:T(1,128)} %bitcast.6), custom_call_target="tpu_custom_call" | custom-call | flops 20000000000 | bytes 675872 | tf_op jit(solution)/shard_map/pallas_call | solution.py:258
  2.7 0.7 %copy-done.8 = bf16[32,2,1408]{2,1,0:T(2,128)(2,1)} copy-done((bf16[32,2,1408]{2,1,0:T(2,128)(2,1)}, bf16[32,2,1408]{2,1,0:T(2,128)(2,1)S(1)}, u32[]{:S(2)}) %copy-start.8) | copy-done | bytes 180248
  3.3 7.3 %all-to-all-start = ((bf16[32,2,1408]{2,1,0:T(2,128)(2,1)}), bf16[32,2,1408]{2,1,0:T(2,128)(2,1)S(1)}, u32[]{:S(2)}, u32[]{:S(2)}) async-start(bf16[32,2,1408]{2,1,0:T(2,128)(2,1)} %copy-done.8), calls=%async_computation | async-start | bytes 360448 | tf_op jit(solution)/shard_map/all_to_all | solution.py:283
  10.6 1.8 %collective-permute-start = (bf16[1,128,1280]{2,1,0:T(8,128)(2,1)S(1)}, bf16[1,128,1280]{2,1,0:T(8,128)(2,1)S(1)}, u32[]{:S(2)}, u32[]{:S(2)}) collective-permute-start(bf16[1,128,1280]{2,1,0:T(8,128)(2,1)S(1)} %copy-done.2), channel_id=1, source_target_pairs={{0,1},{1,0},{2,3},{3,2},{4,5},{5,4},{6,7},{7,6},{8,9},{9,8},{10,11... | collective-permute-start | bytes 983048 | tf_op jit(solution)/shard_map/ppermute | solution.py:287
  12.5 0.3 collective-permute-start.1
  12.7 10.2 %collective-permute-done.refs_6_ = bf16[1,128,1280]{2,1,0:T(8,128)(2,1)S(1)} collective-permute-done((bf16[1,128,1280]{2,1,0:T(8,128)(2,1)S(1)}, bf16[1,128,1280]{2,1,0:T(8,128)(2,1)S(1)}, u32[]{:S(2)}, u32[]{:S(2)}) %collective-permute-start) | collective-permute-done | bytes 327712 | tf_op jit(solution)/shard_map/ppermute | solution.py:287
  22.9 0.7 %copy-done.4 = bf16[1,128,1280]{2,1,0:T(8,128)(2,1)} copy-done((bf16[1,128,1280]{2,1,0:T(8,128)(2,1)}, bf16[1,128,1280]{2,1,0:T(8,128)(2,1)S(1)}, u32[]{:S(2)}) %copy-start.4) | copy-done | bytes 327704
  23.6 5.8 %collective-permute-done.1.refs_8_ = bf16[1,128,1280]{2,1,0:T(8,128)(2,1)S(1)} collective-permute-done((bf16[1,128,1280]{2,1,0:T(8,128)(2,1)S(1)}, bf16[1,128,1280]{2,1,0:T(8,128)(2,1)S(1)}, u32[]{:S(2)}, u32[]{:S(2)}) %collective-permute-start.1) | collective-permute-done | bytes 327712 | tf_op jit(solution)/shard_map/ppermute | solution.py:287
  29.5 0.7 %copy-done.6 = bf16[1,128,1280]{2,1,0:T(8,128)(2,1)} copy-done((bf16[1,128,1280]{2,1,0:T(8,128)(2,1)}, bf16[1,128,1280]{2,1,0:T(8,128)(2,1)S(1)}, u32[]{:S(2)}) %copy-start.6) | copy-done | bytes 327704
  30.2 1.7 %copy-done.1 = bf16[1,1024,1280]{2,1,0:T(8,128)(2,1)S(1)} copy-done((bf16[1,1024,1280]{2,1,0:T(8,128)(2,1)S(1)}, bf16[1,1024,1280]{2,1,0:T(8,128)(2,1)}, u32[]{:S(2)}) %copy-start.1) | copy-done | bytes 2621464
  31.9 2.5 %shard_map.110 = (bf16[32,2,1408]{2,1,0:T(2,128)(2,1)S(1)}, bf16[16,1280]{1,0:T(8,128)(2,1)S(1)}, bf16[16,1280]{1,0:T(8,128)(2,1)S(1)}, bf16[16,1024]{1,0:T(8,128)(2,1)S(1)}, bf16[16,1024]{1,0:T(8,128)(2,1)S(1)}) custom-call(bf16[32,2,1408]{2,1,0:T(2,128)(2,1)S(1)} %all-to-all-done.got_ref, bf16[1,1280,1024]{2,1,0:T(8,128)(2,1)S(1)} %copy-done, ...), custom_call_target="tpu_custom_call" | custom-call | flops 1000000000 | bytes 5423104 | tf_op jit(solution)/shard_map/pallas_call | solution.py:258
  34.5 13.9 %all_to_all.10.refs_0_ = bf16[32,2,1408]{2,1,0:T(2,128)(2,1)S(1)} all-to-all(bf16[32,2,1408]{2,1,0:T(2,128)(2,1)S(1)} %get-tuple-element.34), channel_id=1, replica_groups=mesh['img'=16,'tok'=2] {'img','tok'}, dimensions={0} | all-to-all | bytes 360448 | tf_op jit(solution)/shard_map/all_to_all | solution.py:283
  48.4 1.0 %shard_map.111 = (f32[8,1408]{1,0:T(8,128)S(1)}, bf16[8,1280]{1,0:T(8,128)(2,1)S(1)}, bf16[16,128]{1,0:T(8,128)(2,1)S(1)}, bf16[16,1280]{1,0:T(8,128)(2,1)S(1)}, f32[1,128]{1,0:T(1,128)S(1)}) custom-call(bf16[32,2,1408]{2,1,0:T(2,128)(2,1)S(1)} %all_to_all.10.refs_0_, f32[8,128]{1,0:T(8,128)S(1)} %get-tuple-element.35.refs_1_.logit_ref, ...), custom_call_target="tpu_custom_call" | custom-call | flops 10000000 | bytes 1516064 | tf_op jit(solution)/shard_map/pallas_call | solution.py:258
  49.4 0.0 collective-permute-start.2
  49.5 1.2 %collective-permute-done.2 = f32[8,1408]{1,0:T(8,128)S(1)} collective-permute-done((f32[8,1408]{1,0:T(8,128)S(1)}, f32[8,1408]{1,0:T(8,128)S(1)}, u32[]{:S(2)}, u32[]{:S(2)}) %collective-permute-start.2) | collective-permute-done | bytes 45088 | tf_op jit(solution)/shard_map/ppermute | solution.py:287
  50.7 0.1 collective-permute-start.5
  50.8 1.2 %collective-permute-start.4 = (bf16[8,1408]{1,0:T(8,128)(2,1)S(1)}, bf16[8,1408]{1,0:T(8,128)(2,1)S(1)}, u32[]{:S(2)}, u32[]{:S(2)}) collective-permute-start(bf16[8,1408]{1,0:T(8,128)(2,1)S(1)} %add_convert_fusion.1), channel_id=1, source_target_pairs={{0,8},{2,10},{4,12},{6,14},{8,0},{10,2},{12,4},{14,6},{16,24},{18,... | collective-permute-start | bytes 67592 | tf_op jit(solution)/shard_map/ppermute | solution.py:287
  52.0 2.3 %collective-permute-start.3 = (bf16[8,1408]{1,0:T(8,128)(2,1)S(1)}, bf16[8,1408]{1,0:T(8,128)(2,1)S(1)}, u32[]{:S(2)}, u32[]{:S(2)}) collective-permute-start(bf16[8,1408]{1,0:T(8,128)(2,1)S(1)} %add_convert_fusion.1), channel_id=1, source_target_pairs={{0,4},{2,6},{4,0},{6,2},{8,12},{10,14},{12,8},{14,10},{16,20},{18,... | collective-permute-start | bytes 67592 | tf_op jit(solution)/shard_map/ppermute | solution.py:287
  54.2 1.8 %shard_map.112 = bf16[1,1280,1024]{2,1,0:T(8,128)(2,1)} custom-call(bf16[16,1280]{1,0:T(8,128)(2,1)S(1)} %get-tuple-element.40.left_ref, bf16[16,1024]{1,0:T(8,128)(2,1)S(1)} %get-tuple-element.41.right_ref), custom_call_target="tpu_custom_call" | custom-call | flops 1000000000 | bytes 73728 | tf_op jit(solution)/shard_map/pallas_call | solution.py:258
  56.1 0.7 %collective-permute-start.6 = (bf16[8,1408]{1,0:T(8,128)(2,1)S(1)}, bf16[8,1408]{1,0:T(8,128)(2,1)S(1)}, u32[]{:S(2)}, u32[]{:S(2)}) collective-permute-start(bf16[8,1408]{1,0:T(8,128)(2,1)S(1)} %add_convert_fusion.own_ref), channel_id=1, source_target_pairs={{0,16},{2,18},{4,20},{6,22},{8,24},{10,26},{12,28},{14,30},{16,0},... | collective-permute-start | bytes 67592 | tf_op jit(solution)/shard_map/ppermute | solution.py:287
  56.8 1.9 %shard_map.113 = bf16[1,1024,1280]{2,1,0:T(8,128)(2,1)} custom-call(bf16[16,1024]{1,0:T(8,128)(2,1)S(1)} %get-tuple-element.43.left_ref, bf16[16,1280]{1,0:T(8,128)(2,1)S(1)} %get-tuple-element.44.right_ref), custom_call_target="tpu_custom_call" | custom-call | flops 1000000000 | bytes 73728 | tf_op jit(solution)/shard_map/pallas_call | solution.py:258
  58.7 1.1 %shard_map.114 = (bf16[1,128,1280]{2,1,0:T(8,128)(2,1)}, bf16[1,128,1280]{2,1,0:T(8,128)(2,1)}) custom-call(bf16[1,128,1280]{2,1,0:T(8,128)(2,1)S(1)} %copy-done.2, f32[8,128]{1,0:T(8,128)S(1)} %get-tuple-element.35.refs_1_.logit_ref, bf16[8,1280]{1,0:T(8,128)(2,1)S(1)} %get-tuple-element.45.outs_ref, bf16[16,128]{1,0:T(8,128)(2,1)S(1)} %get-tuple-element.46.coef_ref, ...), custom_call_target="tpu_custom_call" | custom-call | flops 10000000 | bytes 397824 | tf_op jit(solution)/shard_map/pallas_call | solution.py:258
  59.9 1.3 %collective-permute-done.6.other_ref = bf16[8,1408]{1,0:T(8,128)(2,1)S(1)} collective-permute-done((bf16[8,1408]{1,0:T(8,128)(2,1)S(1)}, bf16[8,1408]{1,0:T(8,128)(2,1)S(1)}, u32[]{:S(2)}, u32[]{:S(2)}) %collective-permute-start.6) | collective-permute-done | bytes 22560 | tf_op jit(solution)/shard_map/ppermute | solution.py:287
  61.1 0.6 %shard_map.115 = (f32[8,1280]{1,0:T(8,128)}, f32[1,8]{1,0:T(1,128)}) custom-call(bf16[8,1408]{1,0:T(8,128)(2,1)S(1)} %add_convert_fusion.own_ref, bf16[8,1408]{1,0:T(8,128)(2,1)S(1)} %collective-permute-done.6.other_ref), custom_call_target="tpu_custom_call" | custom-call | flops 10000000 | bytes 45056 | tf_op jit(solution)/shard_map/pallas_call | solution.py:258
  (24 shorter events, 0.1 us)
Async XLA Ops:
  0.6 10.0 %copy-start.2 = (bf16[1,128,1280]{2,1,0:T(8,128)(2,1)S(1)}, bf16[1,128,1280]{2,1,0:T(8,128)(2,1)}, u32[]{:S(2)}) copy-start(bf16[1,128,1280]{2,1,0:T(8,128)(2,1)} %tok_ref.1) | copy-start | bytes 983044
  0.6 11.8 %copy-start.3 = (bf16[1,128,1280]{2,1,0:T(8,128)(2,1)S(1)}, bf16[1,128,1280]{2,1,0:T(8,128)(2,1)}, u32[]{:S(2)}) copy-start(bf16[1,128,1280]{2,1,0:T(8,128)(2,1)} %refs_7_.1) | copy-start | bytes 983044
  0.7 29.5 %copy-start = (bf16[1,1280,1024]{2,1,0:T(8,128)(2,1)S(1)}, bf16[1,1280,1024]{2,1,0:T(8,128)(2,1)}, u32[]{:S(2)}) copy-start(bf16[1,1280,1024]{2,1,0:T(8,128)(2,1)} %one_ref.1) | copy-start | bytes 7864324
  2.7 0.7 %copy-start.8 = (bf16[32,2,1408]{2,1,0:T(2,128)(2,1)}, bf16[32,2,1408]{2,1,0:T(2,128)(2,1)S(1)}, u32[]{:S(2)}) copy-start(bf16[32,2,1408]{2,1,0:T(2,128)(2,1)S(1)} %get-tuple-element.32) | copy-start | bytes 540676
  3.3 45.1 %copy-start.9 = (bf16[1280,8]{0,1:T(8,128)(2,1)S(1)}, bf16[1280,8]{0,1:T(8,128)(2,1)}, u32[]{:S(2)}) copy-start(bf16[1280,8]{0,1:T(8,128)(2,1)} %param.8) | copy-start | bytes 61444
  3.3 45.1 %copy-start.10 = (f32[8]{0:T(128)S(1)}, f32[8]{0:T(128)}, u32[]{:S(2)}) copy-start(f32[8]{0:T(128)} %param.9) | copy-start | bytes 100
  3.3 26.9 %all-to-all-start = ((bf16[32,2,1408]{2,1,0:T(2,128)(2,1)}), bf16[32,2,1408]{2,1,0:T(2,128)(2,1)S(1)}, u32[]{:S(2)}, u32[]{:S(2)}) async-start(bf16[32,2,1408]{2,1,0:T(2,128)(2,1)} %copy-done.8), calls=%async_computation | async-start | bytes 360448 | tf_op jit(solution)/shard_map/all_to_all | solution.py:283
  10.6 12.3 %collective-permute-start = (bf16[1,128,1280]{2,1,0:T(8,128)(2,1)S(1)}, bf16[1,128,1280]{2,1,0:T(8,128)(2,1)S(1)}, u32[]{:S(2)}, u32[]{:S(2)}) collective-permute-start(bf16[1,128,1280]{2,1,0:T(8,128)(2,1)S(1)} %copy-done.2), channel_id=1, source_target_pairs={{0,1},{1,0},{2,3},{3,2},{4,5},{5,4},{6,7},{7,6},{8,9},{9,8},{10,11... | collective-permute-start | bytes 983048 | tf_op jit(solution)/shard_map/ppermute | solution.py:287
  12.5 17.0 %collective-permute-start.1 = (bf16[1,128,1280]{2,1,0:T(8,128)(2,1)S(1)}, bf16[1,128,1280]{2,1,0:T(8,128)(2,1)S(1)}, u32[]{:S(2)}, u32[]{:S(2)}) collective-permute-start(bf16[1,128,1280]{2,1,0:T(8,128)(2,1)S(1)} %copy-done.3), channel_id=1, source_target_pairs={{0,1},{1,0},{2,3},{3,2},{4,5},{5,4},{6,7},{7,6},{8,9},{9,8},{10,11... | collective-permute-start | bytes 983048 | tf_op jit(solution)/shard_map/ppermute | solution.py:287
  22.9 0.7 %copy-start.4 = (bf16[1,128,1280]{2,1,0:T(8,128)(2,1)}, bf16[1,128,1280]{2,1,0:T(8,128)(2,1)S(1)}, u32[]{:S(2)}) copy-start(bf16[1,128,1280]{2,1,0:T(8,128)(2,1)S(1)} %collective-permute-done.refs_6_) | copy-start | bytes 983044
  29.5 0.7 %copy-start.6 = (bf16[1,128,1280]{2,1,0:T(8,128)(2,1)}, bf16[1,128,1280]{2,1,0:T(8,128)(2,1)S(1)}, u32[]{:S(2)}) copy-start(bf16[1,128,1280]{2,1,0:T(8,128)(2,1)S(1)} %collective-permute-done.1.refs_8_) | copy-start | bytes 983044
  30.2 1.7 %copy-start.1 = (bf16[1,1024,1280]{2,1,0:T(8,128)(2,1)S(1)}, bf16[1,1024,1280]{2,1,0:T(8,128)(2,1)}, u32[]{:S(2)}) copy-start(bf16[1,1024,1280]{2,1,0:T(8,128)(2,1)} %two_ref.1) | copy-start | bytes 7864324
  31.9 16.5 %copy-start.5 = (bf16[1,128,1280]{2,1,0:T(8,128)(2,1)S(1)}, bf16[1,128,1280]{2,1,0:T(8,128)(2,1)}, u32[]{:S(2)}) copy-start(bf16[1,128,1280]{2,1,0:T(8,128)(2,1)} %copy-done.4) | copy-start | bytes 983044
  31.9 16.5 %copy-start.7 = (bf16[1,128,1280]{2,1,0:T(8,128)(2,1)S(1)}, bf16[1,128,1280]{2,1,0:T(8,128)(2,1)}, u32[]{:S(2)}) copy-start(bf16[1,128,1280]{2,1,0:T(8,128)(2,1)} %copy-done.6) | copy-start | bytes 983044
  49.4 1.3 %collective-permute-start.2 = (f32[8,1408]{1,0:T(8,128)S(1)}, f32[8,1408]{1,0:T(8,128)S(1)}, u32[]{:S(2)}, u32[]{:S(2)}) collective-permute-start(f32[8,1408]{1,0:T(8,128)S(1)} %get-tuple-element.39), channel_id=1, source_target_pairs={{0,2},{2,0},{4,6},{6,4},{8,10},{10,8},{12,14},{14,12},{16,18},{18,... | collective-permute-start | bytes 135176 | tf_op jit(solution)/shard_map/ppermute | solution.py:287
  50.7 5.4 %collective-permute-start.5 = (bf16[8,1408]{1,0:T(8,128)(2,1)S(1)}, bf16[8,1408]{1,0:T(8,128)(2,1)S(1)}, u32[]{:S(2)}, u32[]{:S(2)}) collective-permute-start(bf16[8,1408]{1,0:T(8,128)(2,1)S(1)} %add_convert_fusion.1), channel_id=1, source_target_pairs={{0,12},{2,14},{4,8},{6,10},{8,4},{10,6},{12,0},{14,2},{16,28},{18,... | collective-permute-start | bytes 67592 | tf_op jit(solution)/shard_map/ppermute | solution.py:287
  50.8 5.3 %collective-permute-start.4 = (bf16[8,1408]{1,0:T(8,128)(2,1)S(1)}, bf16[8,1408]{1,0:T(8,128)(2,1)S(1)}, u32[]{:S(2)}, u32[]{:S(2)}) collective-permute-start(bf16[8,1408]{1,0:T(8,128)(2,1)S(1)} %add_convert_fusion.1), channel_id=1, source_target_pairs={{0,8},{2,10},{4,12},{6,14},{8,0},{10,2},{12,4},{14,6},{16,24},{18,... | collective-permute-start | bytes 67592 | tf_op jit(solution)/shard_map/ppermute | solution.py:287
  52.0 4.1 %collective-permute-start.3 = (bf16[8,1408]{1,0:T(8,128)(2,1)S(1)}, bf16[8,1408]{1,0:T(8,128)(2,1)S(1)}, u32[]{:S(2)}, u32[]{:S(2)}) collective-permute-start(bf16[8,1408]{1,0:T(8,128)(2,1)S(1)} %add_convert_fusion.1), channel_id=1, source_target_pairs={{0,4},{2,6},{4,0},{6,2},{8,12},{10,14},{12,8},{14,10},{16,20},{18,... | collective-permute-start | bytes 67592 | tf_op jit(solution)/shard_map/ppermute | solution.py:287
  56.1 5.0 %collective-permute-start.6 = (bf16[8,1408]{1,0:T(8,128)(2,1)S(1)}, bf16[8,1408]{1,0:T(8,128)(2,1)S(1)}, u32[]{:S(2)}, u32[]{:S(2)}) collective-permute-start(bf16[8,1408]{1,0:T(8,128)(2,1)S(1)} %add_convert_fusion.own_ref), channel_id=1, source_target_pairs={{0,16},{2,18},{4,20},{6,22},{8,24},{10,26},{12,28},{14,30},{16,0},... | collective-permute-start | bytes 67592 | tf_op jit(solution)/shard_map/ppermute | solution.py:287

commit v5 on v3

--- a/solution.py
+++ b/solution.py
@@ -229,11 +229,8 @@
     grads_ref[0] = (grads - column * tok_ref[0].astype(F32)).astype(BF)
 
 
-def last_kernel(own_ref, other_ref, *refs):
-    *more, router_ref, scale_ref = refs
-    sums = own_ref[...].astype(F32) + other_ref[...].astype(F32)
-    if more:
-        sums = sums + (more[0][...].astype(F32) + more[1][...].astype(F32))
+def last_kernel(mine_ref, other_ref, router_ref, scale_ref):
+    sums = mine_ref[...] + other_ref[...]
     experts, width = router_ref.shape
     router_ref[...] = sums[:, :width]
     eye = iota((experts, experts), 0) == iota((experts, experts), 1)
@@ -274,29 +271,38 @@
     return lax.all_to_all(block, BOTH, split_axis=0, concat_axis=0, tiled=True)
 
 
-def pair(term, mask, devices):
-    return lax.ppermute(term, BOTH, [(d, d ^ mask) for d in range(devices)])
+def pair(term, masks):
+    return lax.ppermute(term, BOTH, [(d, d ^ mask) for d, mask in enumerate(masks)])
 
 
 def sum_everywhere(term, devices, beside):
-    term = term + pair(term, 2, devices)
+    core = (lax.axis_index("img") & 1) == 0
+    bit = 2
     masks = [1] + [1 << place for place in range(2, log2(devices))]
-    rounds = [masks[place : place + 2] for place in range(0, len(masks), 2)]
     done = []
-    for group in rounds:
-        if group is not rounds[0]:
-            term = (terms[0].astype(F32) + terms[1].astype(F32)) + (
-                terms[2].astype(F32) + terms[3].astype(F32)
-            )
-        own = term.astype(BF)
-        terms = [own, pair(own, group[0], devices)]
-        if len(group) == 2:
-            terms += [pair(own, group[1], devices), pair(own, group[0] ^ group[1], devices)]
-        if beside:
-            terms[1], ready = lax.optimization_barrier((terms[1], beside[0]))
-            beside = beside[1:]
+
+    def together(value):
+        if len(done) < len(beside):
+            value, ready = lax.optimization_barrier((value, beside[len(done)]))
             done.append(ready)
-    return terms, done + list(beside)
+        return value
+
+    mine, other = term, pair(term, [bit] * devices)
+    for place in range(0, len(masks), 2):
+        group = masks[place : place + 2]
+        own = (mine + other).astype(BF)
+        if len(group) == 1:
+            mine, other = own.astype(F32), together(pair(own, group * devices)).astype(F32)
+            continue
+        near, far = group
+        first = pair(own, [near if d & bit else near ^ far for d in range(devices)])
+        second = pair(own, [far] * devices)
+        first = together(first)
+        mine = first.astype(F32) + jnp.where(core, own, second).astype(F32)
+        other = pair(mine, [bit] * devices)
+        if place + 2 >= len(masks):
+            other = together(other)
+    return mine, other, done + beside[len(done) :]
 
 
 def shards(images, halves, tokens, grad_out, router, slot_scale, w_in, w_out):
@@ -339,11 +345,11 @@
         [(tokens.shape, BF), (tokens.shape, BF)],
         tokens, logit, ys, coef, mix, signal,
     )
-    terms, (grad_w_in, (grad_w_out, combined, grad_tokens)) = sum_everywhere(
-        sums, devices, [grad_w_in, (grad_w_out, combined, grad_tokens)]
+    mine, other, (grad_w_in, grad_w_out, (combined, grad_tokens)) = sum_everywhere(
+        sums, devices, [grad_w_in, grad_w_out, (combined, grad_tokens)]
     )
     grad_router, grad_scale = call(
-        last_kernel, [((experts, width), F32), ((1, experts), F32)], *terms
+        last_kernel, [((experts, width), F32), ((1, experts), F32)], mine, other
     )
     return (combined, grad_tokens, grad_router.T, grad_scale[0], grad_w_in, grad_w_out)
 

time: 49.1 us -> 49.2 us (level)
  waiting for transfers between devices: 1.85 us -> 5.23 us
  starting transfers between devices: 8.03 us -> 4.79 us
    ppermute x7, waiting for transfers between devices: 1.85 us -> 5.23 us  [pair(): lax.ppermute(term, BOTH, [(d, d ^ mask) for d, mask in enumerate(masks)])]
    ppermute x7, starting transfers between devices: 8.03 us -> 4.79 us  [pair(): lax.ppermute(term, BOTH, [(d, d ^ mask) for d, mask in enumerate(masks)])]
  transfers between devices with their start and end apart: 7 -> 7, of which waited for: 3 -> 5; matrix products, arithmetic and copies ran while one was open for 0% -> 0% of each run, Pallas kernels for 10% -> 10%
where the time goes in v5:
time: 49.2 us; the launch traced here: 49 us
  blocking collectives  27.6 us (56%)
  Pallas kernels  10.6 us (22%)
  waiting for transfers between devices  5.23 us (11%)
  starting transfers between devices  4.79 us (10%)
  between operations  0.77 us (2%)
    all_to_all x2, blocking collectives, exchange(): return lax.all_to_all(block, BOTH, split_axis=0, concat_axis=0, tiled=True)  27.6 us
    pallas_call x7, Pallas kernels, call(): pl.pallas_call(kernel, out_shape=[jax.ShapeDtypeStruct(shape, dtype) for...  10.6 us
    ppermute x7, waiting for transfers between devices, pair(): lax.ppermute(term, BOTH, [(d, d ^ mask) for d, mask in enumerate(masks)])  5.23 us
    ppermute x7, starting transfers between devices, pair(): lax.ppermute(term, BOTH, [(d, d ^ mask) for d, mask in enumerate(masks)])  4.79 us
  transfers between devices with their start and end apart: 7, of which 5 were waited for; matrix products, arithmetic and copies ran while one was open for 0% of the time, Pallas kernels for 10%

profile of v5, /device:TPU:0, one launch (start us, length us, event | category | flops | bytes accessed | tf_op | source)
XLA Modules:
  0.0 49.0 jit_solution(4566725925498831073)
XLA Ops:
  0.7 2.0 %shard_map.109 = (bf16[32,2,1408]{2,1,0:T(2,128)(2,1)S(1)}, f32[8,128]{1,0:T(8,128)S(1)}, f32[1,128]{1,0:T(1,128)S(1)}) custom-call(bf16[1,128,1280]{2,1,0:T(8,128)(2,1)} %tok_ref.3, bf16[1,128,1280]{2,1,0:T(8,128)(2,1)} %grad_ref.1, bf16[8,1280]{1,0:T(8,128)(2,1)} %bitcast.4, f32[1,8]{1,0:T(1,128)} %bitcast.6), custom_call_target="tpu_custom_call" | custom-call | flops 4000000000 | bytes 675872 | tf_op jit(solution)/shard_map/pallas_call | solution.py:246
  2.6 16.5 %all_to_all.10.got_ref = bf16[32,2,1408]{2,1,0:T(2,128)(2,1)S(1)} all-to-all(bf16[32,2,1408]{2,1,0:T(2,128)(2,1)S(1)} %get-tuple-element.30), channel_id=1, replica_groups=mesh['img'=16,'tok'=2] {'img','tok'}, dimensions={0} | all-to-all | bytes 360448 | tf_op jit(solution)/shard_map/all_to_all | solution.py:271
  19.2 0.0 copy-start.4
  19.2 0.0 copy-start.5
  19.2 2.6 %shard_map.110 = (bf16[32,2,1408]{2,1,0:T(2,128)(2,1)S(1)}, bf16[16,1280]{1,0:T(8,128)(2,1)S(1)}, bf16[16,1280]{1,0:T(8,128)(2,1)S(1)}, bf16[16,1024]{1,0:T(8,128)(2,1)S(1)}, bf16[16,1024]{1,0:T(8,128)(2,1)S(1)}) custom-call(bf16[32,2,1408]{2,1,0:T(2,128)(2,1)S(1)} %all_to_all.10.got_ref, bf16[1,1280,1024]{2,1,0:T(8,128)(2,1)S(1)} %copy-done, ...), custom_call_target="tpu_custom_call" | custom-call | flops 1000000000 | bytes 5423104 | tf_op jit(solution)/shard_map/pallas_call | solution.py:246
  21.7 11.1 %all_to_all.11.back_ref = bf16[32,2,1408]{2,1,0:T(2,128)(2,1)S(1)} all-to-all(bf16[32,2,1408]{2,1,0:T(2,128)(2,1)S(1)} %get-tuple-element.31), channel_id=1, replica_groups=mesh['img'=16,'tok'=2] {'img','tok'}, dimensions={0} | all-to-all | bytes 360448 | tf_op jit(solution)/shard_map/all_to_all | solution.py:271
  32.9 0.5 %shard_map.111 = (f32[8,1408]{1,0:T(8,128)S(1)}, bf16[8,1280]{1,0:T(8,128)(2,1)S(1)}, bf16[16,128]{1,0:T(8,128)(2,1)S(1)}, bf16[16,1280]{1,0:T(8,128)(2,1)S(1)}, f32[1,128]{1,0:T(1,128)S(1)}) custom-call(bf16[32,2,1408]{2,1,0:T(2,128)(2,1)S(1)} %all_to_all.11.back_ref, bf16[1,128,1280]{2,1,0:T(8,128)(2,1)S(1)} %copy-done.2, ...), custom_call_target="tpu_custom_call" | custom-call | flops 10000000 | bytes 860704 | tf_op jit(solution)/shard_map/pallas_call | solution.py:246
  33.4 0.0 collective-permute-start
  33.5 1.2 %collective-permute-done = f32[8,1408]{1,0:T(8,128)S(1)} collective-permute-done((f32[8,1408]{1,0:T(8,128)S(1)}, f32[8,1408]{1,0:T(8,128)S(1)}, u32[]{:S(2)}, u32[]{:S(2)}) %collective-permute-start) | collective-permute-done | bytes 45088 | tf_op jit(solution)/shard_map/ppermute | solution.py:275
  34.7 0.1 collective-permute-start.2
  34.7 1.7 %collective-permute-start.1 = (bf16[8,1408]{1,0:T(8,128)(2,1)S(1)}, bf16[8,1408]{1,0:T(8,128)(2,1)S(1)}, u32[]{:S(2)}, u32[]{:S(2)}) collective-permute-start(bf16[8,1408]{1,0:T(8,128)(2,1)S(1)} %add_convert_fusion.1), channel_id=1, source_target_pairs={{0,5},{1,4},{2,3},{3,2},{4,1},{5,0},{6,7},{7,6},{8,13},{9,12},{10,... | collective-permute-start | bytes 67592 | tf_op jit(solution)/shard_map/ppermute | solution.py:275
  36.4 1.8 %shard_map.112 = bf16[1,1280,1024]{2,1,0:T(8,128)(2,1)} custom-call(bf16[16,1280]{1,0:T(8,128)(2,1)S(1)} %get-tuple-element.35.left_ref, bf16[16,1024]{1,0:T(8,128)(2,1)S(1)} %get-tuple-element.36.right_ref), custom_call_target="tpu_custom_call" | custom-call | flops 1000000000 | bytes 73728 | tf_op jit(solution)/shard_map/pallas_call | solution.py:246
  38.3 1.2 %collective-permute-done.1 = bf16[8,1408]{1,0:T(8,128)(2,1)S(1)} collective-permute-done((bf16[8,1408]{1,0:T(8,128)(2,1)S(1)}, bf16[8,1408]{1,0:T(8,128)(2,1)S(1)}, u32[]{:S(2)}, u32[]{:S(2)}) %collective-permute-start.1) | collective-permute-done | bytes 22560 | tf_op jit(solution)/shard_map/ppermute | solution.py:275
  39.5 0.0 collective-permute-done.2
  39.5 0.1 collective-permute-start.3
  39.6 1.2 %collective-permute-done.3 = f32[8,1408]{1,0:T(8,128)S(1)} collective-permute-done((f32[8,1408]{1,0:T(8,128)S(1)}, f32[8,1408]{1,0:T(8,128)S(1)}, u32[]{:S(2)}, u32[]{:S(2)}) %collective-permute-start.3) | collective-permute-done | bytes 45088 | tf_op jit(solution)/shard_map/ppermute | solution.py:275
  40.8 0.7 %collective-permute-start.5 = (bf16[8,1408]{1,0:T(8,128)(2,1)S(1)}, bf16[8,1408]{1,0:T(8,128)(2,1)S(1)}, u32[]{:S(2)}, u32[]{:S(2)}) collective-permute-start(bf16[8,1408]{1,0:T(8,128)(2,1)S(1)} %add_convert_fusion), channel_id=1, source_target_pairs={{0,16},{1,17},{2,18},{3,19},{4,20},{5,21},{6,22},{7,23},{8,24},{9,... | collective-permute-start | bytes 67592 | tf_op jit(solution)/shard_map/ppermute | solution.py:275
  41.5 2.2 %collective-permute-start.4 = (bf16[8,1408]{1,0:T(8,128)(2,1)S(1)}, bf16[8,1408]{1,0:T(8,128)(2,1)S(1)}, u32[]{:S(2)}, u32[]{:S(2)}) collective-permute-start(bf16[8,1408]{1,0:T(8,128)(2,1)S(1)} %add_convert_fusion), channel_id=1, source_target_pairs={{0,24},{1,25},{2,10},{3,11},{4,28},{5,29},{6,14},{7,15},{8,16},{9,... | collective-permute-start | bytes 67592 | tf_op jit(solution)/shard_map/ppermute | solution.py:275
  43.7 1.9 %shard_map.113 = bf16[1,1024,1280]{2,1,0:T(8,128)(2,1)} custom-call(bf16[16,1024]{1,0:T(8,128)(2,1)S(1)} %get-tuple-element.38.left_ref, bf16[16,1280]{1,0:T(8,128)(2,1)S(1)} %get-tuple-element.39.right_ref), custom_call_target="tpu_custom_call" | custom-call | flops 1000000000 | bytes 73728 | tf_op jit(solution)/shard_map/pallas_call | solution.py:246
  45.6 1.5 %collective-permute-done.4 = bf16[8,1408]{1,0:T(8,128)(2,1)S(1)} collective-permute-done((bf16[8,1408]{1,0:T(8,128)(2,1)S(1)}, bf16[8,1408]{1,0:T(8,128)(2,1)S(1)}, u32[]{:S(2)}, u32[]{:S(2)}) %collective-permute-start.4) | collective-permute-done | bytes 22560 | tf_op jit(solution)/shard_map/ppermute | solution.py:275
  47.1 0.1 collective-permute-start.6
  47.2 1.1 %shard_map.114 = (bf16[1,128,1280]{2,1,0:T(8,128)(2,1)}, bf16[1,128,1280]{2,1,0:T(8,128)(2,1)}) custom-call(bf16[1,128,1280]{2,1,0:T(8,128)(2,1)S(1)} %copy-done.2, f32[8,128]{1,0:T(8,128)S(1)} %get-tuple-element.32.logit_ref, bf16[8,1280]{1,0:T(8,128)(2,1)S(1)} %get-tuple-element.41.outs_ref, bf16[16,128]{1,0:T(8,128)(2,1)S(1)} %get-tuple-element.42.coef_ref, ...), custom_call_target="tpu_custom_call" | custom-call | flops 10000000 | bytes 397824 | tf_op jit(solution)/shard_map/pallas_call | solution.py:246
  48.3 0.1 collective-permute-done.6.other_ref
  48.4 0.6 %shard_map.115 = (f32[8,1280]{1,0:T(8,128)}, f32[1,8]{1,0:T(1,128)}) custom-call(f32[8,1408]{1,0:T(8,128)S(1)} %convert_add_fusion.mine_ref, f32[8,1408]{1,0:T(8,128)S(1)} %collective-permute-done.6.other_ref), custom_call_target="tpu_custom_call" | custom-call | flops 10000000 | bytes 90112 | tf_op jit(solution)/shard_map/pallas_call | solution.py:246
  (15 shorter events, 0.1 us)
Async XLA Ops:
  0.6 18.5 %copy-start = (bf16[1,1280,1024]{2,1,0:T(8,128)(2,1)S(1)}, bf16[1,1280,1024]{2,1,0:T(8,128)(2,1)}, u32[]{:S(2)}) copy-start(bf16[1,1280,1024]{2,1,0:T(8,128)(2,1)} %one_ref.1) | copy-start | bytes 7864324
  0.6 18.5 %copy-start.1 = (bf16[1,1024,1280]{2,1,0:T(8,128)(2,1)S(1)}, bf16[1,1024,1280]{2,1,0:T(8,128)(2,1)}, u32[]{:S(2)}) copy-start(bf16[1,1024,1280]{2,1,0:T(8,128)(2,1)} %two_ref.1) | copy-start | bytes 7864324
  19.2 13.7 %copy-start.2 = (bf16[1,128,1280]{2,1,0:T(8,128)(2,1)S(1)}, bf16[1,128,1280]{2,1,0:T(8,128)(2,1)}, u32[]{:S(2)}) copy-start(bf16[1,128,1280]{2,1,0:T(8,128)(2,1)} %tok_ref.3) | copy-start | bytes 983044
  19.2 13.7 %copy-start.3 = (bf16[1,128,1280]{2,1,0:T(8,128)(2,1)S(1)}, bf16[1,128,1280]{2,1,0:T(8,128)(2,1)}, u32[]{:S(2)}) copy-start(bf16[1,128,1280]{2,1,0:T(8,128)(2,1)} %grad_ref.1) | copy-start | bytes 983044
  19.2 13.7 %copy-start.4 = (bf16[1280,8]{0,1:T(8,128)(2,1)S(1)}, bf16[1280,8]{0,1:T(8,128)(2,1)}, u32[]{:S(2)}) copy-start(bf16[1280,8]{0,1:T(8,128)(2,1)} %param.8) | copy-start | bytes 61444
  19.2 13.7 %copy-start.5 = (f32[8]{0:T(128)S(1)}, f32[8]{0:T(128)}, u32[]{:S(2)}) copy-start(f32[8]{0:T(128)} %param.9) | copy-start | bytes 100
  33.4 1.2 %collective-permute-start = (f32[8,1408]{1,0:T(8,128)S(1)}, f32[8,1408]{1,0:T(8,128)S(1)}, u32[]{:S(2)}, u32[]{:S(2)}) collective-permute-start(f32[8,1408]{1,0:T(8,128)S(1)} %get-tuple-element.34), channel_id=1, source_target_pairs={{0,2},{1,3},{2,0},{3,1},{4,6},{5,7},{6,4},{7,5},{8,10},{9,11},{10,... | collective-permute-start | bytes 135176 | tf_op jit(solution)/shard_map/ppermute | solution.py:275
  34.7 4.8 %collective-permute-start.2 = (bf16[8,1408]{1,0:T(8,128)(2,1)S(1)}, bf16[8,1408]{1,0:T(8,128)(2,1)S(1)}, u32[]{:S(2)}, u32[]{:S(2)}) collective-permute-start(bf16[8,1408]{1,0:T(8,128)(2,1)S(1)} %add_convert_fusion.1), channel_id=1, source_target_pairs={{0,4},{1,5},{2,6},{3,7},{4,0},{5,1},{6,2},{7,3},{8,12},{9,13},{10,... | collective-permute-start | bytes 67592 | tf_op jit(solution)/shard_map/ppermute | solution.py:275
  34.7 4.8 %collective-permute-start.1 = (bf16[8,1408]{1,0:T(8,128)(2,1)S(1)}, bf16[8,1408]{1,0:T(8,128)(2,1)S(1)}, u32[]{:S(2)}, u32[]{:S(2)}) collective-permute-start(bf16[8,1408]{1,0:T(8,128)(2,1)S(1)} %add_convert_fusion.1), channel_id=1, source_target_pairs={{0,5},{1,4},{2,3},{3,2},{4,1},{5,0},{6,7},{7,6},{8,13},{9,12},{10,... | collective-permute-start | bytes 67592 | tf_op jit(solution)/shard_map/ppermute | solution.py:275
  39.5 1.3 %collective-permute-start.3 = (f32[8,1408]{1,0:T(8,128)S(1)}, f32[8,1408]{1,0:T(8,128)S(1)}, u32[]{:S(2)}, u32[]{:S(2)}) collective-permute-start(f32[8,1408]{1,0:T(8,128)S(1)} %convert_add_fusion.1), channel_id=1, source_target_pairs={{0,2},{1,3},{2,0},{3,1},{4,6},{5,7},{6,4},{7,5},{8,10},{9,11},{10,... | collective-permute-start | bytes 135176 | tf_op jit(solution)/shard_map/ppermute | solution.py:275
  40.8 6.3 %collective-permute-start.5 = (bf16[8,1408]{1,0:T(8,128)(2,1)S(1)}, bf16[8,1408]{1,0:T(8,128)(2,1)S(1)}, u32[]{:S(2)}, u32[]{:S(2)}) collective-permute-start(bf16[8,1408]{1,0:T(8,128)(2,1)S(1)} %add_convert_fusion), channel_id=1, source_target_pairs={{0,16},{1,17},{2,18},{3,19},{4,20},{5,21},{6,22},{7,23},{8,24},{9,... | collective-permute-start | bytes 67592 | tf_op jit(solution)/shard_map/ppermute | solution.py:275
  41.5 5.6 %collective-permute-start.4 = (bf16[8,1408]{1,0:T(8,128)(2,1)S(1)}, bf16[8,1408]{1,0:T(8,128)(2,1)S(1)}, u32[]{:S(2)}, u32[]{:S(2)}) collective-permute-start(bf16[8,1408]{1,0:T(8,128)(2,1)S(1)} %add_convert_fusion), channel_id=1, source_target_pairs={{0,24},{1,25},{2,10},{3,11},{4,28},{5,29},{6,14},{7,15},{8,16},{9,... | collective-permute-start | bytes 67592 | tf_op jit(solution)/shard_map/ppermute | solution.py:275
  47.1 1.3 %collective-permute-start.6 = (f32[8,1408]{1,0:T(8,128)S(1)}, f32[8,1408]{1,0:T(8,128)S(1)}, u32[]{:S(2)}, u32[]{:S(2)}) collective-permute-start(f32[8,1408]{1,0:T(8,128)S(1)} %convert_add_fusion.mine_ref), channel_id=1, source_target_pairs={{0,2},{1,3},{2,0},{3,1},{4,6},{5,7},{6,4},{7,5},{8,10},{9,11},{10,... | collective-permute-start | bytes 135176 | tf_op jit(solution)/shard_map/ppermute | solution.py:275

commit v6 on v3

--- a/solution.py
+++ b/solution.py
@@ -120,6 +120,10 @@
         return kind * images + place
 
     return key
+
+
+def lane_factor(shape):
+    return 1.0 + iota(shape, 1).astype(F32) * (1.0 / LANES)
 
 
 def front_kernel(
@@ -212,8 +216,7 @@
     outer = dot(grad_q, tok, ((1,), (0,)))
     total = jnp.sum(product, 1, keepdims=True)
     local = outer - inv_p * inv_p * total * router_f
-    lane = iota((experts, LANES), 1)
-    sums_ref[...] = jnp.concatenate([local, jnp.where(lane == 0, total / scale, 0.0)], 1)
+    sums_ref[...] = jnp.concatenate([local, total / scale * lane_factor((experts, LANES))], 1)
     outs_ref[...] = ys
     coef_ref[...] = jnp.concatenate([expo, grad_q.astype(F32)], 0).astype(BF)
     mix_ref[...] = jnp.concatenate([dxs.astype(F32) / den, router_f], 0).astype(BF)
@@ -237,7 +240,8 @@
     experts, width = router_ref.shape
     router_ref[...] = sums[:, :width]
     eye = iota((experts, experts), 0) == iota((experts, experts), 1)
-    scale_ref[...] = jnp.sum(jnp.where(eye, sums[:, width : width + 1], 0.0), 0, keepdims=True)
+    scale = jnp.sum(sums[:, width:] / lane_factor((experts, LANES)), 1, keepdims=True) * (1.0 / LANES)
+    scale_ref[...] = jnp.sum(jnp.where(eye, scale, 0.0), 0, keepdims=True)
 
 
 def call(kernel, outs, *args, stays=(), buffers=(), flops=10**7, room=24 * 2**20, home=pltpu.VMEM):
@@ -279,24 +283,27 @@
 
 
 def sum_everywhere(term, devices, beside):
-    term = term + pair(term, 2, devices)
+    done = []
+
+    def together(value):
+        if len(done) < len(beside):
+            value, ready = lax.optimization_barrier((value, beside[len(done)]))
+            done.append(ready)
+        return value
+
+    term = term + together(pair(term, 2, devices))
     masks = [1] + [1 << place for place in range(2, log2(devices))]
     rounds = [masks[place : place + 2] for place in range(0, len(masks), 2)]
-    done = []
     for group in rounds:
         if group is not rounds[0]:
             term = (terms[0].astype(F32) + terms[1].astype(F32)) + (
                 terms[2].astype(F32) + terms[3].astype(F32)
             )
         own = term.astype(BF)
-        terms = [own, pair(own, group[0], devices)]
-        if len(group) == 2:
-            terms += [pair(own, group[1], devices), pair(own, group[0] ^ group[1], devices)]
-        if beside:
-            terms[1], ready = lax.optimization_barrier((terms[1], beside[0]))
-            beside = beside[1:]
-            done.append(ready)
-    return terms, done + list(beside)
+        steps = [group[1], group[0], group[0] ^ group[1]] if len(group) == 2 else group
+        terms = [own] + [pair(own, mask, devices) for mask in steps]
+        terms[-1] = together(terms[-1])
+    return terms, done + beside[len(done) :]
 
 
 def shards(images, halves, tokens, grad_out, router, slot_scale, w_in, w_out):
@@ -339,8 +346,8 @@
         [(tokens.shape, BF), (tokens.shape, BF)],
         tokens, logit, ys, coef, mix, signal,
     )
-    terms, (grad_w_in, (grad_w_out, combined, grad_tokens)) = sum_everywhere(
-        sums, devices, [grad_w_in, (grad_w_out, combined, grad_tokens)]
+    terms, ((combined, grad_tokens), grad_w_in, grad_w_out) = sum_everywhere(
+        sums, devices, [(combined, grad_tokens), grad_w_in, grad_w_out]
     )
     grad_router, grad_scale = call(
         last_kernel, [((experts, width), F32), ((1, experts), F32)], *terms

time: 49.1 us -> 47.6 us (0.969)
  waiting for transfers between devices: 1.85 us -> 0.34 us
    ppermute x7, waiting for transfers between devices: 1.85 us -> 0.34 us  [pair(): return lax.ppermute(term, BOTH, [(d, d ^ mask) for d in range(devices)])]
where the time goes in v6:
time: 47.6 us; the launch traced here: 47.4 us
  blocking collectives  27.6 us (58%)
  Pallas kernels  10.6 us (22%)
  starting transfers between devices  8.03 us (17%)
  between operations  0.76 us (2%)
    all_to_all x2, blocking collectives, exchange(): return lax.all_to_all(block, BOTH, split_axis=0, concat_axis=0, tiled=True)  27.6 us
    pallas_call x7, Pallas kernels, call(): pl.pallas_call(kernel, out_shape=[jax.ShapeDtypeStruct(shape, dtype) for...  10.6 us
    ppermute x7, starting transfers between devices, pair(): return lax.ppermute(term, BOTH, [(d, d ^ mask) for d in range(devices)])  8.03 us
  transfers between devices with their start and end apart: 7, of which 3 were waited for; matrix products, arithmetic and copies ran while one was open for 0% of the time, Pallas kernels for 10%

profile of v6, /device:TPU:0, one launch (start us, length us, event | category | flops | bytes accessed | tf_op | source)
XLA Modules:
  0.0 47.4 jit_solution(12070247441398193055)
XLA Ops:
  0.7 2.0 %shard_map.109 = (bf16[32,2,1408]{2,1,0:T(2,128)(2,1)S(1)}, f32[8,128]{1,0:T(8,128)S(1)}, f32[1,128]{1,0:T(1,128)S(1)}) custom-call(bf16[1,128,1280]{2,1,0:T(8,128)(2,1)} %tok_ref.3, bf16[1,128,1280]{2,1,0:T(8,128)(2,1)} %grad_ref.1, bf16[8,1280]{1,0:T(8,128)(2,1)} %bitcast.4, f32[1,8]{1,0:T(1,128)} %bitcast.6), custom_call_target="tpu_custom_call" | custom-call | flops 4000000000 | bytes 675872 | tf_op jit(solution)/shard_map/pallas_call | solution.py:253
  2.6 16.5 %all_to_all.10.got_ref = bf16[32,2,1408]{2,1,0:T(2,128)(2,1)S(1)} all-to-all(bf16[32,2,1408]{2,1,0:T(2,128)(2,1)S(1)} %get-tuple-element.30), channel_id=1, replica_groups=mesh['img'=16,'tok'=2] {'img','tok'}, dimensions={0} | all-to-all | bytes 360448 | tf_op jit(solution)/shard_map/all_to_all | solution.py:278
  19.2 0.0 copy-start.4
  19.2 0.0 copy-start.5
  19.2 2.6 %shard_map.110 = (bf16[32,2,1408]{2,1,0:T(2,128)(2,1)S(1)}, bf16[16,1280]{1,0:T(8,128)(2,1)S(1)}, bf16[16,1280]{1,0:T(8,128)(2,1)S(1)}, bf16[16,1024]{1,0:T(8,128)(2,1)S(1)}, bf16[16,1024]{1,0:T(8,128)(2,1)S(1)}) custom-call(bf16[32,2,1408]{2,1,0:T(2,128)(2,1)S(1)} %all_to_all.10.got_ref, bf16[1,1280,1024]{2,1,0:T(8,128)(2,1)S(1)} %copy-done, ...), custom_call_target="tpu_custom_call" | custom-call | flops 1000000000 | bytes 5423104 | tf_op jit(solution)/shard_map/pallas_call | solution.py:253
  21.7 11.1 %all_to_all.11.back_ref = bf16[32,2,1408]{2,1,0:T(2,128)(2,1)S(1)} all-to-all(bf16[32,2,1408]{2,1,0:T(2,128)(2,1)S(1)} %get-tuple-element.31), channel_id=1, replica_groups=mesh['img'=16,'tok'=2] {'img','tok'}, dimensions={0} | all-to-all | bytes 360448 | tf_op jit(solution)/shard_map/all_to_all | solution.py:278
  32.9 0.5 %shard_map.111 = (f32[8,1408]{1,0:T(8,128)S(1)}, bf16[8,1280]{1,0:T(8,128)(2,1)S(1)}, bf16[16,128]{1,0:T(8,128)(2,1)S(1)}, bf16[16,1280]{1,0:T(8,128)(2,1)S(1)}, f32[1,128]{1,0:T(1,128)S(1)}) custom-call(bf16[32,2,1408]{2,1,0:T(2,128)(2,1)S(1)} %all_to_all.11.back_ref, bf16[1,128,1280]{2,1,0:T(8,128)(2,1)S(1)} %copy-done.2, ...), custom_call_target="tpu_custom_call" | custom-call | flops 10000000 | bytes 860704 | tf_op jit(solution)/shard_map/pallas_call | solution.py:253
  33.4 0.0 collective-permute-start
  33.4 1.1 %shard_map.112 = (bf16[1,128,1280]{2,1,0:T(8,128)(2,1)}, bf16[1,128,1280]{2,1,0:T(8,128)(2,1)}) custom-call(bf16[1,128,1280]{2,1,0:T(8,128)(2,1)S(1)} %copy-done.2, f32[8,128]{1,0:T(8,128)S(1)} %get-tuple-element.32.logit_ref, bf16[8,1280]{1,0:T(8,128)(2,1)S(1)} %get-tuple-element.35.outs_ref, bf16[16,128]{1,0:T(8,128)(2,1)S(1)} %get-tuple-element.36.coef_ref, ...), custom_call_target="tpu_custom_call" | custom-call | flops 10000000 | bytes 397824 | tf_op jit(solution)/shard_map/pallas_call | solution.py:253
  34.6 0.1 collective-permute-done
  34.7 0.6 %collective-permute-start.3 = (bf16[8,1408]{1,0:T(8,128)(2,1)S(1)}, bf16[8,1408]{1,0:T(8,128)(2,1)S(1)}, u32[]{:S(2)}, u32[]{:S(2)}) collective-permute-start(bf16[8,1408]{1,0:T(8,128)(2,1)S(1)} %add_convert_fusion.1), channel_id=1, source_target_pairs={{0,5},{1,4},{2,7},{3,6},{4,1},{5,0},{6,3},{7,2},{8,13},{9,12},{10,... | collective-permute-start | bytes 67592 | tf_op jit(solution)/shard_map/ppermute | solution.py:282
  35.2 1.2 %collective-permute-start.1 = (bf16[8,1408]{1,0:T(8,128)(2,1)S(1)}, bf16[8,1408]{1,0:T(8,128)(2,1)S(1)}, u32[]{:S(2)}, u32[]{:S(2)}) collective-permute-start(bf16[8,1408]{1,0:T(8,128)(2,1)S(1)} %add_convert_fusion.1), channel_id=1, source_target_pairs={{0,4},{1,5},{2,6},{3,7},{4,0},{5,1},{6,2},{7,3},{8,12},{9,13},{10,... | collective-permute-start | bytes 67592 | tf_op jit(solution)/shard_map/ppermute | solution.py:282
  36.4 1.8 %collective-permute-start.2 = (bf16[8,1408]{1,0:T(8,128)(2,1)S(1)}, bf16[8,1408]{1,0:T(8,128)(2,1)S(1)}, u32[]{:S(2)}, u32[]{:S(2)}) collective-permute-start(bf16[8,1408]{1,0:T(8,128)(2,1)S(1)} %add_convert_fusion.1), channel_id=1, source_target_pairs={{0,1},{1,0},{2,3},{3,2},{4,5},{5,4},{6,7},{7,6},{8,9},{9,8},{10,11... | collective-permute-start | bytes 67592 | tf_op jit(solution)/shard_map/ppermute | solution.py:282
  38.2 1.8 %shard_map.113 = bf16[1,1280,1024]{2,1,0:T(8,128)(2,1)} custom-call(bf16[16,1280]{1,0:T(8,128)(2,1)S(1)} %get-tuple-element.44.left_ref, bf16[16,1024]{1,0:T(8,128)(2,1)S(1)} %get-tuple-element.45.right_ref), custom_call_target="tpu_custom_call" | custom-call | flops 1000000000 | bytes 73728 | tf_op jit(solution)/shard_map/pallas_call | solution.py:253
  40.1 0.0 collective-permute-done.3
  40.1 0.0 collective-permute-done.1
  40.1 0.2 collective-permute-done.2
  40.3 1.7 %collective-permute-start.6 = (bf16[8,1408]{1,0:T(8,128)(2,1)S(1)}, bf16[8,1408]{1,0:T(8,128)(2,1)S(1)}, u32[]{:S(2)}, u32[]{:S(2)}) collective-permute-start(bf16[8,1408]{1,0:T(8,128)(2,1)S(1)} %add_convert_fusion.own_ref), channel_id=1, source_target_pairs={{0,24},{1,25},{2,26},{3,27},{4,28},{5,29},{6,30},{7,31},{8,16},{9,... | collective-permute-start | bytes 67592 | tf_op jit(solution)/shard_map/ppermute | solution.py:282
  42.0 0.6 %collective-permute-start.4 = (bf16[8,1408]{1,0:T(8,128)(2,1)S(1)}, bf16[8,1408]{1,0:T(8,128)(2,1)S(1)}, u32[]{:S(2)}, u32[]{:S(2)}) collective-permute-start(bf16[8,1408]{1,0:T(8,128)(2,1)S(1)} %add_convert_fusion.own_ref), channel_id=1, source_target_pairs={{0,16},{1,17},{2,18},{3,19},{4,20},{5,21},{6,22},{7,23},{8,24},{9,... | collective-permute-start | bytes 67592 | tf_op jit(solution)/shard_map/ppermute | solution.py:282
  42.5 2.2 %collective-permute-start.5 = (bf16[8,1408]{1,0:T(8,128)(2,1)S(1)}, bf16[8,1408]{1,0:T(8,128)(2,1)S(1)}, u32[]{:S(2)}, u32[]{:S(2)}) collective-permute-start(bf16[8,1408]{1,0:T(8,128)(2,1)S(1)} %add_convert_fusion.own_ref), channel_id=1, source_target_pairs={{0,8},{1,9},{2,10},{3,11},{4,12},{5,13},{6,14},{7,15},{8,0},{9,1},... | collective-permute-start | bytes 67592 | tf_op jit(solution)/shard_map/ppermute | solution.py:282
  44.7 1.9 %shard_map.114 = bf16[1,1024,1280]{2,1,0:T(8,128)(2,1)} custom-call(bf16[16,1024]{1,0:T(8,128)(2,1)S(1)} %get-tuple-element.47.left_ref, bf16[16,1280]{1,0:T(8,128)(2,1)S(1)} %get-tuple-element.48.right_ref), custom_call_target="tpu_custom_call" | custom-call | flops 1000000000 | bytes 73728 | tf_op jit(solution)/shard_map/pallas_call | solution.py:253
  46.6 0.0 collective-permute-done.6.refs_1_
  46.6 0.1 collective-permute-done.4.other_ref
  46.7 0.6 %shard_map.115 = (f32[8,1280]{1,0:T(8,128)}, f32[1,8]{1,0:T(1,128)}) custom-call(bf16[8,1408]{1,0:T(8,128)(2,1)S(1)} %add_convert_fusion.own_ref, bf16[8,1408]{1,0:T(8,128)(2,1)S(1)} %collective-permute-done.4.other_ref, bf16[8,1408]{1,0:T(8,128)(2,1)S(1)} %collective-permute-done.5.refs_0_, bf16[8,1408]{1,0:T(8,128)(2,1)S(1)} %collective-permute-done.6.refs_1_), custom_call_target="tpu_custom_call" | custom-call | flops 10000000 | bytes 90112 | tf_op jit(solution)/shard_map/pallas_call | solution.py:253
  (13 shorter events, 0.0 us)
Async XLA Ops:
  0.6 18.5 %copy-start = (bf16[1,1280,1024]{2,1,0:T(8,128)(2,1)S(1)}, bf16[1,1280,1024]{2,1,0:T(8,128)(2,1)}, u32[]{:S(2)}) copy-start(bf16[1,1280,1024]{2,1,0:T(8,128)(2,1)} %one_ref.1) | copy-start | bytes 7864324
  0.6 18.5 %copy-start.1 = (bf16[1,1024,1280]{2,1,0:T(8,128)(2,1)S(1)}, bf16[1,1024,1280]{2,1,0:T(8,128)(2,1)}, u32[]{:S(2)}) copy-start(bf16[1,1024,1280]{2,1,0:T(8,128)(2,1)} %two_ref.1) | copy-start | bytes 7864324
  19.2 13.7 %copy-start.2 = (bf16[1,128,1280]{2,1,0:T(8,128)(2,1)S(1)}, bf16[1,128,1280]{2,1,0:T(8,128)(2,1)}, u32[]{:S(2)}) copy-start(bf16[1,128,1280]{2,1,0:T(8,128)(2,1)} %tok_ref.3) | copy-start | bytes 983044
  19.2 13.7 %copy-start.3 = (bf16[1,128,1280]{2,1,0:T(8,128)(2,1)S(1)}, bf16[1,128,1280]{2,1,0:T(8,128)(2,1)}, u32[]{:S(2)}) copy-start(bf16[1,128,1280]{2,1,0:T(8,128)(2,1)} %grad_ref.1) | copy-start | bytes 983044
  19.2 13.7 %copy-start.4 = (bf16[1280,8]{0,1:T(8,128)(2,1)S(1)}, bf16[1280,8]{0,1:T(8,128)(2,1)}, u32[]{:S(2)}) copy-start(bf16[1280,8]{0,1:T(8,128)(2,1)} %param.8) | copy-start | bytes 61444
  19.2 13.7 %copy-start.5 = (f32[8]{0:T(128)S(1)}, f32[8]{0:T(128)}, u32[]{:S(2)}) copy-start(f32[8]{0:T(128)} %param.9) | copy-start | bytes 100
  33.4 1.2 %collective-permute-start = (f32[8,1408]{1,0:T(8,128)S(1)}, f32[8,1408]{1,0:T(8,128)S(1)}, u32[]{:S(2)}, u32[]{:S(2)}) collective-permute-start(f32[8,1408]{1,0:T(8,128)S(1)} %get-tuple-element.34), channel_id=1, source_target_pairs={{0,2},{1,3},{2,0},{3,1},{4,6},{5,7},{6,4},{7,5},{8,10},{9,11},{10,... | collective-permute-start | bytes 135176 | tf_op jit(solution)/shard_map/ppermute | solution.py:282
  34.7 5.4 %collective-permute-start.3 = (bf16[8,1408]{1,0:T(8,128)(2,1)S(1)}, bf16[8,1408]{1,0:T(8,128)(2,1)S(1)}, u32[]{:S(2)}, u32[]{:S(2)}) collective-permute-start(bf16[8,1408]{1,0:T(8,128)(2,1)S(1)} %add_convert_fusion.1), channel_id=1, source_target_pairs={{0,5},{1,4},{2,7},{3,6},{4,1},{5,0},{6,3},{7,2},{8,13},{9,12},{10,... | collective-permute-start | bytes 67592 | tf_op jit(solution)/shard_map/ppermute | solution.py:282
  35.2 4.8 %collective-permute-start.1 = (bf16[8,1408]{1,0:T(8,128)(2,1)S(1)}, bf16[8,1408]{1,0:T(8,128)(2,1)S(1)}, u32[]{:S(2)}, u32[]{:S(2)}) collective-permute-start(bf16[8,1408]{1,0:T(8,128)(2,1)S(1)} %add_convert_fusion.1), channel_id=1, source_target_pairs={{0,4},{1,5},{2,6},{3,7},{4,0},{5,1},{6,2},{7,3},{8,12},{9,13},{10,... | collective-permute-start | bytes 67592 | tf_op jit(solution)/shard_map/ppermute | solution.py:282
  36.4 3.8 %collective-permute-start.2 = (bf16[8,1408]{1,0:T(8,128)(2,1)S(1)}, bf16[8,1408]{1,0:T(8,128)(2,1)S(1)}, u32[]{:S(2)}, u32[]{:S(2)}) collective-permute-start(bf16[8,1408]{1,0:T(8,128)(2,1)S(1)} %add_convert_fusion.1), channel_id=1, source_target_pairs={{0,1},{1,0},{2,3},{3,2},{4,5},{5,4},{6,7},{7,6},{8,9},{9,8},{10,11... | collective-permute-start | bytes 67592 | tf_op jit(solution)/shard_map/ppermute | solution.py:282
  40.3 6.4 %collective-permute-start.6 = (bf16[8,1408]{1,0:T(8,128)(2,1)S(1)}, bf16[8,1408]{1,0:T(8,128)(2,1)S(1)}, u32[]{:S(2)}, u32[]{:S(2)}) collective-permute-start(bf16[8,1408]{1,0:T(8,128)(2,1)S(1)} %add_convert_fusion.own_ref), channel_id=1, source_target_pairs={{0,24},{1,25},{2,26},{3,27},{4,28},{5,29},{6,30},{7,31},{8,16},{9,... | collective-permute-start | bytes 67592 | tf_op jit(solution)/shard_map/ppermute | solution.py:282
  42.0 4.8 %collective-permute-start.4 = (bf16[8,1408]{1,0:T(8,128)(2,1)S(1)}, bf16[8,1408]{1,0:T(8,128)(2,1)S(1)}, u32[]{:S(2)}, u32[]{:S(2)}) collective-permute-start(bf16[8,1408]{1,0:T(8,128)(2,1)S(1)} %add_convert_fusion.own_ref), channel_id=1, source_target_pairs={{0,16},{1,17},{2,18},{3,19},{4,20},{5,21},{6,22},{7,23},{8,24},{9,... | collective-permute-start | bytes 67592 | tf_op jit(solution)/shard_map/ppermute | solution.py:282
  42.5 4.2 %collective-permute-start.5 = (bf16[8,1408]{1,0:T(8,128)(2,1)S(1)}, bf16[8,1408]{1,0:T(8,128)(2,1)S(1)}, u32[]{:S(2)}, u32[]{:S(2)}) collective-permute-start(bf16[8,1408]{1,0:T(8,128)(2,1)S(1)} %add_convert_fusion.own_ref), channel_id=1, source_target_pairs={{0,8},{1,9},{2,10},{3,11},{4,12},{5,13},{6,14},{7,15},{8,0},{9,1},... | collective-permute-start | bytes 67592 | tf_op jit(solution)/shard_map/ppermute | solution.py:282

commit v7 on v6

--- a/solution.py
+++ b/solution.py
@@ -15,6 +15,7 @@
 BOTH = ("img", "tok")
 LANES = 128
 FRONT = 4 * 10**9
+PIECES = 4
 
 
 def dot(left, right, dims):
@@ -130,10 +131,16 @@
     plan, tok_hbm, grad_hbm, router_hbm, scale_hbm, sent_ref, logit_ref, inv_ref,
     tok_ref, grad_ref, router_ref, scale_ref, sems,
 ):
+    size = tok_ref.shape[1] // PIECES
+    pieces = [pl.ds(place * size, size) for place in range(PIECES)]
     arrived = fetch(
-        [tok_hbm, router_hbm, scale_hbm, grad_hbm], [tok_ref, router_ref, scale_ref, grad_ref], sems
-    )
-    for copy in arrived[:3]:
+        [tok_hbm.at[:, piece] for piece in pieces] + [router_hbm, scale_hbm]
+        + [grad_hbm.at[:, piece] for piece in pieces],
+        [tok_ref.at[:, piece] for piece in pieces] + [router_ref, scale_ref]
+        + [grad_ref.at[:, piece] for piece in pieces],
+        sems,
+    )
+    for copy in arrived[: PIECES + 2]:
         copy.wait()
     tok = tok_ref[0]
     tok_f = tok.astype(F32)
@@ -143,7 +150,8 @@
     logit = raw * inv_x * (inv_p * scale)
     expo, comb = softmax(logit)
     numer = dot(expo.astype(BF), tok, ((1,), (0,)))
-    arrived[3].wait()
+    for copy in arrived[PIECES + 2 :]:
+        copy.wait()
     dys = dot(comb.astype(BF), grad_ref[0], ((1,), (0,)))
     rows = stack_rows(numer, dys, [jnp.sum(expo, 1, keepdims=True)])
     store_blocks(sent_ref, pick(expert_rows(plan, router_ref.shape[0]), 2 * sent_ref.shape[0], rows, itself))
@@ -160,20 +168,24 @@
     den = sums[:images, width : width + 1] + sums[images:, width : width + 1]
     rows = (sums[:images, :width] / den).astype(BF)
     grad_rows = sums[images:, :width].astype(BF)
-    act = dot(rows, one_ref[0], ((1,), (0,)))
-    grad_h = dot(grad_rows, two_ref[0], ((1,), (1,)))
-    phi = 0.5 * (1.0 + lax.erf(act * ROOT_HALF))
-    hidden = (act * phi).astype(BF)
-    dact = (grad_h * (phi + act * jnp.exp(-0.5 * act * act) * DENSITY)).astype(BF)
-    out_part = dot(hidden, two_ref[0], ((1,), (0,)))
-    in_part = dot(dact, one_ref[0], ((1,), (1,)))
-    corr = jnp.sum(dact.astype(F32) * act, 1, keepdims=True)
+    out_part = in_part = corr = 0.0
+    size = one_ref.shape[2] // 2
+    for start in (0, size):
+        part = slice(start, start + size)
+        act = dot(rows, one_ref[0, :, part], ((1,), (0,)))
+        grad_h = dot(grad_rows, two_ref[0, part], ((1,), (1,)))
+        phi = 0.5 * (1.0 + lax.erf(act * ROOT_HALF))
+        hidden = (act * phi).astype(BF)
+        dact = (grad_h * (phi + act * jnp.exp(-0.5 * act * act) * DENSITY)).astype(BF)
+        out_part += dot(hidden, two_ref[0, part], ((1,), (0,)))
+        in_part += dot(dact, one_ref[0, :, part], ((1,), (1,)))
+        corr += jnp.sum(dact.astype(F32) * act, 1, keepdims=True)
+        hidden_ref[:, part] = hidden
+        dact_ref[:, part] = dact
     packed = stack_rows(out_part, in_part, [den, corr])
     store_blocks(back_ref, pick(key, 2 * back_ref.shape[0], packed, itself))
     rows_ref[...] = rows
     grad_rows_ref[...] = grad_rows
-    hidden_ref[...] = hidden
-    dact_ref[...] = dact
 
 
 def outer_kernel(size, left_ref, right_ref, out_hbm, out_ref, sems):
@@ -216,7 +228,7 @@
     outer = dot(grad_q, tok, ((1,), (0,)))
     total = jnp.sum(product, 1, keepdims=True)
     local = outer - inv_p * inv_p * total * router_f
-    sums_ref[...] = jnp.concatenate([local, total / scale * lane_factor((experts, LANES))], 1)
+    sums_ref[...] = jnp.concatenate([local, total / scale * lane_factor((experts, LANES))], 1).astype(BF)
     outs_ref[...] = ys
     coef_ref[...] = jnp.concatenate([expo, grad_q.astype(F32)], 0).astype(BF)
     mix_ref[...] = jnp.concatenate([dxs.astype(F32) / den, router_f], 0).astype(BF)
@@ -291,7 +303,7 @@
             done.append(ready)
         return value
 
-    term = term + together(pair(term, 2, devices))
+    term = term.astype(F32) + together(pair(term, 2, devices)).astype(F32)
     masks = [1] + [1 << place for place in range(2, log2(devices))]
     rounds = [masks[place : place + 2] for place in range(0, len(masks), 2)]
     for group in rounds:
@@ -321,7 +333,7 @@
         [((devices, 2, long), BF), ((experts, tok_rows), F32), ((1, tok_rows), F32)],
         *inputs,
         stays=range(4),
-        buffers=[pltpu.VMEM(a.shape, a.dtype) for a in inputs] + [pltpu.SemaphoreType.DMA((4,))],
+        buffers=[pltpu.VMEM(a.shape, a.dtype) for a in inputs] + [pltpu.SemaphoreType.DMA((2 * PIECES + 2,))],
         flops=FRONT,
     )
     got = exchange(sent)
@@ -337,7 +349,7 @@
     grad_w_out = weight_grad(hidden, grad_rows)
     sums, ys, coef, mix, signal = call(
         functools.partial(middle_kernel, plan),
-        [((experts, long), F32), ((experts, width), BF), ((2 * experts, tok_rows), BF),
+        [((experts, long), BF), ((experts, width), BF), ((2 * experts, tok_rows), BF),
          ((2 * experts, width), BF), ((1, tok_rows), F32)],
         back, tokens, grad_out, logit, inv_x, router_t, scale_row,
     )

time: 47.6 us -> 47.7 us (level)
  transfers between devices with their start and end apart: 7 -> 7, of which waited for: 3 -> 2; matrix products, arithmetic and copies ran while one was open for 0% -> 0% of each run, Pallas kernels for 10% -> 10%
where the time goes in v7:
time: 47.7 us; the launch traced here: 47.5 us
  blocking collectives  27.6 us (58%)
  Pallas kernels  10.7 us (22%)
  starting transfers between devices  8.06 us (17%)
  between operations  0.76 us (2%)
    all_to_all x2, blocking collectives, exchange(): return lax.all_to_all(block, BOTH, split_axis=0, concat_axis=0, tiled=True)  27.6 us
    pallas_call x7, Pallas kernels, call(): pl.pallas_call(kernel, out_shape=[jax.ShapeDtypeStruct(shape, dtype) for...  10.7 us
    ppermute x7, starting transfers between devices, pair(): return lax.ppermute(term, BOTH, [(d, d ^ mask) for d in range(devices)])  8.06 us
  transfers between devices with their start and end apart: 7, of which 2 were waited for; matrix products, arithmetic and copies ran while one was open for 0% of the time, Pallas kernels for 10%

profile of v7, /device:TPU:0, one launch (start us, length us, event | category | flops | bytes accessed | tf_op | source)
XLA Modules:
  0.0 47.5 jit_solution(3179866061811919641)
XLA Ops:
  0.7 2.1 %shard_map.109 = (bf16[32,2,1408]{2,1,0:T(2,128)(2,1)S(1)}, f32[8,128]{1,0:T(8,128)S(1)}, f32[1,128]{1,0:T(1,128)S(1)}) custom-call(bf16[1,128,1280]{2,1,0:T(8,128)(2,1)} %tok_ref.3, bf16[1,128,1280]{2,1,0:T(8,128)(2,1)} %grad_ref.1, bf16[8,1280]{1,0:T(8,128)(2,1)} %bitcast.4, f32[1,8]{1,0:T(1,128)} %bitcast.6), custom_call_target="tpu_custom_call" | custom-call | flops 4000000000 | bytes 675872 | tf_op jit(solution)/shard_map/pallas_call | solution.py:265
  2.7 16.5 %all_to_all.10.got_ref = bf16[32,2,1408]{2,1,0:T(2,128)(2,1)S(1)} all-to-all(bf16[32,2,1408]{2,1,0:T(2,128)(2,1)S(1)} %get-tuple-element.30), channel_id=1, replica_groups=mesh['img'=16,'tok'=2] {'img','tok'}, dimensions={0} | all-to-all | bytes 360448 | tf_op jit(solution)/shard_map/all_to_all | solution.py:290
  19.3 0.0 copy-start.4
  19.3 0.0 copy-start.5
  19.3 2.6 %shard_map.110 = (bf16[32,2,1408]{2,1,0:T(2,128)(2,1)S(1)}, bf16[16,1280]{1,0:T(8,128)(2,1)S(1)}, bf16[16,1280]{1,0:T(8,128)(2,1)S(1)}, bf16[16,1024]{1,0:T(8,128)(2,1)S(1)}, bf16[16,1024]{1,0:T(8,128)(2,1)S(1)}) custom-call(bf16[32,2,1408]{2,1,0:T(2,128)(2,1)S(1)} %all_to_all.10.got_ref, bf16[1,1280,1024]{2,1,0:T(8,128)(2,1)S(1)} %copy-done, ...), custom_call_target="tpu_custom_call" | custom-call | flops 1000000000 | bytes 5423104 | tf_op jit(solution)/shard_map/pallas_call | solution.py:265
  21.9 11.1 %all_to_all.11.back_ref = bf16[32,2,1408]{2,1,0:T(2,128)(2,1)S(1)} all-to-all(bf16[32,2,1408]{2,1,0:T(2,128)(2,1)S(1)} %get-tuple-element.31), channel_id=1, replica_groups=mesh['img'=16,'tok'=2] {'img','tok'}, dimensions={0} | all-to-all | bytes 360448 | tf_op jit(solution)/shard_map/all_to_all | solution.py:290
  33.0 0.5 %shard_map.111 = (bf16[8,1408]{1,0:T(8,128)(2,1)S(1)}, bf16[8,1280]{1,0:T(8,128)(2,1)S(1)}, bf16[16,128]{1,0:T(8,128)(2,1)S(1)}, bf16[16,1280]{1,0:T(8,128)(2,1)S(1)}, f32[1,128]{1,0:T(1,128)S(1)}) custom-call(bf16[32,2,1408]{2,1,0:T(2,128)(2,1)S(1)} %all_to_all.11.back_ref, bf16[1,128,1280]{2,1,0:T(8,128)(2,1)S(1)} %copy-done.2, ...), custom_call_target="tpu_custom_call" | custom-call | flops 10000000 | bytes 860704 | tf_op jit(solution)/shard_map/pallas_call | solution.py:265
  33.5 0.1 collective-permute-start
  33.6 1.1 %shard_map.112 = (bf16[1,128,1280]{2,1,0:T(8,128)(2,1)}, bf16[1,128,1280]{2,1,0:T(8,128)(2,1)}) custom-call(bf16[1,128,1280]{2,1,0:T(8,128)(2,1)S(1)} %copy-done.2, f32[8,128]{1,0:T(8,128)S(1)} %get-tuple-element.32.logit_ref, bf16[8,1280]{1,0:T(8,128)(2,1)S(1)} %get-tuple-element.35.outs_ref, bf16[16,128]{1,0:T(8,128)(2,1)S(1)} %get-tuple-element.36.coef_ref, ...), custom_call_target="tpu_custom_call" | custom-call | flops 10000000 | bytes 397824 | tf_op jit(solution)/shard_map/pallas_call | solution.py:265
  34.7 0.0 collective-permute-done
  34.8 0.6 %collective-permute-start.3 = (bf16[8,1408]{1,0:T(8,128)(2,1)S(1)}, bf16[8,1408]{1,0:T(8,128)(2,1)S(1)}, u32[]{:S(2)}, u32[]{:S(2)}) collective-permute-start(bf16[8,1408]{1,0:T(8,128)(2,1)S(1)} %add_convert_fusion.1), channel_id=1, source_target_pairs={{0,5},{1,4},{2,7},{3,6},{4,1},{5,0},{6,3},{7,2},{8,13},{9,12},{10,... | collective-permute-start | bytes 67592 | tf_op jit(solution)/shard_map/ppermute | solution.py:294
  35.3 1.2 %collective-permute-start.1 = (bf16[8,1408]{1,0:T(8,128)(2,1)S(1)}, bf16[8,1408]{1,0:T(8,128)(2,1)S(1)}, u32[]{:S(2)}, u32[]{:S(2)}) collective-permute-start(bf16[8,1408]{1,0:T(8,128)(2,1)S(1)} %add_convert_fusion.1), channel_id=1, source_target_pairs={{0,4},{1,5},{2,6},{3,7},{4,0},{5,1},{6,2},{7,3},{8,12},{9,13},{10,... | collective-permute-start | bytes 67592 | tf_op jit(solution)/shard_map/ppermute | solution.py:294
  36.5 1.8 %collective-permute-start.2 = (bf16[8,1408]{1,0:T(8,128)(2,1)S(1)}, bf16[8,1408]{1,0:T(8,128)(2,1)S(1)}, u32[]{:S(2)}, u32[]{:S(2)}) collective-permute-start(bf16[8,1408]{1,0:T(8,128)(2,1)S(1)} %add_convert_fusion.1), channel_id=1, source_target_pairs={{0,1},{1,0},{2,3},{3,2},{4,5},{5,4},{6,7},{7,6},{8,9},{9,8},{10,11... | collective-permute-start | bytes 67592 | tf_op jit(solution)/shard_map/ppermute | solution.py:294
  38.3 1.8 %shard_map.113 = bf16[1,1280,1024]{2,1,0:T(8,128)(2,1)} custom-call(bf16[16,1280]{1,0:T(8,128)(2,1)S(1)} %get-tuple-element.44.left_ref, bf16[16,1024]{1,0:T(8,128)(2,1)S(1)} %get-tuple-element.45.right_ref), custom_call_target="tpu_custom_call" | custom-call | flops 1000000000 | bytes 73728 | tf_op jit(solution)/shard_map/pallas_call | solution.py:265
  40.2 0.0 collective-permute-done.1
  40.2 0.2 collective-permute-done.2
  40.4 1.7 %collective-permute-start.6 = (bf16[8,1408]{1,0:T(8,128)(2,1)S(1)}, bf16[8,1408]{1,0:T(8,128)(2,1)S(1)}, u32[]{:S(2)}, u32[]{:S(2)}) collective-permute-start(bf16[8,1408]{1,0:T(8,128)(2,1)S(1)} %add_convert_fusion.own_ref), channel_id=1, source_target_pairs={{0,24},{1,25},{2,26},{3,27},{4,28},{5,29},{6,30},{7,31},{8,16},{9,... | collective-permute-start | bytes 67592 | tf_op jit(solution)/shard_map/ppermute | solution.py:294
  42.1 0.6 %collective-permute-start.4 = (bf16[8,1408]{1,0:T(8,128)(2,1)S(1)}, bf16[8,1408]{1,0:T(8,128)(2,1)S(1)}, u32[]{:S(2)}, u32[]{:S(2)}) collective-permute-start(bf16[8,1408]{1,0:T(8,128)(2,1)S(1)} %add_convert_fusion.own_ref), channel_id=1, source_target_pairs={{0,16},{1,17},{2,18},{3,19},{4,20},{5,21},{6,22},{7,23},{8,24},{9,... | collective-permute-start | bytes 67592 | tf_op jit(solution)/shard_map/ppermute | solution.py:294
  42.6 2.2 %collective-permute-start.5 = (bf16[8,1408]{1,0:T(8,128)(2,1)S(1)}, bf16[8,1408]{1,0:T(8,128)(2,1)S(1)}, u32[]{:S(2)}, u32[]{:S(2)}) collective-permute-start(bf16[8,1408]{1,0:T(8,128)(2,1)S(1)} %add_convert_fusion.own_ref), channel_id=1, source_target_pairs={{0,8},{1,9},{2,10},{3,11},{4,12},{5,13},{6,14},{7,15},{8,0},{9,1},... | collective-permute-start | bytes 67592 | tf_op jit(solution)/shard_map/ppermute | solution.py:294
  44.8 1.9 %shard_map.114 = bf16[1,1024,1280]{2,1,0:T(8,128)(2,1)} custom-call(bf16[16,1024]{1,0:T(8,128)(2,1)S(1)} %get-tuple-element.47.left_ref, bf16[16,1280]{1,0:T(8,128)(2,1)S(1)} %get-tuple-element.48.right_ref), custom_call_target="tpu_custom_call" | custom-call | flops 1000000000 | bytes 73728 | tf_op jit(solution)/shard_map/pallas_call | solution.py:265
  46.7 0.0 collective-permute-done.6.refs_1_
  46.7 0.1 collective-permute-done.4.other_ref
  46.8 0.0 collective-permute-done.5.refs_0_
  46.8 0.6 %shard_map.115 = (f32[8,1280]{1,0:T(8,128)}, f32[1,8]{1,0:T(1,128)}) custom-call(bf16[8,1408]{1,0:T(8,128)(2,1)S(1)} %add_convert_fusion.own_ref, bf16[8,1408]{1,0:T(8,128)(2,1)S(1)} %collective-permute-done.4.other_ref, bf16[8,1408]{1,0:T(8,128)(2,1)S(1)} %collective-permute-done.5.refs_0_, bf16[8,1408]{1,0:T(8,128)(2,1)S(1)} %collective-permute-done.6.refs_1_), custom_call_target="tpu_custom_call" | custom-call | flops 10000000 | bytes 90112 | tf_op jit(solution)/shard_map/pallas_call | solution.py:265
  (13 shorter events, 0.0 us)
Async XLA Ops:
  0.6 18.6 %copy-start = (bf16[1,1280,1024]{2,1,0:T(8,128)(2,1)S(1)}, bf16[1,1280,1024]{2,1,0:T(8,128)(2,1)}, u32[]{:S(2)}) copy-start(bf16[1,1280,1024]{2,1,0:T(8,128)(2,1)} %one_ref.1) | copy-start | bytes 7864324
  0.6 18.6 %copy-start.1 = (bf16[1,1024,1280]{2,1,0:T(8,128)(2,1)S(1)}, bf16[1,1024,1280]{2,1,0:T(8,128)(2,1)}, u32[]{:S(2)}) copy-start(bf16[1,1024,1280]{2,1,0:T(8,128)(2,1)} %two_ref.1) | copy-start | bytes 7864324
  19.2 13.7 %copy-start.2 = (bf16[1,128,1280]{2,1,0:T(8,128)(2,1)S(1)}, bf16[1,128,1280]{2,1,0:T(8,128)(2,1)}, u32[]{:S(2)}) copy-start(bf16[1,128,1280]{2,1,0:T(8,128)(2,1)} %tok_ref.3) | copy-start | bytes 983044
  19.2 13.7 %copy-start.3 = (bf16[1,128,1280]{2,1,0:T(8,128)(2,1)S(1)}, bf16[1,128,1280]{2,1,0:T(8,128)(2,1)}, u32[]{:S(2)}) copy-start(bf16[1,128,1280]{2,1,0:T(8,128)(2,1)} %grad_ref.1) | copy-start | bytes 983044
  19.3 13.7 %copy-start.4 = (bf16[1280,8]{0,1:T(8,128)(2,1)S(1)}, bf16[1280,8]{0,1:T(8,128)(2,1)}, u32[]{:S(2)}) copy-start(bf16[1280,8]{0,1:T(8,128)(2,1)} %param.8) | copy-start | bytes 61444
  19.3 13.7 %copy-start.5 = (f32[8]{0:T(128)S(1)}, f32[8]{0:T(128)}, u32[]{:S(2)}) copy-start(f32[8]{0:T(128)} %param.9) | copy-start | bytes 100
  33.5 1.2 %collective-permute-start = (bf16[8,1408]{1,0:T(8,128)(2,1)S(1)}, bf16[8,1408]{1,0:T(8,128)(2,1)S(1)}, u32[]{:S(2)}, u32[]{:S(2)}) collective-permute-start(bf16[8,1408]{1,0:T(8,128)(2,1)S(1)} %get-tuple-element.34), channel_id=1, source_target_pairs={{0,2},{1,3},{2,0},{3,1},{4,6},{5,7},{6,4},{7,5},{8,10},{9,11},{10,... | collective-permute-start | bytes 67592 | tf_op jit(solution)/shard_map/ppermute | solution.py:294
  34.8 5.4 %collective-permute-start.3 = (bf16[8,1408]{1,0:T(8,128)(2,1)S(1)}, bf16[8,1408]{1,0:T(8,128)(2,1)S(1)}, u32[]{:S(2)}, u32[]{:S(2)}) collective-permute-start(bf16[8,1408]{1,0:T(8,128)(2,1)S(1)} %add_convert_fusion.1), channel_id=1, source_target_pairs={{0,5},{1,4},{2,7},{3,6},{4,1},{5,0},{6,3},{7,2},{8,13},{9,12},{10,... | collective-permute-start | bytes 67592 | tf_op jit(solution)/shard_map/ppermute | solution.py:294
  35.3 4.8 %collective-permute-start.1 = (bf16[8,1408]{1,0:T(8,128)(2,1)S(1)}, bf16[8,1408]{1,0:T(8,128)(2,1)S(1)}, u32[]{:S(2)}, u32[]{:S(2)}) collective-permute-start(bf16[8,1408]{1,0:T(8,128)(2,1)S(1)} %add_convert_fusion.1), channel_id=1, source_target_pairs={{0,4},{1,5},{2,6},{3,7},{4,0},{5,1},{6,2},{7,3},{8,12},{9,13},{10,... | collective-permute-start | bytes 67592 | tf_op jit(solution)/shard_map/ppermute | solution.py:294
  36.5 3.8 %collective-permute-start.2 = (bf16[8,1408]{1,0:T(8,128)(2,1)S(1)}, bf16[8,1408]{1,0:T(8,128)(2,1)S(1)}, u32[]{:S(2)}, u32[]{:S(2)}) collective-permute-start(bf16[8,1408]{1,0:T(8,128)(2,1)S(1)} %add_convert_fusion.1), channel_id=1, source_target_pairs={{0,1},{1,0},{2,3},{3,2},{4,5},{5,4},{6,7},{7,6},{8,9},{9,8},{10,11... | collective-permute-start | bytes 67592 | tf_op jit(solution)/shard_map/ppermute | solution.py:294
  40.4 6.4 %collective-permute-start.6 = (bf16[8,1408]{1,0:T(8,128)(2,1)S(1)}, bf16[8,1408]{1,0:T(8,128)(2,1)S(1)}, u32[]{:S(2)}, u32[]{:S(2)}) collective-permute-start(bf16[8,1408]{1,0:T(8,128)(2,1)S(1)} %add_convert_fusion.own_ref), channel_id=1, source_target_pairs={{0,24},{1,25},{2,26},{3,27},{4,28},{5,29},{6,30},{7,31},{8,16},{9,... | collective-permute-start | bytes 67592 | tf_op jit(solution)/shard_map/ppermute | solution.py:294
  42.1 4.8 %collective-permute-start.4 = (bf16[8,1408]{1,0:T(8,128)(2,1)S(1)}, bf16[8,1408]{1,0:T(8,128)(2,1)S(1)}, u32[]{:S(2)}, u32[]{:S(2)}) collective-permute-start(bf16[8,1408]{1,0:T(8,128)(2,1)S(1)} %add_convert_fusion.own_ref), channel_id=1, source_target_pairs={{0,16},{1,17},{2,18},{3,19},{4,20},{5,21},{6,22},{7,23},{8,24},{9,... | collective-permute-start | bytes 67592 | tf_op jit(solution)/shard_map/ppermute | solution.py:294
  42.6 4.2 %collective-permute-start.5 = (bf16[8,1408]{1,0:T(8,128)(2,1)S(1)}, bf16[8,1408]{1,0:T(8,128)(2,1)S(1)}, u32[]{:S(2)}, u32[]{:S(2)}) collective-permute-start(bf16[8,1408]{1,0:T(8,128)(2,1)S(1)} %add_convert_fusion.own_ref), channel_id=1, source_target_pairs={{0,8},{1,9},{2,10},{3,11},{4,12},{5,13},{6,14},{7,15},{8,0},{9,1},... | collective-permute-start | bytes 67592 | tf_op jit(solution)/shard_map/ppermute | solution.py:294

commit v8 on v6

--- a/solution.py
+++ b/solution.py
@@ -160,13 +160,17 @@
     den = sums[:images, width : width + 1] + sums[images:, width : width + 1]
     rows = (sums[:images, :width] / den).astype(BF)
     grad_rows = sums[images:, :width].astype(BF)
-    act = dot(rows, one_ref[0], ((1,), (0,)))
+    act = jnp.concatenate(
+        [dot(rows, one_ref[0, :, n : n + 256], ((1,), (0,))) for n in range(0, one_ref.shape[2], 256)], 1
+    )
     grad_h = dot(grad_rows, two_ref[0], ((1,), (1,)))
     phi = 0.5 * (1.0 + lax.erf(act * ROOT_HALF))
     hidden = (act * phi).astype(BF)
     dact = (grad_h * (phi + act * jnp.exp(-0.5 * act * act) * DENSITY)).astype(BF)
     out_part = dot(hidden, two_ref[0], ((1,), (0,)))
-    in_part = dot(dact, one_ref[0], ((1,), (1,)))
+    in_part = jnp.concatenate(
+        [dot(dact, one_ref[0, n : n + 256], ((1,), (1,))) for n in range(0, width, 256)], 1
+    )
     corr = jnp.sum(dact.astype(F32) * act, 1, keepdims=True)
     packed = stack_rows(out_part, in_part, [den, corr])
     store_blocks(back_ref, pick(key, 2 * back_ref.shape[0], packed, itself))

time: 47.6 us -> 47.6 us (level)
  no operation moved by 1% of the time
where the time goes in v8:
time: 47.6 us; the launch traced here: 47.4 us
  blocking collectives  27.6 us (58%)
  Pallas kernels  10.6 us (22%)
  starting transfers between devices  8.03 us (17%)
  between operations  0.76 us (2%)
    all_to_all x2, blocking collectives, exchange(): return lax.all_to_all(block, BOTH, split_axis=0, concat_axis=0, tiled=True)  27.6 us
    pallas_call x7, Pallas kernels, call(): pl.pallas_call(kernel, out_shape=[jax.ShapeDtypeStruct(shape, dtype) for...  10.6 us
    ppermute x7, starting transfers between devices, pair(): return lax.ppermute(term, BOTH, [(d, d ^ mask) for d in range(devices)])  8.03 us
  transfers between devices with their start and end apart: 7, of which 3 were waited for; matrix products, arithmetic and copies ran while one was open for 0% of the time, Pallas kernels for 10%

profile of v8, /device:TPU:0, one launch (start us, length us, event | category | flops | bytes accessed | tf_op | source)
XLA Modules:
  0.0 47.4 jit_solution(8221414789581160727)
XLA Ops:
  0.7 2.0 %shard_map.109 = (bf16[32,2,1408]{2,1,0:T(2,128)(2,1)S(1)}, f32[8,128]{1,0:T(8,128)S(1)}, f32[1,128]{1,0:T(1,128)S(1)}) custom-call(bf16[1,128,1280]{2,1,0:T(8,128)(2,1)} %tok_ref.3, bf16[1,128,1280]{2,1,0:T(8,128)(2,1)} %grad_ref.1, bf16[8,1280]{1,0:T(8,128)(2,1)} %bitcast.4, f32[1,8]{1,0:T(1,128)} %bitcast.6), custom_call_target="tpu_custom_call" | custom-call | flops 4000000000 | bytes 675872 | tf_op jit(solution)/shard_map/pallas_call | solution.py:257
  2.6 16.5 %all_to_all.10.got_ref = bf16[32,2,1408]{2,1,0:T(2,128)(2,1)S(1)} all-to-all(bf16[32,2,1408]{2,1,0:T(2,128)(2,1)S(1)} %get-tuple-element.30), channel_id=1, replica_groups=mesh['img'=16,'tok'=2] {'img','tok'}, dimensions={0} | all-to-all | bytes 360448 | tf_op jit(solution)/shard_map/all_to_all | solution.py:282
  19.2 0.0 copy-start.4
  19.2 0.0 copy-start.5
  19.2 2.6 %shard_map.110 = (bf16[32,2,1408]{2,1,0:T(2,128)(2,1)S(1)}, bf16[16,1280]{1,0:T(8,128)(2,1)S(1)}, bf16[16,1280]{1,0:T(8,128)(2,1)S(1)}, bf16[16,1024]{1,0:T(8,128)(2,1)S(1)}, bf16[16,1024]{1,0:T(8,128)(2,1)S(1)}) custom-call(bf16[32,2,1408]{2,1,0:T(2,128)(2,1)S(1)} %all_to_all.10.got_ref, bf16[1,1280,1024]{2,1,0:T(8,128)(2,1)S(1)} %copy-done, ...), custom_call_target="tpu_custom_call" | custom-call | flops 1000000000 | bytes 5423104 | tf_op jit(solution)/shard_map/pallas_call | solution.py:257
  21.7 11.1 %all_to_all.11.back_ref = bf16[32,2,1408]{2,1,0:T(2,128)(2,1)S(1)} all-to-all(bf16[32,2,1408]{2,1,0:T(2,128)(2,1)S(1)} %get-tuple-element.31), channel_id=1, replica_groups=mesh['img'=16,'tok'=2] {'img','tok'}, dimensions={0} | all-to-all | bytes 360448 | tf_op jit(solution)/shard_map/all_to_all | solution.py:282
  32.9 0.5 %shard_map.111 = (f32[8,1408]{1,0:T(8,128)S(1)}, bf16[8,1280]{1,0:T(8,128)(2,1)S(1)}, bf16[16,128]{1,0:T(8,128)(2,1)S(1)}, bf16[16,1280]{1,0:T(8,128)(2,1)S(1)}, f32[1,128]{1,0:T(1,128)S(1)}) custom-call(bf16[32,2,1408]{2,1,0:T(2,128)(2,1)S(1)} %all_to_all.11.back_ref, bf16[1,128,1280]{2,1,0:T(8,128)(2,1)S(1)} %copy-done.2, ...), custom_call_target="tpu_custom_call" | custom-call | flops 10000000 | bytes 860704 | tf_op jit(solution)/shard_map/pallas_call | solution.py:257
  33.4 0.0 collective-permute-start
  33.4 1.1 %shard_map.112 = (bf16[1,128,1280]{2,1,0:T(8,128)(2,1)}, bf16[1,128,1280]{2,1,0:T(8,128)(2,1)}) custom-call(bf16[1,128,1280]{2,1,0:T(8,128)(2,1)S(1)} %copy-done.2, f32[8,128]{1,0:T(8,128)S(1)} %get-tuple-element.32.logit_ref, bf16[8,1280]{1,0:T(8,128)(2,1)S(1)} %get-tuple-element.35.outs_ref, bf16[16,128]{1,0:T(8,128)(2,1)S(1)} %get-tuple-element.36.coef_ref, ...), custom_call_target="tpu_custom_call" | custom-call | flops 10000000 | bytes 397824 | tf_op jit(solution)/shard_map/pallas_call | solution.py:257
  34.6 0.1 collective-permute-done
  34.7 0.6 %collective-permute-start.3 = (bf16[8,1408]{1,0:T(8,128)(2,1)S(1)}, bf16[8,1408]{1,0:T(8,128)(2,1)S(1)}, u32[]{:S(2)}, u32[]{:S(2)}) collective-permute-start(bf16[8,1408]{1,0:T(8,128)(2,1)S(1)} %add_convert_fusion.1), channel_id=1, source_target_pairs={{0,5},{1,4},{2,7},{3,6},{4,1},{5,0},{6,3},{7,2},{8,13},{9,12},{10,... | collective-permute-start | bytes 67592 | tf_op jit(solution)/shard_map/ppermute | solution.py:286
  35.2 1.2 %collective-permute-start.1 = (bf16[8,1408]{1,0:T(8,128)(2,1)S(1)}, bf16[8,1408]{1,0:T(8,128)(2,1)S(1)}, u32[]{:S(2)}, u32[]{:S(2)}) collective-permute-start(bf16[8,1408]{1,0:T(8,128)(2,1)S(1)} %add_convert_fusion.1), channel_id=1, source_target_pairs={{0,4},{1,5},{2,6},{3,7},{4,0},{5,1},{6,2},{7,3},{8,12},{9,13},{10,... | collective-permute-start | bytes 67592 | tf_op jit(solution)/shard_map/ppermute | solution.py:286
  36.4 1.8 %collective-permute-start.2 = (bf16[8,1408]{1,0:T(8,128)(2,1)S(1)}, bf16[8,1408]{1,0:T(8,128)(2,1)S(1)}, u32[]{:S(2)}, u32[]{:S(2)}) collective-permute-start(bf16[8,1408]{1,0:T(8,128)(2,1)S(1)} %add_convert_fusion.1), channel_id=1, source_target_pairs={{0,1},{1,0},{2,3},{3,2},{4,5},{5,4},{6,7},{7,6},{8,9},{9,8},{10,11... | collective-permute-start | bytes 67592 | tf_op jit(solution)/shard_map/ppermute | solution.py:286
  38.2 1.8 %shard_map.113 = bf16[1,1280,1024]{2,1,0:T(8,128)(2,1)} custom-call(bf16[16,1280]{1,0:T(8,128)(2,1)S(1)} %get-tuple-element.44.left_ref, bf16[16,1024]{1,0:T(8,128)(2,1)S(1)} %get-tuple-element.45.right_ref), custom_call_target="tpu_custom_call" | custom-call | flops 1000000000 | bytes 73728 | tf_op jit(solution)/shard_map/pallas_call | solution.py:257
  40.1 0.0 collective-permute-done.1
  40.1 0.2 collective-permute-done.2
  40.3 1.7 %collective-permute-start.6 = (bf16[8,1408]{1,0:T(8,128)(2,1)S(1)}, bf16[8,1408]{1,0:T(8,128)(2,1)S(1)}, u32[]{:S(2)}, u32[]{:S(2)}) collective-permute-start(bf16[8,1408]{1,0:T(8,128)(2,1)S(1)} %add_convert_fusion.own_ref), channel_id=1, source_target_pairs={{0,24},{1,25},{2,26},{3,27},{4,28},{5,29},{6,30},{7,31},{8,16},{9,... | collective-permute-start | bytes 67592 | tf_op jit(solution)/shard_map/ppermute | solution.py:286
  42.0 0.6 %collective-permute-start.4 = (bf16[8,1408]{1,0:T(8,128)(2,1)S(1)}, bf16[8,1408]{1,0:T(8,128)(2,1)S(1)}, u32[]{:S(2)}, u32[]{:S(2)}) collective-permute-start(bf16[8,1408]{1,0:T(8,128)(2,1)S(1)} %add_convert_fusion.own_ref), channel_id=1, source_target_pairs={{0,16},{1,17},{2,18},{3,19},{4,20},{5,21},{6,22},{7,23},{8,24},{9,... | collective-permute-start | bytes 67592 | tf_op jit(solution)/shard_map/ppermute | solution.py:286
  42.5 2.2 %collective-permute-start.5 = (bf16[8,1408]{1,0:T(8,128)(2,1)S(1)}, bf16[8,1408]{1,0:T(8,128)(2,1)S(1)}, u32[]{:S(2)}, u32[]{:S(2)}) collective-permute-start(bf16[8,1408]{1,0:T(8,128)(2,1)S(1)} %add_convert_fusion.own_ref), channel_id=1, source_target_pairs={{0,8},{1,9},{2,10},{3,11},{4,12},{5,13},{6,14},{7,15},{8,0},{9,1},... | collective-permute-start | bytes 67592 | tf_op jit(solution)/shard_map/ppermute | solution.py:286
  44.7 1.9 %shard_map.114 = bf16[1,1024,1280]{2,1,0:T(8,128)(2,1)} custom-call(bf16[16,1024]{1,0:T(8,128)(2,1)S(1)} %get-tuple-element.47.left_ref, bf16[16,1280]{1,0:T(8,128)(2,1)S(1)} %get-tuple-element.48.right_ref), custom_call_target="tpu_custom_call" | custom-call | flops 1000000000 | bytes 73728 | tf_op jit(solution)/shard_map/pallas_call | solution.py:257
  46.6 0.0 collective-permute-done.6.refs_1_
  46.6 0.1 collective-permute-done.4.other_ref
  46.7 0.0 collective-permute-done.5.refs_0_
  46.7 0.6 %shard_map.115 = (f32[8,1280]{1,0:T(8,128)}, f32[1,8]{1,0:T(1,128)}) custom-call(bf16[8,1408]{1,0:T(8,128)(2,1)S(1)} %add_convert_fusion.own_ref, bf16[8,1408]{1,0:T(8,128)(2,1)S(1)} %collective-permute-done.4.other_ref, bf16[8,1408]{1,0:T(8,128)(2,1)S(1)} %collective-permute-done.5.refs_0_, bf16[8,1408]{1,0:T(8,128)(2,1)S(1)} %collective-permute-done.6.refs_1_), custom_call_target="tpu_custom_call" | custom-call | flops 10000000 | bytes 90112 | tf_op jit(solution)/shard_map/pallas_call | solution.py:257
  (13 shorter events, 0.0 us)
Async XLA Ops:
  0.6 18.5 %copy-start = (bf16[1,1280,1024]{2,1,0:T(8,128)(2,1)S(1)}, bf16[1,1280,1024]{2,1,0:T(8,128)(2,1)}, u32[]{:S(2)}) copy-start(bf16[1,1280,1024]{2,1,0:T(8,128)(2,1)} %one_ref.1) | copy-start | bytes 7864324
  0.6 18.5 %copy-start.1 = (bf16[1,1024,1280]{2,1,0:T(8,128)(2,1)S(1)}, bf16[1,1024,1280]{2,1,0:T(8,128)(2,1)}, u32[]{:S(2)}) copy-start(bf16[1,1024,1280]{2,1,0:T(8,128)(2,1)} %two_ref.1) | copy-start | bytes 7864324
  19.2 13.7 %copy-start.2 = (bf16[1,128,1280]{2,1,0:T(8,128)(2,1)S(1)}, bf16[1,128,1280]{2,1,0:T(8,128)(2,1)}, u32[]{:S(2)}) copy-start(bf16[1,128,1280]{2,1,0:T(8,128)(2,1)} %tok_ref.3) | copy-start | bytes 983044
  19.2 13.7 %copy-start.3 = (bf16[1,128,1280]{2,1,0:T(8,128)(2,1)S(1)}, bf16[1,128,1280]{2,1,0:T(8,128)(2,1)}, u32[]{:S(2)}) copy-start(bf16[1,128,1280]{2,1,0:T(8,128)(2,1)} %grad_ref.1) | copy-start | bytes 983044
  19.2 13.7 %copy-start.4 = (bf16[1280,8]{0,1:T(8,128)(2,1)S(1)}, bf16[1280,8]{0,1:T(8,128)(2,1)}, u32[]{:S(2)}) copy-start(bf16[1280,8]{0,1:T(8,128)(2,1)} %param.8) | copy-start | bytes 61444
  19.2 13.7 %copy-start.5 = (f32[8]{0:T(128)S(1)}, f32[8]{0:T(128)}, u32[]{:S(2)}) copy-start(f32[8]{0:T(128)} %param.9) | copy-start | bytes 100
  33.4 1.2 %collective-permute-start = (f32[8,1408]{1,0:T(8,128)S(1)}, f32[8,1408]{1,0:T(8,128)S(1)}, u32[]{:S(2)}, u32[]{:S(2)}) collective-permute-start(f32[8,1408]{1,0:T(8,128)S(1)} %get-tuple-element.34), channel_id=1, source_target_pairs={{0,2},{1,3},{2,0},{3,1},{4,6},{5,7},{6,4},{7,5},{8,10},{9,11},{10,... | collective-permute-start | bytes 135176 | tf_op jit(solution)/shard_map/ppermute | solution.py:286
  34.7 5.4 %collective-permute-start.3 = (bf16[8,1408]{1,0:T(8,128)(2,1)S(1)}, bf16[8,1408]{1,0:T(8,128)(2,1)S(1)}, u32[]{:S(2)}, u32[]{:S(2)}) collective-permute-start(bf16[8,1408]{1,0:T(8,128)(2,1)S(1)} %add_convert_fusion.1), channel_id=1, source_target_pairs={{0,5},{1,4},{2,7},{3,6},{4,1},{5,0},{6,3},{7,2},{8,13},{9,12},{10,... | collective-permute-start | bytes 67592 | tf_op jit(solution)/shard_map/ppermute | solution.py:286
  35.2 4.8 %collective-permute-start.1 = (bf16[8,1408]{1,0:T(8,128)(2,1)S(1)}, bf16[8,1408]{1,0:T(8,128)(2,1)S(1)}, u32[]{:S(2)}, u32[]{:S(2)}) collective-permute-start(bf16[8,1408]{1,0:T(8,128)(2,1)S(1)} %add_convert_fusion.1), channel_id=1, source_target_pairs={{0,4},{1,5},{2,6},{3,7},{4,0},{5,1},{6,2},{7,3},{8,12},{9,13},{10,... | collective-permute-start | bytes 67592 | tf_op jit(solution)/shard_map/ppermute | solution.py:286
  36.4 3.8 %collective-permute-start.2 = (bf16[8,1408]{1,0:T(8,128)(2,1)S(1)}, bf16[8,1408]{1,0:T(8,128)(2,1)S(1)}, u32[]{:S(2)}, u32[]{:S(2)}) collective-permute-start(bf16[8,1408]{1,0:T(8,128)(2,1)S(1)} %add_convert_fusion.1), channel_id=1, source_target_pairs={{0,1},{1,0},{2,3},{3,2},{4,5},{5,4},{6,7},{7,6},{8,9},{9,8},{10,11... | collective-permute-start | bytes 67592 | tf_op jit(solution)/shard_map/ppermute | solution.py:286
  40.3 6.4 %collective-permute-start.6 = (bf16[8,1408]{1,0:T(8,128)(2,1)S(1)}, bf16[8,1408]{1,0:T(8,128)(2,1)S(1)}, u32[]{:S(2)}, u32[]{:S(2)}) collective-permute-start(bf16[8,1408]{1,0:T(8,128)(2,1)S(1)} %add_convert_fusion.own_ref), channel_id=1, source_target_pairs={{0,24},{1,25},{2,26},{3,27},{4,28},{5,29},{6,30},{7,31},{8,16},{9,... | collective-permute-start | bytes 67592 | tf_op jit(solution)/shard_map/ppermute | solution.py:286
  42.0 4.8 %collective-permute-start.4 = (bf16[8,1408]{1,0:T(8,128)(2,1)S(1)}, bf16[8,1408]{1,0:T(8,128)(2,1)S(1)}, u32[]{:S(2)}, u32[]{:S(2)}) collective-permute-start(bf16[8,1408]{1,0:T(8,128)(2,1)S(1)} %add_convert_fusion.own_ref), channel_id=1, source_target_pairs={{0,16},{1,17},{2,18},{3,19},{4,20},{5,21},{6,22},{7,23},{8,24},{9,... | collective-permute-start | bytes 67592 | tf_op jit(solution)/shard_map/ppermute | solution.py:286
  42.5 4.2 %collective-permute-start.5 = (bf16[8,1408]{1,0:T(8,128)(2,1)S(1)}, bf16[8,1408]{1,0:T(8,128)(2,1)S(1)}, u32[]{:S(2)}, u32[]{:S(2)}) collective-permute-start(bf16[8,1408]{1,0:T(8,128)(2,1)S(1)} %add_convert_fusion.own_ref), channel_id=1, source_target_pairs={{0,8},{1,9},{2,10},{3,11},{4,12},{5,13},{6,14},{7,15},{8,0},{9,1},... | collective-permute-start | bytes 67592 | tf_op jit(solution)/shard_map/ppermute | solution.py:286

commit v9 on v6

--- a/solution.py
+++ b/solution.py
@@ -112,6 +112,14 @@
         return kind * experts + place
 
     return key
+
+
+def half_first(key, inner, halves):
+    def moved(row):
+        half, place, kind = digits(row, (halves, inner, 2))
+        return key((place * halves + half) * 2 + kind)
+
+    return moved
 
 
 def image_rows(images, halves):
@@ -146,7 +154,9 @@
     arrived[3].wait()
     dys = dot(comb.astype(BF), grad_ref[0], ((1,), (0,)))
     rows = stack_rows(numer, dys, [jnp.sum(expo, 1, keepdims=True)])
-    store_blocks(sent_ref, pick(expert_rows(plan, router_ref.shape[0]), 2 * sent_ref.shape[0], rows, itself))
+    experts = router_ref.shape[0]
+    key = half_first(expert_rows(plan, experts), plan[0] * experts, plan[1])
+    store_blocks(sent_ref, pick(key, 2 * sent_ref.shape[0], rows, itself))
     logit_ref[...] = logit
     inv_ref[...] = inv_x
 
@@ -156,7 +166,7 @@
 ):
     width = one_ref.shape[1]
     key = image_rows(images, halves)
-    sums = pick(itself, 2 * images, load_blocks(got_ref), key)
+    sums = pick(itself, 2 * images, load_blocks(got_ref), half_first(key, images, halves))
     den = sums[:images, width : width + 1] + sums[images:, width : width + 1]
     rows = (sums[:images, :width] / den).astype(BF)
     grad_rows = sums[images:, :width].astype(BF)
@@ -274,8 +284,8 @@
     return out
 
 
-def exchange(block):
-    return lax.all_to_all(block, BOTH, split_axis=0, concat_axis=0, tiled=True)
+def exchange(block, axes):
+    return lax.all_to_all(block, axes, split_axis=0, concat_axis=0, tiled=True)
 
 
 def pair(term, mask, devices):
@@ -324,7 +334,7 @@
         buffers=[pltpu.VMEM(a.shape, a.dtype) for a in inputs] + [pltpu.SemaphoreType.DMA((4,))],
         flops=FRONT,
     )
-    got = exchange(sent)
+    got = exchange(sent, ("tok", "img"))
     back, rows, grad_rows, hidden, dact = call(
         functools.partial(expert_kernel, images, halves),
         [((devices, 2, long), BF), ((images, width), BF), ((images, width), BF),
@@ -332,7 +342,7 @@
         got, w_in, w_out,
         flops=10**9,
     )
-    back = exchange(back)
+    back = exchange(back, BOTH)
     grad_w_in = weight_grad(rows, dact)
     grad_w_out = weight_grad(hidden, grad_rows)
     sums, ys, coef, mix, signal = call(

time: 47.6 us -> 47.4 us (level)
  no operation moved by 1% of the time
where the time goes in v9:
time: 47.4 us; the launch traced here: 47.2 us
  blocking collectives  27.4 us (58%)
  Pallas kernels  10.6 us (22%)
  starting transfers between devices  8.03 us (17%)
  between operations  0.76 us (2%)
    all_to_all x2, blocking collectives, exchange(): return lax.all_to_all(block, axes, split_axis=0, concat_axis=0, tiled=True)  27.4 us
    pallas_call x7, Pallas kernels, call(): pl.pallas_call(kernel, out_shape=[jax.ShapeDtypeStruct(shape, dtype) for...  10.6 us
    ppermute x7, starting transfers between devices, pair(): return lax.ppermute(term, BOTH, [(d, d ^ mask) for d in range(devices)])  8.03 us
  transfers between devices with their start and end apart: 7, of which 3 were waited for; matrix products, arithmetic and copies ran while one was open for 0% of the time, Pallas kernels for 10%

profile of v9, /device:TPU:0, one launch (start us, length us, event | category | flops | bytes accessed | tf_op | source)
XLA Modules:
  0.0 47.2 jit_solution(2609764134391434071)
XLA Ops:
  0.7 2.0 %shard_map.109 = (bf16[32,2,1408]{2,1,0:T(2,128)(2,1)S(1)}, f32[8,128]{1,0:T(8,128)S(1)}, f32[1,128]{1,0:T(1,128)S(1)}) custom-call(bf16[1,128,1280]{2,1,0:T(8,128)(2,1)} %tok_ref.3, bf16[1,128,1280]{2,1,0:T(8,128)(2,1)} %grad_ref.1, bf16[8,1280]{1,0:T(8,128)(2,1)} %bitcast.4, f32[1,8]{1,0:T(1,128)} %bitcast.6), custom_call_target="tpu_custom_call" | custom-call | flops 4000000000 | bytes 675872 | tf_op jit(solution)/shard_map/pallas_call | solution.py:263
  2.6 15.8 %all_to_all.10.got_ref = bf16[32,2,1408]{2,1,0:T(2,128)(2,1)S(1)} all-to-all(bf16[32,2,1408]{2,1,0:T(2,128)(2,1)S(1)} %get-tuple-element.30), channel_id=1, replica_groups=mesh['img'=16,'tok'=2] {'tok','img'}, dimensions={0} | all-to-all | bytes 360448 | tf_op jit(solution)/shard_map/all_to_all | solution.py:288
  18.5 0.0 copy-start.4
  18.5 0.0 copy-start.5
  18.5 2.6 %shard_map.110 = (bf16[32,2,1408]{2,1,0:T(2,128)(2,1)S(1)}, bf16[16,1280]{1,0:T(8,128)(2,1)S(1)}, bf16[16,1280]{1,0:T(8,128)(2,1)S(1)}, bf16[16,1024]{1,0:T(8,128)(2,1)S(1)}, bf16[16,1024]{1,0:T(8,128)(2,1)S(1)}) custom-call(bf16[32,2,1408]{2,1,0:T(2,128)(2,1)S(1)} %all_to_all.10.got_ref, bf16[1,1280,1024]{2,1,0:T(8,128)(2,1)S(1)} %copy-done, ...), custom_call_target="tpu_custom_call" | custom-call | flops 1000000000 | bytes 5423104 | tf_op jit(solution)/shard_map/pallas_call | solution.py:263
  21.1 11.6 %all_to_all.11.back_ref = bf16[32,2,1408]{2,1,0:T(2,128)(2,1)S(1)} all-to-all(bf16[32,2,1408]{2,1,0:T(2,128)(2,1)S(1)} %get-tuple-element.31), channel_id=1, replica_groups=mesh['img'=16,'tok'=2] {'img','tok'}, dimensions={0} | all-to-all | bytes 360448 | tf_op jit(solution)/shard_map/all_to_all | solution.py:288
  32.7 0.5 %shard_map.111 = (f32[8,1408]{1,0:T(8,128)S(1)}, bf16[8,1280]{1,0:T(8,128)(2,1)S(1)}, bf16[16,128]{1,0:T(8,128)(2,1)S(1)}, bf16[16,1280]{1,0:T(8,128)(2,1)S(1)}, f32[1,128]{1,0:T(1,128)S(1)}) custom-call(bf16[32,2,1408]{2,1,0:T(2,128)(2,1)S(1)} %all_to_all.11.back_ref, bf16[1,128,1280]{2,1,0:T(8,128)(2,1)S(1)} %copy-done.2, ...), custom_call_target="tpu_custom_call" | custom-call | flops 10000000 | bytes 860704 | tf_op jit(solution)/shard_map/pallas_call | solution.py:263
  33.2 0.0 collective-permute-start
  33.3 1.1 %shard_map.112 = (bf16[1,128,1280]{2,1,0:T(8,128)(2,1)}, bf16[1,128,1280]{2,1,0:T(8,128)(2,1)}) custom-call(bf16[1,128,1280]{2,1,0:T(8,128)(2,1)S(1)} %copy-done.2, f32[8,128]{1,0:T(8,128)S(1)} %get-tuple-element.32.logit_ref, bf16[8,1280]{1,0:T(8,128)(2,1)S(1)} %get-tuple-element.35.outs_ref, bf16[16,128]{1,0:T(8,128)(2,1)S(1)} %get-tuple-element.36.coef_ref, ...), custom_call_target="tpu_custom_call" | custom-call | flops 10000000 | bytes 397824 | tf_op jit(solution)/shard_map/pallas_call | solution.py:263
  34.4 0.1 collective-permute-done
  34.5 0.6 %collective-permute-start.3 = (bf16[8,1408]{1,0:T(8,128)(2,1)S(1)}, bf16[8,1408]{1,0:T(8,128)(2,1)S(1)}, u32[]{:S(2)}, u32[]{:S(2)}) collective-permute-start(bf16[8,1408]{1,0:T(8,128)(2,1)S(1)} %add_convert_fusion.1), channel_id=1, source_target_pairs={{0,5},{1,4},{2,7},{3,6},{4,1},{5,0},{6,3},{7,2},{8,13},{9,12},{10,... | collective-permute-start | bytes 67592 | tf_op jit(solution)/shard_map/ppermute | solution.py:292
  35.1 1.2 %collective-permute-start.1 = (bf16[8,1408]{1,0:T(8,128)(2,1)S(1)}, bf16[8,1408]{1,0:T(8,128)(2,1)S(1)}, u32[]{:S(2)}, u32[]{:S(2)}) collective-permute-start(bf16[8,1408]{1,0:T(8,128)(2,1)S(1)} %add_convert_fusion.1), channel_id=1, source_target_pairs={{0,4},{1,5},{2,6},{3,7},{4,0},{5,1},{6,2},{7,3},{8,12},{9,13},{10,... | collective-permute-start | bytes 67592 | tf_op jit(solution)/shard_map/ppermute | solution.py:292
  36.3 1.8 %collective-permute-start.2 = (bf16[8,1408]{1,0:T(8,128)(2,1)S(1)}, bf16[8,1408]{1,0:T(8,128)(2,1)S(1)}, u32[]{:S(2)}, u32[]{:S(2)}) collective-permute-start(bf16[8,1408]{1,0:T(8,128)(2,1)S(1)} %add_convert_fusion.1), channel_id=1, source_target_pairs={{0,1},{1,0},{2,3},{3,2},{4,5},{5,4},{6,7},{7,6},{8,9},{9,8},{10,11... | collective-permute-start | bytes 67592 | tf_op jit(solution)/shard_map/ppermute | solution.py:292
  38.0 1.8 %shard_map.113 = bf16[1,1280,1024]{2,1,0:T(8,128)(2,1)} custom-call(bf16[16,1280]{1,0:T(8,128)(2,1)S(1)} %get-tuple-element.44.left_ref, bf16[16,1024]{1,0:T(8,128)(2,1)S(1)} %get-tuple-element.45.right_ref), custom_call_target="tpu_custom_call" | custom-call | flops 1000000000 | bytes 73728 | tf_op jit(solution)/shard_map/pallas_call | solution.py:263
  39.9 0.0 collective-permute-done.3
  39.9 0.0 collective-permute-done.1
  39.9 0.2 collective-permute-done.2
  40.1 1.7 %collective-permute-start.6 = (bf16[8,1408]{1,0:T(8,128)(2,1)S(1)}, bf16[8,1408]{1,0:T(8,128)(2,1)S(1)}, u32[]{:S(2)}, u32[]{:S(2)}) collective-permute-start(bf16[8,1408]{1,0:T(8,128)(2,1)S(1)} %add_convert_fusion.own_ref), channel_id=1, source_target_pairs={{0,24},{1,25},{2,26},{3,27},{4,28},{5,29},{6,30},{7,31},{8,16},{9,... | collective-permute-start | bytes 67592 | tf_op jit(solution)/shard_map/ppermute | solution.py:292
  41.8 0.5 %collective-permute-start.4 = (bf16[8,1408]{1,0:T(8,128)(2,1)S(1)}, bf16[8,1408]{1,0:T(8,128)(2,1)S(1)}, u32[]{:S(2)}, u32[]{:S(2)}) collective-permute-start(bf16[8,1408]{1,0:T(8,128)(2,1)S(1)} %add_convert_fusion.own_ref), channel_id=1, source_target_pairs={{0,16},{1,17},{2,18},{3,19},{4,20},{5,21},{6,22},{7,23},{8,24},{9,... | collective-permute-start | bytes 67592 | tf_op jit(solution)/shard_map/ppermute | solution.py:292
  42.4 2.2 %collective-permute-start.5 = (bf16[8,1408]{1,0:T(8,128)(2,1)S(1)}, bf16[8,1408]{1,0:T(8,128)(2,1)S(1)}, u32[]{:S(2)}, u32[]{:S(2)}) collective-permute-start(bf16[8,1408]{1,0:T(8,128)(2,1)S(1)} %add_convert_fusion.own_ref), channel_id=1, source_target_pairs={{0,8},{1,9},{2,10},{3,11},{4,12},{5,13},{6,14},{7,15},{8,0},{9,1},... | collective-permute-start | bytes 67592 | tf_op jit(solution)/shard_map/ppermute | solution.py:292
  44.5 1.9 %shard_map.114 = bf16[1,1024,1280]{2,1,0:T(8,128)(2,1)} custom-call(bf16[16,1024]{1,0:T(8,128)(2,1)S(1)} %get-tuple-element.47.left_ref, bf16[16,1280]{1,0:T(8,128)(2,1)S(1)} %get-tuple-element.48.right_ref), custom_call_target="tpu_custom_call" | custom-call | flops 1000000000 | bytes 73728 | tf_op jit(solution)/shard_map/pallas_call | solution.py:263
  46.5 0.0 collective-permute-done.6.refs_1_
  46.5 0.1 collective-permute-done.4.other_ref
  46.6 0.6 %shard_map.115 = (f32[8,1280]{1,0:T(8,128)}, f32[1,8]{1,0:T(1,128)}) custom-call(bf16[8,1408]{1,0:T(8,128)(2,1)S(1)} %add_convert_fusion.own_ref, bf16[8,1408]{1,0:T(8,128)(2,1)S(1)} %collective-permute-done.4.other_ref, bf16[8,1408]{1,0:T(8,128)(2,1)S(1)} %collective-permute-done.5.refs_0_, bf16[8,1408]{1,0:T(8,128)(2,1)S(1)} %collective-permute-done.6.refs_1_), custom_call_target="tpu_custom_call" | custom-call | flops 10000000 | bytes 90112 | tf_op jit(solution)/shard_map/pallas_call | solution.py:263
  (13 shorter events, 0.0 us)
Async XLA Ops:
  0.6 17.8 %copy-start = (bf16[1,1280,1024]{2,1,0:T(8,128)(2,1)S(1)}, bf16[1,1280,1024]{2,1,0:T(8,128)(2,1)}, u32[]{:S(2)}) copy-start(bf16[1,1280,1024]{2,1,0:T(8,128)(2,1)} %one_ref.1) | copy-start | bytes 7864324
  0.6 17.8 %copy-start.1 = (bf16[1,1024,1280]{2,1,0:T(8,128)(2,1)S(1)}, bf16[1,1024,1280]{2,1,0:T(8,128)(2,1)}, u32[]{:S(2)}) copy-start(bf16[1,1024,1280]{2,1,0:T(8,128)(2,1)} %two_ref.1) | copy-start | bytes 7864324
  18.5 14.2 %copy-start.2 = (bf16[1,128,1280]{2,1,0:T(8,128)(2,1)S(1)}, bf16[1,128,1280]{2,1,0:T(8,128)(2,1)}, u32[]{:S(2)}) copy-start(bf16[1,128,1280]{2,1,0:T(8,128)(2,1)} %tok_ref.3) | copy-start | bytes 983044
  18.5 14.2 %copy-start.3 = (bf16[1,128,1280]{2,1,0:T(8,128)(2,1)S(1)}, bf16[1,128,1280]{2,1,0:T(8,128)(2,1)}, u32[]{:S(2)}) copy-start(bf16[1,128,1280]{2,1,0:T(8,128)(2,1)} %grad_ref.1) | copy-start | bytes 983044
  18.5 14.2 %copy-start.4 = (bf16[1280,8]{0,1:T(8,128)(2,1)S(1)}, bf16[1280,8]{0,1:T(8,128)(2,1)}, u32[]{:S(2)}) copy-start(bf16[1280,8]{0,1:T(8,128)(2,1)} %param.8) | copy-start | bytes 61444
  18.5 14.2 %copy-start.5 = (f32[8]{0:T(128)S(1)}, f32[8]{0:T(128)}, u32[]{:S(2)}) copy-start(f32[8]{0:T(128)} %param.9) | copy-start | bytes 100
  33.2 1.2 %collective-permute-start = (f32[8,1408]{1,0:T(8,128)S(1)}, f32[8,1408]{1,0:T(8,128)S(1)}, u32[]{:S(2)}, u32[]{:S(2)}) collective-permute-start(f32[8,1408]{1,0:T(8,128)S(1)} %get-tuple-element.34), channel_id=1, source_target_pairs={{0,2},{1,3},{2,0},{3,1},{4,6},{5,7},{6,4},{7,5},{8,10},{9,11},{10,... | collective-permute-start | bytes 135176 | tf_op jit(solution)/shard_map/ppermute | solution.py:292
  34.5 5.4 %collective-permute-start.3 = (bf16[8,1408]{1,0:T(8,128)(2,1)S(1)}, bf16[8,1408]{1,0:T(8,128)(2,1)S(1)}, u32[]{:S(2)}, u32[]{:S(2)}) collective-permute-start(bf16[8,1408]{1,0:T(8,128)(2,1)S(1)} %add_convert_fusion.1), channel_id=1, source_target_pairs={{0,5},{1,4},{2,7},{3,6},{4,1},{5,0},{6,3},{7,2},{8,13},{9,12},{10,... | collective-permute-start | bytes 67592 | tf_op jit(solution)/shard_map/ppermute | solution.py:292
  35.1 4.8 %collective-permute-start.1 = (bf16[8,1408]{1,0:T(8,128)(2,1)S(1)}, bf16[8,1408]{1,0:T(8,128)(2,1)S(1)}, u32[]{:S(2)}, u32[]{:S(2)}) collective-permute-start(bf16[8,1408]{1,0:T(8,128)(2,1)S(1)} %add_convert_fusion.1), channel_id=1, source_target_pairs={{0,4},{1,5},{2,6},{3,7},{4,0},{5,1},{6,2},{7,3},{8,12},{9,13},{10,... | collective-permute-start | bytes 67592 | tf_op jit(solution)/shard_map/ppermute | solution.py:292
  36.3 3.8 %collective-permute-start.2 = (bf16[8,1408]{1,0:T(8,128)(2,1)S(1)}, bf16[8,1408]{1,0:T(8,128)(2,1)S(1)}, u32[]{:S(2)}, u32[]{:S(2)}) collective-permute-start(bf16[8,1408]{1,0:T(8,128)(2,1)S(1)} %add_convert_fusion.1), channel_id=1, source_target_pairs={{0,1},{1,0},{2,3},{3,2},{4,5},{5,4},{6,7},{7,6},{8,9},{9,8},{10,11... | collective-permute-start | bytes 67592 | tf_op jit(solution)/shard_map/ppermute | solution.py:292
  40.1 6.4 %collective-permute-start.6 = (bf16[8,1408]{1,0:T(8,128)(2,1)S(1)}, bf16[8,1408]{1,0:T(8,128)(2,1)S(1)}, u32[]{:S(2)}, u32[]{:S(2)}) collective-permute-start(bf16[8,1408]{1,0:T(8,128)(2,1)S(1)} %add_convert_fusion.own_ref), channel_id=1, source_target_pairs={{0,24},{1,25},{2,26},{3,27},{4,28},{5,29},{6,30},{7,31},{8,16},{9,... | collective-permute-start | bytes 67592 | tf_op jit(solution)/shard_map/ppermute | solution.py:292
  41.8 4.7 %collective-permute-start.4 = (bf16[8,1408]{1,0:T(8,128)(2,1)S(1)}, bf16[8,1408]{1,0:T(8,128)(2,1)S(1)}, u32[]{:S(2)}, u32[]{:S(2)}) collective-permute-start(bf16[8,1408]{1,0:T(8,128)(2,1)S(1)} %add_convert_fusion.own_ref), channel_id=1, source_target_pairs={{0,16},{1,17},{2,18},{3,19},{4,20},{5,21},{6,22},{7,23},{8,24},{9,... | collective-permute-start | bytes 67592 | tf_op jit(solution)/shard_map/ppermute | solution.py:292
  42.4 4.2 %collective-permute-start.5 = (bf16[8,1408]{1,0:T(8,128)(2,1)S(1)}, bf16[8,1408]{1,0:T(8,128)(2,1)S(1)}, u32[]{:S(2)}, u32[]{:S(2)}) collective-permute-start(bf16[8,1408]{1,0:T(8,128)(2,1)S(1)} %add_convert_fusion.own_ref), channel_id=1, source_target_pairs={{0,8},{1,9},{2,10},{3,11},{4,12},{5,13},{6,14},{7,15},{8,0},{9,1},... | collective-permute-start | bytes 67592 | tf_op jit(solution)/shard_map/ppermute | solution.py:292

commit v10 on v9

--- a/solution.py
+++ b/solution.py
@@ -12,7 +12,9 @@
 DENSITY = 0.3989422804014327
 BF = jnp.bfloat16
 F32 = jnp.float32
-BOTH = ("img", "tok")
+BOTH = ("far", "near", "tok")
+OUT_ORDER = ("tok", "near", "far")
+BACK_ORDER = ("tok", "far", "near")
 LANES = 128
 FRONT = 4 * 10**9
 
@@ -114,10 +116,12 @@
     return key
 
 
-def half_first(key, inner, halves):
+def in_order(key, order, sizes):
     def moved(row):
-        half, place, kind = digits(row, (halves, inner, 2))
-        return key((place * halves + half) * 2 + kind)
+        *places, kind = digits(row, [sizes[axis] for axis in order] + [2])
+        at = dict(zip(order, places))
+        place = (at["far"] * sizes["near"] + at["near"]) * sizes["tok"] + at["tok"]
+        return key(place * 2 + kind)
 
     return moved
 
@@ -135,7 +139,7 @@
 
 
 def front_kernel(
-    plan, tok_hbm, grad_hbm, router_hbm, scale_hbm, sent_ref, logit_ref, inv_ref,
+    plan, sizes, tok_hbm, grad_hbm, router_hbm, scale_hbm, sent_ref, logit_ref, inv_ref,
     tok_ref, grad_ref, router_ref, scale_ref, sems,
 ):
     arrived = fetch(
@@ -155,18 +159,18 @@
     dys = dot(comb.astype(BF), grad_ref[0], ((1,), (0,)))
     rows = stack_rows(numer, dys, [jnp.sum(expo, 1, keepdims=True)])
     experts = router_ref.shape[0]
-    key = half_first(expert_rows(plan, experts), plan[0] * experts, plan[1])
+    key = in_order(expert_rows(plan, experts), OUT_ORDER, sizes)
     store_blocks(sent_ref, pick(key, 2 * sent_ref.shape[0], rows, itself))
     logit_ref[...] = logit
     inv_ref[...] = inv_x
 
 
 def expert_kernel(
-    images, halves, got_ref, one_ref, two_ref, back_ref, rows_ref, grad_rows_ref, hidden_ref, dact_ref
+    images, halves, sizes, got_ref, one_ref, two_ref, back_ref, rows_ref, grad_rows_ref, hidden_ref, dact_ref
 ):
     width = one_ref.shape[1]
     key = image_rows(images, halves)
-    sums = pick(itself, 2 * images, load_blocks(got_ref), half_first(key, images, halves))
+    sums = pick(itself, 2 * images, load_blocks(got_ref), in_order(key, OUT_ORDER, sizes))
     den = sums[:images, width : width + 1] + sums[images:, width : width + 1]
     rows = (sums[:images, :width] / den).astype(BF)
     grad_rows = sums[images:, :width].astype(BF)
@@ -179,7 +183,8 @@
     in_part = dot(dact, one_ref[0], ((1,), (1,)))
     corr = jnp.sum(dact.astype(F32) * act, 1, keepdims=True)
     packed = stack_rows(out_part, in_part, [den, corr])
-    store_blocks(back_ref, pick(key, 2 * back_ref.shape[0], packed, itself))
+    back_key = in_order(key, BACK_ORDER, sizes)
+    store_blocks(back_ref, pick(back_key, 2 * back_ref.shape[0], packed, itself))
     rows_ref[...] = rows
     grad_rows_ref[...] = grad_rows
     hidden_ref[...] = hidden
@@ -202,11 +207,11 @@
 
 
 def middle_kernel(
-    plan, back_ref, tok_ref, grad_ref, logit_ref, inv_ref, router_ref, scale_ref,
+    plan, sizes, back_ref, tok_ref, grad_ref, logit_ref, inv_ref, router_ref, scale_ref,
     sums_ref, outs_ref, coef_ref, mix_ref, signal_ref,
 ):
     experts, width = router_ref.shape
-    sums = pick(itself, 2 * experts, load_blocks(back_ref), expert_rows(plan, router_ref.shape[0]))
+    sums = pick(itself, 2 * experts, load_blocks(back_ref), in_order(expert_rows(plan, experts), BACK_ORDER, sizes))
     extras = sums[:experts, width:] + sums[experts:, width:]
     den = extras[:, :1] * (1.0 / (plan[0] * plan[1]))
     corr = extras[:, 1:2]
@@ -316,7 +321,8 @@
     return terms, done + beside[len(done) :]
 
 
-def shards(images, halves, tokens, grad_out, router, slot_scale, w_in, w_out):
+def shards(sizes, tokens, grad_out, router, slot_scale, w_in, w_out):
+    images, halves = sizes["far"] * sizes["near"], sizes["tok"]
     devices = images * halves
     tok_rows, width = tokens.shape[1:]
     experts = router.shape[1]
@@ -327,26 +333,26 @@
     scale_row = slot_scale.reshape(1, experts)
     inputs = (tokens, grad_out, router_t, scale_row)
     sent, logit, inv_x = call(
-        functools.partial(front_kernel, plan),
+        functools.partial(front_kernel, plan, sizes),
         [((devices, 2, long), BF), ((experts, tok_rows), F32), ((1, tok_rows), F32)],
         *inputs,
         stays=range(4),
         buffers=[pltpu.VMEM(a.shape, a.dtype) for a in inputs] + [pltpu.SemaphoreType.DMA((4,))],
         flops=FRONT,
     )
-    got = exchange(sent, ("tok", "img"))
+    got = exchange(sent, OUT_ORDER)
     back, rows, grad_rows, hidden, dact = call(
-        functools.partial(expert_kernel, images, halves),
+        functools.partial(expert_kernel, images, halves, sizes),
         [((devices, 2, long), BF), ((images, width), BF), ((images, width), BF),
          ((images, hidden_dev), BF), ((images, hidden_dev), BF)],
         got, w_in, w_out,
         flops=10**9,
     )
-    back = exchange(back, BOTH)
+    back = exchange(back, BACK_ORDER)
     grad_w_in = weight_grad(rows, dact)
     grad_w_out = weight_grad(hidden, grad_rows)
     sums, ys, coef, mix, signal = call(
-        functools.partial(middle_kernel, plan),
+        functools.partial(middle_kernel, plan, sizes),
         [((experts, long), F32), ((experts, width), BF), ((2 * experts, tok_rows), BF),
          ((2 * experts, width), BF), ((1, tok_rows), F32)],
         back, tokens, grad_out, logit, inv_x, router_t, scale_row,
@@ -367,28 +373,20 @@
 
 def solution(mesh):
     images, halves = mesh.shape["img"], mesh.shape["tok"]
+    near = min(4, images)
+    sizes = {"far": images // near, "near": near, "tok": halves}
+    split = jax.sharding.Mesh(mesh.devices.reshape(tuple(sizes.values())), BOTH)
+    img = ("far", "near")
 
     def body(*args):
-        return shards(images, halves, *args)
-
-    return jax.shard_map(
-        body,
-        mesh=mesh,
-        in_specs=(
-            P("img", "tok", None),
-            P("img", "tok", None),
-            P(),
-            P(),
-            P("img", None, "tok"),
-            P("img", "tok", None),
-        ),
-        out_specs=(
-            P("img", "tok", None),
-            P("img", "tok", None),
-            P(),
-            P(),
-            P("img", None, "tok"),
-            P("img", "tok", None),
-        ),
-        check_vma=False,
-    )
+        return shards(sizes, *args)
+
+    placed = (
+        P(img, "tok", None),
+        P(img, "tok", None),
+        P(),
+        P(),
+        P(img, None, "tok"),
+        P(img, "tok", None),
+    )
+    return jax.shard_map(body, mesh=split, in_specs=placed, out_specs=placed, check_vma=False)

time: 47.4 us -> 47.5 us (level)
  blocking collectives: 27.4 us -> 26.8 us
  starting transfers between devices: 8.03 us -> 8.58 us
    all_to_all x2, blocking collectives: 27.4 us -> 26.8 us  [exchange(): return lax.all_to_all(block, axes, split_axis=0, concat_axis=0, tiled=True)]
    ppermute x7, starting transfers between devices: 8.03 us -> 8.58 us  [pair(): return lax.ppermute(term, BOTH, [(d, d ^ mask) for d in range(devices)])]
  transfers between devices with their start and end apart: 7 -> 7, of which waited for: 3 -> 1; matrix products, arithmetic and copies ran while one was open for 0% -> 0% of each run, Pallas kernels for 10% -> 10%
where the time goes in v10:
time: 47.5 us; the launch traced here: 47.3 us
  blocking collectives  26.8 us (56%)
  Pallas kernels  10.6 us (22%)
  starting transfers between devices  8.58 us (18%)
  between operations  0.76 us (2%)
  waiting for transfers between devices  0.48 us (1%)
    all_to_all x2, blocking collectives, exchange(): return lax.all_to_all(block, axes, split_axis=0, concat_axis=0, tiled=True)  26.8 us
    pallas_call x7, Pallas kernels, call(): pl.pallas_call(kernel, out_shape=[jax.ShapeDtypeStruct(shape, dtype) for...  10.6 us
    ppermute x7, starting transfers between devices, pair(): return lax.ppermute(term, BOTH, [(d, d ^ mask) for d in range(devices)])  8.58 us
  transfers between devices with their start and end apart: 7, of which 1 were waited for; matrix products, arithmetic and copies ran while one was open for 0% of the time, Pallas kernels for 10%

profile of v10, /device:TPU:0, one launch (start us, length us, event | category | flops | bytes accessed | tf_op | source)
XLA Modules:
  0.0 47.3 jit_solution(15185392100230337162)
XLA Ops:
  0.7 2.0 %shard_map.109 = (bf16[32,2,1408]{2,1,0:T(2,128)(2,1)S(1)}, f32[8,128]{1,0:T(8,128)S(1)}, f32[1,128]{1,0:T(1,128)S(1)}) custom-call(bf16[1,128,1280]{2,1,0:T(8,128)(2,1)} %tok_ref.3, bf16[1,128,1280]{2,1,0:T(8,128)(2,1)} %grad_ref.1, bf16[8,1280]{1,0:T(8,128)(2,1)} %bitcast.4, f32[1,8]{1,0:T(1,128)} %bitcast.6), custom_call_target="tpu_custom_call" | custom-call | flops 4000000000 | bytes 675872 | tf_op jit(solution)/shard_map/pallas_call | solution.py:268
  2.6 16.2 %all_to_all.10.got_ref = bf16[32,2,1408]{2,1,0:T(2,128)(2,1)S(1)} all-to-all(bf16[32,2,1408]{2,1,0:T(2,128)(2,1)S(1)} %get-tuple-element.30), channel_id=1, replica_groups=mesh['far'=4,'near'=4,'tok'=2] {'tok','near','far'}, dimensions={0} | all-to-all | bytes 360448 | tf_op jit(solution)/shard_map/all_to_all | solution.py:293
  18.9 0.0 copy-start.4
  18.9 0.0 copy-start.5
  18.9 2.6 %shard_map.110 = (bf16[32,2,1408]{2,1,0:T(2,128)(2,1)S(1)}, bf16[16,1280]{1,0:T(8,128)(2,1)S(1)}, bf16[16,1280]{1,0:T(8,128)(2,1)S(1)}, bf16[16,1024]{1,0:T(8,128)(2,1)S(1)}, bf16[16,1024]{1,0:T(8,128)(2,1)S(1)}) custom-call(bf16[32,2,1408]{2,1,0:T(2,128)(2,1)S(1)} %all_to_all.10.got_ref, bf16[1,1280,1024]{2,1,0:T(8,128)(2,1)S(1)} %copy-done, ...), custom_call_target="tpu_custom_call" | custom-call | flops 1000000000 | bytes 5423104 | tf_op jit(solution)/shard_map/pallas_call | solution.py:268
  21.5 10.6 %all_to_all.11.back_ref = bf16[32,2,1408]{2,1,0:T(2,128)(2,1)S(1)} all-to-all(bf16[32,2,1408]{2,1,0:T(2,128)(2,1)S(1)} %get-tuple-element.31), channel_id=1, replica_groups=mesh['far'=4,'near'=4,'tok'=2] {'tok','far','near'}, dimensions={0} | all-to-all | bytes 360448 | tf_op jit(solution)/shard_map/all_to_all | solution.py:293
  32.1 0.5 %shard_map.111 = (f32[8,1408]{1,0:T(8,128)S(1)}, bf16[8,1280]{1,0:T(8,128)(2,1)S(1)}, bf16[16,128]{1,0:T(8,128)(2,1)S(1)}, bf16[16,1280]{1,0:T(8,128)(2,1)S(1)}, f32[1,128]{1,0:T(1,128)S(1)}) custom-call(bf16[32,2,1408]{2,1,0:T(2,128)(2,1)S(1)} %all_to_all.11.back_ref, bf16[1,128,1280]{2,1,0:T(8,128)(2,1)S(1)} %copy-done.2, ...), custom_call_target="tpu_custom_call" | custom-call | flops 10000000 | bytes 860704 | tf_op jit(solution)/shard_map/pallas_call | solution.py:268
  32.6 0.6 %collective-permute-start = (f32[8,1408]{1,0:T(8,128)S(1)}, f32[8,1408]{1,0:T(8,128)S(1)}, u32[]{:S(2)}, u32[]{:S(2)}) collective-permute-start(f32[8,1408]{1,0:T(8,128)S(1)} %get-tuple-element.34), channel_id=1, source_target_pairs={{0,2},{1,3},{2,0},{3,1},{4,6},{5,7},{6,4},{7,5},{8,10},{9,11},{10,... | collective-permute-start | bytes 135176 | tf_op jit(solution)/shard_map/ppermute | solution.py:297
  33.2 1.1 %shard_map.112 = (bf16[1,128,1280]{2,1,0:T(8,128)(2,1)}, bf16[1,128,1280]{2,1,0:T(8,128)(2,1)}) custom-call(bf16[1,128,1280]{2,1,0:T(8,128)(2,1)S(1)} %copy-done.2, f32[8,128]{1,0:T(8,128)S(1)} %get-tuple-element.32.logit_ref, bf16[8,1280]{1,0:T(8,128)(2,1)S(1)} %get-tuple-element.35.outs_ref, bf16[16,128]{1,0:T(8,128)(2,1)S(1)} %get-tuple-element.36.coef_ref, ...), custom_call_target="tpu_custom_call" | custom-call | flops 10000000 | bytes 397824 | tf_op jit(solution)/shard_map/pallas_call | solution.py:268
  34.4 0.0 collective-permute-done
  34.4 0.8 %collective-permute-start.3 = (bf16[8,1408]{1,0:T(8,128)(2,1)S(1)}, bf16[8,1408]{1,0:T(8,128)(2,1)S(1)}, u32[]{:S(2)}, u32[]{:S(2)}) collective-permute-start(bf16[8,1408]{1,0:T(8,128)(2,1)S(1)} %add_convert_fusion.1), channel_id=1, source_target_pairs={{0,5},{1,4},{2,7},{3,6},{4,1},{5,0},{6,3},{7,2},{8,13},{9,12},{10,... | collective-permute-start | bytes 67592 | tf_op jit(solution)/shard_map/ppermute | solution.py:297
  35.1 1.3 %collective-permute-start.1 = (bf16[8,1408]{1,0:T(8,128)(2,1)S(1)}, bf16[8,1408]{1,0:T(8,128)(2,1)S(1)}, u32[]{:S(2)}, u32[]{:S(2)}) collective-permute-start(bf16[8,1408]{1,0:T(8,128)(2,1)S(1)} %add_convert_fusion.1), channel_id=1, source_target_pairs={{0,4},{1,5},{2,6},{3,7},{4,0},{5,1},{6,2},{7,3},{8,12},{9,13},{10,... | collective-permute-start | bytes 67592 | tf_op jit(solution)/shard_map/ppermute | solution.py:297
  36.4 1.5 %collective-permute-start.2 = (bf16[8,1408]{1,0:T(8,128)(2,1)S(1)}, bf16[8,1408]{1,0:T(8,128)(2,1)S(1)}, u32[]{:S(2)}, u32[]{:S(2)}) collective-permute-start(bf16[8,1408]{1,0:T(8,128)(2,1)S(1)} %add_convert_fusion.1), channel_id=1, source_target_pairs={{0,1},{1,0},{2,3},{3,2},{4,5},{5,4},{6,7},{7,6},{8,9},{9,8},{10,11... | collective-permute-start | bytes 67592 | tf_op jit(solution)/shard_map/ppermute | solution.py:297
  37.9 1.8 %shard_map.113 = bf16[1,1280,1024]{2,1,0:T(8,128)(2,1)} custom-call(bf16[16,1280]{1,0:T(8,128)(2,1)S(1)} %get-tuple-element.44.left_ref, bf16[16,1024]{1,0:T(8,128)(2,1)S(1)} %get-tuple-element.45.right_ref), custom_call_target="tpu_custom_call" | custom-call | flops 1000000000 | bytes 73728 | tf_op jit(solution)/shard_map/pallas_call | solution.py:268
  39.8 0.0 collective-permute-done.3
  39.8 0.0 collective-permute-done.1
  39.8 0.5 collective-permute-done.2
  40.3 1.5 %collective-permute-start.6 = (bf16[8,1408]{1,0:T(8,128)(2,1)S(1)}, bf16[8,1408]{1,0:T(8,128)(2,1)S(1)}, u32[]{:S(2)}, u32[]{:S(2)}) collective-permute-start(bf16[8,1408]{1,0:T(8,128)(2,1)S(1)} %add_convert_fusion.own_ref), channel_id=1, source_target_pairs={{0,24},{1,25},{2,26},{3,27},{4,28},{5,29},{6,30},{7,31},{8,16},{9,... | collective-permute-start | bytes 67592 | tf_op jit(solution)/shard_map/ppermute | solution.py:297
  41.7 0.7 %collective-permute-start.4 = (bf16[8,1408]{1,0:T(8,128)(2,1)S(1)}, bf16[8,1408]{1,0:T(8,128)(2,1)S(1)}, u32[]{:S(2)}, u32[]{:S(2)}) collective-permute-start(bf16[8,1408]{1,0:T(8,128)(2,1)S(1)} %add_convert_fusion.own_ref), channel_id=1, source_target_pairs={{0,16},{1,17},{2,18},{3,19},{4,20},{5,21},{6,22},{7,23},{8,24},{9,... | collective-permute-start | bytes 67592 | tf_op jit(solution)/shard_map/ppermute | solution.py:297
  42.4 2.3 %collective-permute-start.5 = (bf16[8,1408]{1,0:T(8,128)(2,1)S(1)}, bf16[8,1408]{1,0:T(8,128)(2,1)S(1)}, u32[]{:S(2)}, u32[]{:S(2)}) collective-permute-start(bf16[8,1408]{1,0:T(8,128)(2,1)S(1)} %add_convert_fusion.own_ref), channel_id=1, source_target_pairs={{0,8},{1,9},{2,10},{3,11},{4,12},{5,13},{6,14},{7,15},{8,0},{9,1},... | collective-permute-start | bytes 67592 | tf_op jit(solution)/shard_map/ppermute | solution.py:297
  44.7 1.9 %shard_map.114 = bf16[1,1024,1280]{2,1,0:T(8,128)(2,1)} custom-call(bf16[16,1024]{1,0:T(8,128)(2,1)S(1)} %get-tuple-element.47.left_ref, bf16[16,1280]{1,0:T(8,128)(2,1)S(1)} %get-tuple-element.48.right_ref), custom_call_target="tpu_custom_call" | custom-call | flops 1000000000 | bytes 73728 | tf_op jit(solution)/shard_map/pallas_call | solution.py:268
  46.7 0.0 collective-permute-done.4.other_ref
  46.7 0.0 collective-permute-done.5.refs_0_
  46.7 0.6 %shard_map.115 = (f32[8,1280]{1,0:T(8,128)}, f32[1,8]{1,0:T(1,128)}) custom-call(bf16[8,1408]{1,0:T(8,128)(2,1)S(1)} %add_convert_fusion.own_ref, bf16[8,1408]{1,0:T(8,128)(2,1)S(1)} %collective-permute-done.4.other_ref, bf16[8,1408]{1,0:T(8,128)(2,1)S(1)} %collective-permute-done.5.refs_0_, bf16[8,1408]{1,0:T(8,128)(2,1)S(1)} %collective-permute-done.6.refs_1_), custom_call_target="tpu_custom_call" | custom-call | flops 10000000 | bytes 90112 | tf_op jit(solution)/shard_map/pallas_call | solution.py:268
  (13 shorter events, 0.0 us)
Async XLA Ops:
  0.6 18.2 %copy-start = (bf16[1,1280,1024]{2,1,0:T(8,128)(2,1)S(1)}, bf16[1,1280,1024]{2,1,0:T(8,128)(2,1)}, u32[]{:S(2)}) copy-start(bf16[1,1280,1024]{2,1,0:T(8,128)(2,1)} %one_ref.1) | copy-start | bytes 7864324
  0.6 18.2 %copy-start.1 = (bf16[1,1024,1280]{2,1,0:T(8,128)(2,1)S(1)}, bf16[1,1024,1280]{2,1,0:T(8,128)(2,1)}, u32[]{:S(2)}) copy-start(bf16[1,1024,1280]{2,1,0:T(8,128)(2,1)} %two_ref.1) | copy-start | bytes 7864324
  18.9 13.2 %copy-start.2 = (bf16[1,128,1280]{2,1,0:T(8,128)(2,1)S(1)}, bf16[1,128,1280]{2,1,0:T(8,128)(2,1)}, u32[]{:S(2)}) copy-start(bf16[1,128,1280]{2,1,0:T(8,128)(2,1)} %tok_ref.3) | copy-start | bytes 983044
  18.9 13.2 %copy-start.3 = (bf16[1,128,1280]{2,1,0:T(8,128)(2,1)S(1)}, bf16[1,128,1280]{2,1,0:T(8,128)(2,1)}, u32[]{:S(2)}) copy-start(bf16[1,128,1280]{2,1,0:T(8,128)(2,1)} %grad_ref.1) | copy-start | bytes 983044
  18.9 13.2 %copy-start.4 = (bf16[1280,8]{0,1:T(8,128)(2,1)S(1)}, bf16[1280,8]{0,1:T(8,128)(2,1)}, u32[]{:S(2)}) copy-start(bf16[1280,8]{0,1:T(8,128)(2,1)} %param.8) | copy-start | bytes 61444
  18.9 13.2 %copy-start.5 = (f32[8]{0:T(128)S(1)}, f32[8]{0:T(128)}, u32[]{:S(2)}) copy-start(f32[8]{0:T(128)} %param.9) | copy-start | bytes 100
  32.6 1.7 %collective-permute-start = (f32[8,1408]{1,0:T(8,128)S(1)}, f32[8,1408]{1,0:T(8,128)S(1)}, u32[]{:S(2)}, u32[]{:S(2)}) collective-permute-start(f32[8,1408]{1,0:T(8,128)S(1)} %get-tuple-element.34), channel_id=1, source_target_pairs={{0,2},{1,3},{2,0},{3,1},{4,6},{5,7},{6,4},{7,5},{8,10},{9,11},{10,... | collective-permute-start | bytes 135176 | tf_op jit(solution)/shard_map/ppermute | solution.py:297
  34.4 5.4 %collective-permute-start.3 = (bf16[8,1408]{1,0:T(8,128)(2,1)S(1)}, bf16[8,1408]{1,0:T(8,128)(2,1)S(1)}, u32[]{:S(2)}, u32[]{:S(2)}) collective-permute-start(bf16[8,1408]{1,0:T(8,128)(2,1)S(1)} %add_convert_fusion.1), channel_id=1, source_target_pairs={{0,5},{1,4},{2,7},{3,6},{4,1},{5,0},{6,3},{7,2},{8,13},{9,12},{10,... | collective-permute-start | bytes 67592 | tf_op jit(solution)/shard_map/ppermute | solution.py:297
  35.1 4.7 %collective-permute-start.1 = (bf16[8,1408]{1,0:T(8,128)(2,1)S(1)}, bf16[8,1408]{1,0:T(8,128)(2,1)S(1)}, u32[]{:S(2)}, u32[]{:S(2)}) collective-permute-start(bf16[8,1408]{1,0:T(8,128)(2,1)S(1)} %add_convert_fusion.1), channel_id=1, source_target_pairs={{0,4},{1,5},{2,6},{3,7},{4,0},{5,1},{6,2},{7,3},{8,12},{9,13},{10,... | collective-permute-start | bytes 67592 | tf_op jit(solution)/shard_map/ppermute | solution.py:297
  36.4 3.8 %collective-permute-start.2 = (bf16[8,1408]{1,0:T(8,128)(2,1)S(1)}, bf16[8,1408]{1,0:T(8,128)(2,1)S(1)}, u32[]{:S(2)}, u32[]{:S(2)}) collective-permute-start(bf16[8,1408]{1,0:T(8,128)(2,1)S(1)} %add_convert_fusion.1), channel_id=1, source_target_pairs={{0,1},{1,0},{2,3},{3,2},{4,5},{5,4},{6,7},{7,6},{8,9},{9,8},{10,11... | collective-permute-start | bytes 67592 | tf_op jit(solution)/shard_map/ppermute | solution.py:297
  40.3 6.4 %collective-permute-start.6 = (bf16[8,1408]{1,0:T(8,128)(2,1)S(1)}, bf16[8,1408]{1,0:T(8,128)(2,1)S(1)}, u32[]{:S(2)}, u32[]{:S(2)}) collective-permute-start(bf16[8,1408]{1,0:T(8,128)(2,1)S(1)} %add_convert_fusion.own_ref), channel_id=1, source_target_pairs={{0,24},{1,25},{2,26},{3,27},{4,28},{5,29},{6,30},{7,31},{8,16},{9,... | collective-permute-start | bytes 67592 | tf_op jit(solution)/shard_map/ppermute | solution.py:297
  41.7 4.9 %collective-permute-start.4 = (bf16[8,1408]{1,0:T(8,128)(2,1)S(1)}, bf16[8,1408]{1,0:T(8,128)(2,1)S(1)}, u32[]{:S(2)}, u32[]{:S(2)}) collective-permute-start(bf16[8,1408]{1,0:T(8,128)(2,1)S(1)} %add_convert_fusion.own_ref), channel_id=1, source_target_pairs={{0,16},{1,17},{2,18},{3,19},{4,20},{5,21},{6,22},{7,23},{8,24},{9,... | collective-permute-start | bytes 67592 | tf_op jit(solution)/shard_map/ppermute | solution.py:297
  42.4 4.3 %collective-permute-start.5 = (bf16[8,1408]{1,0:T(8,128)(2,1)S(1)}, bf16[8,1408]{1,0:T(8,128)(2,1)S(1)}, u32[]{:S(2)}, u32[]{:S(2)}) collective-permute-start(bf16[8,1408]{1,0:T(8,128)(2,1)S(1)} %add_convert_fusion.own_ref), channel_id=1, source_target_pairs={{0,8},{1,9},{2,10},{3,11},{4,12},{5,13},{6,14},{7,15},{8,0},{9,1},... | collective-permute-start | bytes 67592 | tf_op jit(solution)/shard_map/ppermute | solution.py:297

commit v11 on v9

--- a/solution.py
+++ b/solution.py
@@ -47,8 +47,10 @@
     return dot(selection((left_size, right.shape[0]), left_key, right_key), right, ((1,), (0,)))
 
 
-def store_blocks(ref, rows):
-    ref[...] = rows.astype(BF).reshape(ref.shape)
+def store_copies(ref, rows):
+    pairs = rows.astype(BF).reshape(rows.shape[0] // 2, 2, rows.shape[1])
+    for start in range(0, ref.shape[0], pairs.shape[0]):
+        ref[start : start + pairs.shape[0]] = pairs
 
 
 def load_blocks(ref):
@@ -65,21 +67,20 @@
     return jnp.sum(jnp.where(eye, row, 0.0), 1, keepdims=True)
 
 
-def row_of(column):
-    return jnp.transpose(jnp.broadcast_to(column, (column.shape[0], LANES)))[:1]
-
-
-def stack_rows(first, second, extras):
-    lane = iota((first.shape[0], LANES), 1)
+def lane_pair(extras):
+    lane = iota((extras[0].shape[0], LANES), 1)
     high = jnp.zeros(lane.shape, F32)
     low = jnp.zeros(lane.shape, F32)
     for place, value in enumerate(extras):
         top = value.astype(BF).astype(F32)
         high = jnp.where(lane == place, top, high)
         low = jnp.where(lane == place, value - top, low)
-    return jnp.concatenate(
-        [jnp.concatenate([first, high], 1), jnp.concatenate([second, low], 1)], 0
-    ).astype(BF)
+    return high, low
+
+
+def pick_pairs(rows, kind):
+    hit = iota((2 * rows.shape[0], rows.shape[0]), 0) == 2 * iota((2 * rows.shape[0], rows.shape[0]), 1) + kind
+    return dot(jnp.where(hit, 1.0, 0.0).astype(BF), rows, ((1,), (0,)))
 
 
 def slot_column(router_ref, scale_ref):
@@ -144,19 +145,24 @@
     for copy in arrived[:3]:
         copy.wait()
     tok = tok_ref[0]
-    tok_f = tok.astype(F32)
-    inv_x = row_of(lax.rsqrt(jnp.sum(tok_f * tok_f, 1, keepdims=True) + EPSILON))
+    experts = router_ref.shape[0]
+    square = tok.astype(F32) * tok.astype(F32)
+    top = square.astype(BF)
+    ones = jnp.ones((8, tok.shape[1]), BF)
+    norm = dot(ones, top, ((1,), (1,))) + dot(ones, (square - top.astype(F32)).astype(BF), ((1,), (1,)))
+    inv_x = lax.rsqrt(norm[:1] + EPSILON)
     _, inv_p, scale = slot_column(router_ref, scale_ref)
     raw = dot(router_ref[...], tok, ((1,), (1,)))
     logit = raw * inv_x * (inv_p * scale)
     expo, comb = softmax(logit)
-    numer = dot(expo.astype(BF), tok, ((1,), (0,)))
+    first = pick_pairs(expo.astype(BF), 0)
+    second = pick_pairs(comb.astype(BF), 1)
+    high, low = lane_pair([jnp.sum(expo, 1, keepdims=True)])
+    extras = pick_pairs(high.astype(BF), 0) + pick_pairs(low.astype(BF), 1)
+    numer = dot(first.astype(BF), tok, ((1,), (0,)))
     arrived[3].wait()
-    dys = dot(comb.astype(BF), grad_ref[0], ((1,), (0,)))
-    rows = stack_rows(numer, dys, [jnp.sum(expo, 1, keepdims=True)])
-    experts = router_ref.shape[0]
-    key = half_first(expert_rows(plan, experts), plan[0] * experts, plan[1])
-    store_blocks(sent_ref, pick(key, 2 * sent_ref.shape[0], rows, itself))
+    dys = dot(second.astype(BF), grad_ref[0], ((1,), (0,)))
+    store_copies(sent_ref, jnp.concatenate([numer + dys, extras], 1))
     logit_ref[...] = logit
     inv_ref[...] = inv_x
 
@@ -178,8 +184,10 @@
     out_part = dot(hidden, two_ref[0], ((1,), (0,)))
     in_part = dot(dact, one_ref[0], ((1,), (1,)))
     corr = jnp.sum(dact.astype(F32) * act, 1, keepdims=True)
-    packed = stack_rows(out_part, in_part, [den, corr])
-    store_blocks(back_ref, pick(key, 2 * back_ref.shape[0], packed, itself))
+    high, low = lane_pair([den, corr])
+    first = jnp.concatenate([out_part, high], 1).astype(BF)
+    second = jnp.concatenate([in_part, low], 1).astype(BF)
+    store_copies(back_ref, pick_pairs(first, 0) + pick_pairs(second, 1))
     rows_ref[...] = rows
     grad_rows_ref[...] = grad_rows
     hidden_ref[...] = hidden
@@ -206,7 +214,8 @@
     sums_ref, outs_ref, coef_ref, mix_ref, signal_ref,
 ):
     experts, width = router_ref.shape
-    sums = pick(itself, 2 * experts, load_blocks(back_ref), expert_rows(plan, router_ref.shape[0]))
+    source = half_first(expert_rows(plan, experts), plan[0] * experts, plan[1])
+    sums = pick(itself, 2 * experts, load_blocks(back_ref), source)
     extras = sums[:experts, width:] + sums[experts:, width:]
     den = extras[:, :1] * (1.0 / (plan[0] * plan[1]))
     corr = extras[:, 1:2]
@@ -342,7 +351,7 @@
         got, w_in, w_out,
         flops=10**9,
     )
-    back = exchange(back, BOTH)
+    back = exchange(back, ("tok", "img"))
     grad_w_in = weight_grad(rows, dact)
     grad_w_out = weight_grad(hidden, grad_rows)
     sums, ys, coef, mix, signal = call(

time: 47.4 us -> 47.6 us (level)
  blocking collectives: 27.4 us -> 26.8 us
  starting transfers between devices: 8.03 us -> 8.58 us
    all_to_all x2, blocking collectives: 27.4 us -> 26.8 us  [exchange(): return lax.all_to_all(block, axes, split_axis=0, concat_axis=0, tiled=True)]
    ppermute x7, starting transfers between devices: 8.03 us -> 8.58 us  [pair(): return lax.ppermute(term, BOTH, [(d, d ^ mask) for d in range(devices)])]
  transfers between devices with their start and end apart: 7 -> 7, of which waited for: 3 -> 1; matrix products, arithmetic and copies ran while one was open for 0% -> 0% of each run, Pallas kernels for 10% -> 10%
where the time goes in v11:
time: 47.6 us; the launch traced here: 47.4 us
  blocking collectives  26.8 us (56%)
  Pallas kernels  10.8 us (23%)
  starting transfers between devices  8.58 us (18%)
  between operations  0.76 us (2%)
  waiting for transfers between devices  0.48 us (1%)
    all_to_all x2, blocking collectives, exchange(): return lax.all_to_all(block, axes, split_axis=0, concat_axis=0, tiled=True)  26.8 us
    pallas_call x7, Pallas kernels, call(): pl.pallas_call(kernel, out_shape=[jax.ShapeDtypeStruct(shape, dtype) for...  10.8 us
    ppermute x7, starting transfers between devices, pair(): return lax.ppermute(term, BOTH, [(d, d ^ mask) for d in range(devices)])  8.58 us
  transfers between devices with their start and end apart: 7, of which 1 were waited for; matrix products, arithmetic and copies ran while one was open for 0% of the time, Pallas kernels for 10%

profile of v11, /device:TPU:0, one launch (start us, length us, event | category | flops | bytes accessed | tf_op | source)
XLA Modules:
  0.0 47.4 jit_solution(20295358588611331)
XLA Ops:
  0.7 2.1 %shard_map.109 = (bf16[32,2,1408]{2,1,0:T(2,128)(2,1)S(1)}, f32[8,128]{1,0:T(8,128)S(1)}, f32[1,128]{1,0:T(1,128)S(1)}) custom-call(bf16[1,128,1280]{2,1,0:T(8,128)(2,1)} %tok_ref.3, bf16[1,128,1280]{2,1,0:T(8,128)(2,1)} %grad_ref.1, bf16[8,1280]{1,0:T(8,128)(2,1)} %bitcast.4, f32[1,8]{1,0:T(1,128)} %bitcast.6), custom_call_target="tpu_custom_call" | custom-call | flops 4000000000 | bytes 675872 | tf_op jit(solution)/shard_map/pallas_call | solution.py:272
  2.8 15.8 %all_to_all.10.got_ref = bf16[32,2,1408]{2,1,0:T(2,128)(2,1)S(1)} all-to-all(bf16[32,2,1408]{2,1,0:T(2,128)(2,1)S(1)} %get-tuple-element.30), channel_id=1, replica_groups=mesh['img'=16,'tok'=2] {'tok','img'}, dimensions={0} | all-to-all | bytes 360448 | tf_op jit(solution)/shard_map/all_to_all | solution.py:297
  18.7 0.0 copy-start.4
  18.7 0.0 copy-start.5
  18.7 2.6 %shard_map.110 = (bf16[32,2,1408]{2,1,0:T(2,128)(2,1)S(1)}, bf16[16,1280]{1,0:T(8,128)(2,1)S(1)}, bf16[16,1280]{1,0:T(8,128)(2,1)S(1)}, bf16[16,1024]{1,0:T(8,128)(2,1)S(1)}, bf16[16,1024]{1,0:T(8,128)(2,1)S(1)}) custom-call(bf16[32,2,1408]{2,1,0:T(2,128)(2,1)S(1)} %all_to_all.10.got_ref, bf16[1,1280,1024]{2,1,0:T(8,128)(2,1)S(1)} %copy-done, ...), custom_call_target="tpu_custom_call" | custom-call | flops 1000000000 | bytes 5423104 | tf_op jit(solution)/shard_map/pallas_call | solution.py:272
  21.3 10.9 %all_to_all.11.back_ref = bf16[32,2,1408]{2,1,0:T(2,128)(2,1)S(1)} all-to-all(bf16[32,2,1408]{2,1,0:T(2,128)(2,1)S(1)} %get-tuple-element.31), channel_id=1, replica_groups=mesh['img'=16,'tok'=2] {'tok','img'}, dimensions={0} | all-to-all | bytes 360448 | tf_op jit(solution)/shard_map/all_to_all | solution.py:297
  32.2 0.5 %shard_map.111 = (f32[8,1408]{1,0:T(8,128)S(1)}, bf16[8,1280]{1,0:T(8,128)(2,1)S(1)}, bf16[16,128]{1,0:T(8,128)(2,1)S(1)}, bf16[16,1280]{1,0:T(8,128)(2,1)S(1)}, f32[1,128]{1,0:T(1,128)S(1)}) custom-call(bf16[32,2,1408]{2,1,0:T(2,128)(2,1)S(1)} %all_to_all.11.back_ref, bf16[1,128,1280]{2,1,0:T(8,128)(2,1)S(1)} %copy-done.2, ...), custom_call_target="tpu_custom_call" | custom-call | flops 10000000 | bytes 860704 | tf_op jit(solution)/shard_map/pallas_call | solution.py:272
  32.8 0.6 %collective-permute-start = (f32[8,1408]{1,0:T(8,128)S(1)}, f32[8,1408]{1,0:T(8,128)S(1)}, u32[]{:S(2)}, u32[]{:S(2)}) collective-permute-start(f32[8,1408]{1,0:T(8,128)S(1)} %get-tuple-element.34), channel_id=1, source_target_pairs={{0,2},{1,3},{2,0},{3,1},{4,6},{5,7},{6,4},{7,5},{8,10},{9,11},{10,... | collective-permute-start | bytes 135176 | tf_op jit(solution)/shard_map/ppermute | solution.py:301
  33.3 1.1 %shard_map.112 = (bf16[1,128,1280]{2,1,0:T(8,128)(2,1)}, bf16[1,128,1280]{2,1,0:T(8,128)(2,1)}) custom-call(bf16[1,128,1280]{2,1,0:T(8,128)(2,1)S(1)} %copy-done.2, f32[8,128]{1,0:T(8,128)S(1)} %get-tuple-element.32.logit_ref, bf16[8,1280]{1,0:T(8,128)(2,1)S(1)} %get-tuple-element.35.outs_ref, bf16[16,128]{1,0:T(8,128)(2,1)S(1)} %get-tuple-element.36.coef_ref, ...), custom_call_target="tpu_custom_call" | custom-call | flops 10000000 | bytes 397824 | tf_op jit(solution)/shard_map/pallas_call | solution.py:272
  34.5 0.0 collective-permute-done
  34.5 0.7 %collective-permute-start.3 = (bf16[8,1408]{1,0:T(8,128)(2,1)S(1)}, bf16[8,1408]{1,0:T(8,128)(2,1)S(1)}, u32[]{:S(2)}, u32[]{:S(2)}) collective-permute-start(bf16[8,1408]{1,0:T(8,128)(2,1)S(1)} %add_convert_fusion.1), channel_id=1, source_target_pairs={{0,5},{1,4},{2,7},{3,6},{4,1},{5,0},{6,3},{7,2},{8,13},{9,12},{10,... | collective-permute-start | bytes 67592 | tf_op jit(solution)/shard_map/ppermute | solution.py:301
  35.2 1.3 %collective-permute-start.1 = (bf16[8,1408]{1,0:T(8,128)(2,1)S(1)}, bf16[8,1408]{1,0:T(8,128)(2,1)S(1)}, u32[]{:S(2)}, u32[]{:S(2)}) collective-permute-start(bf16[8,1408]{1,0:T(8,128)(2,1)S(1)} %add_convert_fusion.1), channel_id=1, source_target_pairs={{0,4},{1,5},{2,6},{3,7},{4,0},{5,1},{6,2},{7,3},{8,12},{9,13},{10,... | collective-permute-start | bytes 67592 | tf_op jit(solution)/shard_map/ppermute | solution.py:301
  36.6 1.5 %collective-permute-start.2 = (bf16[8,1408]{1,0:T(8,128)(2,1)S(1)}, bf16[8,1408]{1,0:T(8,128)(2,1)S(1)}, u32[]{:S(2)}, u32[]{:S(2)}) collective-permute-start(bf16[8,1408]{1,0:T(8,128)(2,1)S(1)} %add_convert_fusion.1), channel_id=1, source_target_pairs={{0,1},{1,0},{2,3},{3,2},{4,5},{5,4},{6,7},{7,6},{8,9},{9,8},{10,11... | collective-permute-start | bytes 67592 | tf_op jit(solution)/shard_map/ppermute | solution.py:301
  38.1 1.8 %shard_map.113 = bf16[1,1280,1024]{2,1,0:T(8,128)(2,1)} custom-call(bf16[16,1280]{1,0:T(8,128)(2,1)S(1)} %get-tuple-element.44.left_ref, bf16[16,1024]{1,0:T(8,128)(2,1)S(1)} %get-tuple-element.45.right_ref), custom_call_target="tpu_custom_call" | custom-call | flops 1000000000 | bytes 73728 | tf_op jit(solution)/shard_map/pallas_call | solution.py:272
  39.9 0.0 collective-permute-done.3
  39.9 0.0 collective-permute-done.1
  39.9 0.5 collective-permute-done.2
  40.4 1.5 %collective-permute-start.6 = (bf16[8,1408]{1,0:T(8,128)(2,1)S(1)}, bf16[8,1408]{1,0:T(8,128)(2,1)S(1)}, u32[]{:S(2)}, u32[]{:S(2)}) collective-permute-start(bf16[8,1408]{1,0:T(8,128)(2,1)S(1)} %add_convert_fusion.own_ref), channel_id=1, source_target_pairs={{0,24},{1,25},{2,26},{3,27},{4,28},{5,29},{6,30},{7,31},{8,16},{9,... | collective-permute-start | bytes 67592 | tf_op jit(solution)/shard_map/ppermute | solution.py:301
  41.9 0.7 %collective-permute-start.4 = (bf16[8,1408]{1,0:T(8,128)(2,1)S(1)}, bf16[8,1408]{1,0:T(8,128)(2,1)S(1)}, u32[]{:S(2)}, u32[]{:S(2)}) collective-permute-start(bf16[8,1408]{1,0:T(8,128)(2,1)S(1)} %add_convert_fusion.own_ref), channel_id=1, source_target_pairs={{0,16},{1,17},{2,18},{3,19},{4,20},{5,21},{6,22},{7,23},{8,24},{9,... | collective-permute-start | bytes 67592 | tf_op jit(solution)/shard_map/ppermute | solution.py:301
  42.5 2.3 %collective-permute-start.5 = (bf16[8,1408]{1,0:T(8,128)(2,1)S(1)}, bf16[8,1408]{1,0:T(8,128)(2,1)S(1)}, u32[]{:S(2)}, u32[]{:S(2)}) collective-permute-start(bf16[8,1408]{1,0:T(8,128)(2,1)S(1)} %add_convert_fusion.own_ref), channel_id=1, source_target_pairs={{0,8},{1,9},{2,10},{3,11},{4,12},{5,13},{6,14},{7,15},{8,0},{9,1},... | collective-permute-start | bytes 67592 | tf_op jit(solution)/shard_map/ppermute | solution.py:301
  44.9 1.9 %shard_map.114 = bf16[1,1024,1280]{2,1,0:T(8,128)(2,1)} custom-call(bf16[16,1024]{1,0:T(8,128)(2,1)S(1)} %get-tuple-element.47.left_ref, bf16[16,1280]{1,0:T(8,128)(2,1)S(1)} %get-tuple-element.48.right_ref), custom_call_target="tpu_custom_call" | custom-call | flops 1000000000 | bytes 73728 | tf_op jit(solution)/shard_map/pallas_call | solution.py:272
  46.8 0.0 collective-permute-done.6.refs_1_
  46.8 0.0 collective-permute-done.5.refs_0_
  46.8 0.6 %shard_map.115 = (f32[8,1280]{1,0:T(8,128)}, f32[1,8]{1,0:T(1,128)}) custom-call(bf16[8,1408]{1,0:T(8,128)(2,1)S(1)} %add_convert_fusion.own_ref, bf16[8,1408]{1,0:T(8,128)(2,1)S(1)} %collective-permute-done.4.other_ref, bf16[8,1408]{1,0:T(8,128)(2,1)S(1)} %collective-permute-done.5.refs_0_, bf16[8,1408]{1,0:T(8,128)(2,1)S(1)} %collective-permute-done.6.refs_1_), custom_call_target="tpu_custom_call" | custom-call | flops 10000000 | bytes 90112 | tf_op jit(solution)/shard_map/pallas_call | solution.py:272
  (13 shorter events, 0.0 us)
Async XLA Ops:
  0.6 18.0 %copy-start = (bf16[1,1280,1024]{2,1,0:T(8,128)(2,1)S(1)}, bf16[1,1280,1024]{2,1,0:T(8,128)(2,1)}, u32[]{:S(2)}) copy-start(bf16[1,1280,1024]{2,1,0:T(8,128)(2,1)} %one_ref.1) | copy-start | bytes 7864324
  0.6 18.0 %copy-start.1 = (bf16[1,1024,1280]{2,1,0:T(8,128)(2,1)S(1)}, bf16[1,1024,1280]{2,1,0:T(8,128)(2,1)}, u32[]{:S(2)}) copy-start(bf16[1,1024,1280]{2,1,0:T(8,128)(2,1)} %two_ref.1) | copy-start | bytes 7864324
  18.6 13.6 %copy-start.2 = (bf16[1,128,1280]{2,1,0:T(8,128)(2,1)S(1)}, bf16[1,128,1280]{2,1,0:T(8,128)(2,1)}, u32[]{:S(2)}) copy-start(bf16[1,128,1280]{2,1,0:T(8,128)(2,1)} %tok_ref.3) | copy-start | bytes 983044
  18.6 13.6 %copy-start.3 = (bf16[1,128,1280]{2,1,0:T(8,128)(2,1)S(1)}, bf16[1,128,1280]{2,1,0:T(8,128)(2,1)}, u32[]{:S(2)}) copy-start(bf16[1,128,1280]{2,1,0:T(8,128)(2,1)} %grad_ref.1) | copy-start | bytes 983044
  18.7 13.6 %copy-start.4 = (bf16[1280,8]{0,1:T(8,128)(2,1)S(1)}, bf16[1280,8]{0,1:T(8,128)(2,1)}, u32[]{:S(2)}) copy-start(bf16[1280,8]{0,1:T(8,128)(2,1)} %param.8) | copy-start | bytes 61444
  18.7 13.6 %copy-start.5 = (f32[8]{0:T(128)S(1)}, f32[8]{0:T(128)}, u32[]{:S(2)}) copy-start(f32[8]{0:T(128)} %param.9) | copy-start | bytes 100
  32.8 1.7 %collective-permute-start = (f32[8,1408]{1,0:T(8,128)S(1)}, f32[8,1408]{1,0:T(8,128)S(1)}, u32[]{:S(2)}, u32[]{:S(2)}) collective-permute-start(f32[8,1408]{1,0:T(8,128)S(1)} %get-tuple-element.34), channel_id=1, source_target_pairs={{0,2},{1,3},{2,0},{3,1},{4,6},{5,7},{6,4},{7,5},{8,10},{9,11},{10,... | collective-permute-start | bytes 135176 | tf_op jit(solution)/shard_map/ppermute | solution.py:301
  34.5 5.4 %collective-permute-start.3 = (bf16[8,1408]{1,0:T(8,128)(2,1)S(1)}, bf16[8,1408]{1,0:T(8,128)(2,1)S(1)}, u32[]{:S(2)}, u32[]{:S(2)}) collective-permute-start(bf16[8,1408]{1,0:T(8,128)(2,1)S(1)} %add_convert_fusion.1), channel_id=1, source_target_pairs={{0,5},{1,4},{2,7},{3,6},{4,1},{5,0},{6,3},{7,2},{8,13},{9,12},{10,... | collective-permute-start | bytes 67592 | tf_op jit(solution)/shard_map/ppermute | solution.py:301
  35.2 4.7 %collective-permute-start.1 = (bf16[8,1408]{1,0:T(8,128)(2,1)S(1)}, bf16[8,1408]{1,0:T(8,128)(2,1)S(1)}, u32[]{:S(2)}, u32[]{:S(2)}) collective-permute-start(bf16[8,1408]{1,0:T(8,128)(2,1)S(1)} %add_convert_fusion.1), channel_id=1, source_target_pairs={{0,4},{1,5},{2,6},{3,7},{4,0},{5,1},{6,2},{7,3},{8,12},{9,13},{10,... | collective-permute-start | bytes 67592 | tf_op jit(solution)/shard_map/ppermute | solution.py:301
  36.6 3.8 %collective-permute-start.2 = (bf16[8,1408]{1,0:T(8,128)(2,1)S(1)}, bf16[8,1408]{1,0:T(8,128)(2,1)S(1)}, u32[]{:S(2)}, u32[]{:S(2)}) collective-permute-start(bf16[8,1408]{1,0:T(8,128)(2,1)S(1)} %add_convert_fusion.1), channel_id=1, source_target_pairs={{0,1},{1,0},{2,3},{3,2},{4,5},{5,4},{6,7},{7,6},{8,9},{9,8},{10,11... | collective-permute-start | bytes 67592 | tf_op jit(solution)/shard_map/ppermute | solution.py:301
  40.4 6.4 %collective-permute-start.6 = (bf16[8,1408]{1,0:T(8,128)(2,1)S(1)}, bf16[8,1408]{1,0:T(8,128)(2,1)S(1)}, u32[]{:S(2)}, u32[]{:S(2)}) collective-permute-start(bf16[8,1408]{1,0:T(8,128)(2,1)S(1)} %add_convert_fusion.own_ref), channel_id=1, source_target_pairs={{0,24},{1,25},{2,26},{3,27},{4,28},{5,29},{6,30},{7,31},{8,16},{9,... | collective-permute-start | bytes 67592 | tf_op jit(solution)/shard_map/ppermute | solution.py:301
  41.9 4.9 %collective-permute-start.4 = (bf16[8,1408]{1,0:T(8,128)(2,1)S(1)}, bf16[8,1408]{1,0:T(8,128)(2,1)S(1)}, u32[]{:S(2)}, u32[]{:S(2)}) collective-permute-start(bf16[8,1408]{1,0:T(8,128)(2,1)S(1)} %add_convert_fusion.own_ref), channel_id=1, source_target_pairs={{0,16},{1,17},{2,18},{3,19},{4,20},{5,21},{6,22},{7,23},{8,24},{9,... | collective-permute-start | bytes 67592 | tf_op jit(solution)/shard_map/ppermute | solution.py:301
  42.5 4.3 %collective-permute-start.5 = (bf16[8,1408]{1,0:T(8,128)(2,1)S(1)}, bf16[8,1408]{1,0:T(8,128)(2,1)S(1)}, u32[]{:S(2)}, u32[]{:S(2)}) collective-permute-start(bf16[8,1408]{1,0:T(8,128)(2,1)S(1)} %add_convert_fusion.own_ref), channel_id=1, source_target_pairs={{0,8},{1,9},{2,10},{3,11},{4,12},{5,13},{6,14},{7,15},{8,0},{9,1},... | collective-permute-start | bytes 67592 | tf_op jit(solution)/shard_map/ppermute | solution.py:301

commit v12 on v9

--- a/solution.py
+++ b/solution.py
@@ -165,8 +165,8 @@
     images, halves, got_ref, one_ref, two_ref, back_ref, rows_ref, grad_rows_ref, hidden_ref, dact_ref
 ):
     width = one_ref.shape[1]
-    key = image_rows(images, halves)
-    sums = pick(itself, 2 * images, load_blocks(got_ref), half_first(key, images, halves))
+    key = half_first(image_rows(images, halves), images, halves)
+    sums = pick(itself, 2 * images, load_blocks(got_ref), key)
     den = sums[:images, width : width + 1] + sums[images:, width : width + 1]
     rows = (sums[:images, :width] / den).astype(BF)
     grad_rows = sums[images:, :width].astype(BF)
@@ -206,7 +206,8 @@
     sums_ref, outs_ref, coef_ref, mix_ref, signal_ref,
 ):
     experts, width = router_ref.shape
-    sums = pick(itself, 2 * experts, load_blocks(back_ref), expert_rows(plan, router_ref.shape[0]))
+    source = half_first(expert_rows(plan, experts), plan[0] * experts, plan[1])
+    sums = pick(itself, 2 * experts, load_blocks(back_ref), source)
     extras = sums[:experts, width:] + sums[experts:, width:]
     den = extras[:, :1] * (1.0 / (plan[0] * plan[1]))
     corr = extras[:, 1:2]
@@ -342,7 +343,7 @@
         got, w_in, w_out,
         flops=10**9,
     )
-    back = exchange(back, BOTH)
+    back = exchange(back, ("tok", "img"))
     grad_w_in = weight_grad(rows, dact)
     grad_w_out = weight_grad(hidden, grad_rows)
     sums, ys, coef, mix, signal = call(

time: 47.4 us -> 47.4 us (level)
  blocking collectives: 27.4 us -> 26.8 us
  starting transfers between devices: 8.03 us -> 8.58 us
    all_to_all x2, blocking collectives: 27.4 us -> 26.8 us  [exchange(): return lax.all_to_all(block, axes, split_axis=0, concat_axis=0, tiled=True)]
    ppermute x7, starting transfers between devices: 8.03 us -> 8.58 us  [pair(): return lax.ppermute(term, BOTH, [(d, d ^ mask) for d in range(devices)])]
  transfers between devices with their start and end apart: 7 -> 7, of which waited for: 3 -> 1; matrix products, arithmetic and copies ran while one was open for 0% -> 0% of each run, Pallas kernels for 10% -> 10%
where the time goes in v12:
time: 47.4 us; the launch traced here: 47.2 us
  blocking collectives  26.8 us (57%)
  Pallas kernels  10.6 us (22%)
  starting transfers between devices  8.58 us (18%)
  between operations  0.76 us (2%)
  waiting for transfers between devices  0.49 us (1%)
    all_to_all x2, blocking collectives, exchange(): return lax.all_to_all(block, axes, split_axis=0, concat_axis=0, tiled=True)  26.8 us
    pallas_call x7, Pallas kernels, call(): pl.pallas_call(kernel, out_shape=[jax.ShapeDtypeStruct(shape, dtype) for...  10.6 us
    ppermute x7, starting transfers between devices, pair(): return lax.ppermute(term, BOTH, [(d, d ^ mask) for d in range(devices)])  8.58 us
  transfers between devices with their start and end apart: 7, of which 1 were waited for; matrix products, arithmetic and copies ran while one was open for 0% of the time, Pallas kernels for 10%

profile of v12, /device:TPU:0, one launch (start us, length us, event | category | flops | bytes accessed | tf_op | source)
XLA Modules:
  0.0 47.2 jit_solution(12319891295624901295)
XLA Ops:
  0.7 2.0 %shard_map.109 = (bf16[32,2,1408]{2,1,0:T(2,128)(2,1)S(1)}, f32[8,128]{1,0:T(8,128)S(1)}, f32[1,128]{1,0:T(1,128)S(1)}) custom-call(bf16[1,128,1280]{2,1,0:T(8,128)(2,1)} %tok_ref.3, bf16[1,128,1280]{2,1,0:T(8,128)(2,1)} %grad_ref.1, bf16[8,1280]{1,0:T(8,128)(2,1)} %bitcast.4, f32[1,8]{1,0:T(1,128)} %bitcast.6), custom_call_target="tpu_custom_call" | custom-call | flops 4000000000 | bytes 675872 | tf_op jit(solution)/shard_map/pallas_call | solution.py:264
  2.6 15.8 %all_to_all.10.got_ref = bf16[32,2,1408]{2,1,0:T(2,128)(2,1)S(1)} all-to-all(bf16[32,2,1408]{2,1,0:T(2,128)(2,1)S(1)} %get-tuple-element.30), channel_id=1, replica_groups=mesh['img'=16,'tok'=2] {'tok','img'}, dimensions={0} | all-to-all | bytes 360448 | tf_op jit(solution)/shard_map/all_to_all | solution.py:289
  18.5 0.0 copy-start.4
  18.5 0.0 copy-start.5
  18.5 2.6 %shard_map.110 = (bf16[32,2,1408]{2,1,0:T(2,128)(2,1)S(1)}, bf16[16,1280]{1,0:T(8,128)(2,1)S(1)}, bf16[16,1280]{1,0:T(8,128)(2,1)S(1)}, bf16[16,1024]{1,0:T(8,128)(2,1)S(1)}, bf16[16,1024]{1,0:T(8,128)(2,1)S(1)}) custom-call(bf16[32,2,1408]{2,1,0:T(2,128)(2,1)S(1)} %all_to_all.10.got_ref, bf16[1,1280,1024]{2,1,0:T(8,128)(2,1)S(1)} %copy-done, ...), custom_call_target="tpu_custom_call" | custom-call | flops 1000000000 | bytes 5423104 | tf_op jit(solution)/shard_map/pallas_call | solution.py:264
  21.1 10.9 %all_to_all.11.back_ref = bf16[32,2,1408]{2,1,0:T(2,128)(2,1)S(1)} all-to-all(bf16[32,2,1408]{2,1,0:T(2,128)(2,1)S(1)} %get-tuple-element.31), channel_id=1, replica_groups=mesh['img'=16,'tok'=2] {'tok','img'}, dimensions={0} | all-to-all | bytes 360448 | tf_op jit(solution)/shard_map/all_to_all | solution.py:289
  32.0 0.5 %shard_map.111 = (f32[8,1408]{1,0:T(8,128)S(1)}, bf16[8,1280]{1,0:T(8,128)(2,1)S(1)}, bf16[16,128]{1,0:T(8,128)(2,1)S(1)}, bf16[16,1280]{1,0:T(8,128)(2,1)S(1)}, f32[1,128]{1,0:T(1,128)S(1)}) custom-call(bf16[32,2,1408]{2,1,0:T(2,128)(2,1)S(1)} %all_to_all.11.back_ref, bf16[1,128,1280]{2,1,0:T(8,128)(2,1)S(1)} %copy-done.2, ...), custom_call_target="tpu_custom_call" | custom-call | flops 10000000 | bytes 860704 | tf_op jit(solution)/shard_map/pallas_call | solution.py:264
  32.6 0.6 %collective-permute-start = (f32[8,1408]{1,0:T(8,128)S(1)}, f32[8,1408]{1,0:T(8,128)S(1)}, u32[]{:S(2)}, u32[]{:S(2)}) collective-permute-start(f32[8,1408]{1,0:T(8,128)S(1)} %get-tuple-element.34), channel_id=1, source_target_pairs={{0,2},{1,3},{2,0},{3,1},{4,6},{5,7},{6,4},{7,5},{8,10},{9,11},{10,... | collective-permute-start | bytes 135176 | tf_op jit(solution)/shard_map/ppermute | solution.py:293
  33.1 1.1 %shard_map.112 = (bf16[1,128,1280]{2,1,0:T(8,128)(2,1)}, bf16[1,128,1280]{2,1,0:T(8,128)(2,1)}) custom-call(bf16[1,128,1280]{2,1,0:T(8,128)(2,1)S(1)} %copy-done.2, f32[8,128]{1,0:T(8,128)S(1)} %get-tuple-element.32.logit_ref, bf16[8,1280]{1,0:T(8,128)(2,1)S(1)} %get-tuple-element.35.outs_ref, bf16[16,128]{1,0:T(8,128)(2,1)S(1)} %get-tuple-element.36.coef_ref, ...), custom_call_target="tpu_custom_call" | custom-call | flops 10000000 | bytes 397824 | tf_op jit(solution)/shard_map/pallas_call | solution.py:264
  34.3 0.0 collective-permute-done
  34.3 0.7 %collective-permute-start.3 = (bf16[8,1408]{1,0:T(8,128)(2,1)S(1)}, bf16[8,1408]{1,0:T(8,128)(2,1)S(1)}, u32[]{:S(2)}, u32[]{:S(2)}) collective-permute-start(bf16[8,1408]{1,0:T(8,128)(2,1)S(1)} %add_convert_fusion.1), channel_id=1, source_target_pairs={{0,5},{1,4},{2,7},{3,6},{4,1},{5,0},{6,3},{7,2},{8,13},{9,12},{10,... | collective-permute-start | bytes 67592 | tf_op jit(solution)/shard_map/ppermute | solution.py:293
  35.0 1.3 %collective-permute-start.1 = (bf16[8,1408]{1,0:T(8,128)(2,1)S(1)}, bf16[8,1408]{1,0:T(8,128)(2,1)S(1)}, u32[]{:S(2)}, u32[]{:S(2)}) collective-permute-start(bf16[8,1408]{1,0:T(8,128)(2,1)S(1)} %add_convert_fusion.1), channel_id=1, source_target_pairs={{0,4},{1,5},{2,6},{3,7},{4,0},{5,1},{6,2},{7,3},{8,12},{9,13},{10,... | collective-permute-start | bytes 67592 | tf_op jit(solution)/shard_map/ppermute | solution.py:293
  36.4 1.5 %collective-permute-start.2 = (bf16[8,1408]{1,0:T(8,128)(2,1)S(1)}, bf16[8,1408]{1,0:T(8,128)(2,1)S(1)}, u32[]{:S(2)}, u32[]{:S(2)}) collective-permute-start(bf16[8,1408]{1,0:T(8,128)(2,1)S(1)} %add_convert_fusion.1), channel_id=1, source_target_pairs={{0,1},{1,0},{2,3},{3,2},{4,5},{5,4},{6,7},{7,6},{8,9},{9,8},{10,11... | collective-permute-start | bytes 67592 | tf_op jit(solution)/shard_map/ppermute | solution.py:293
  37.9 1.8 %shard_map.113 = bf16[1,1280,1024]{2,1,0:T(8,128)(2,1)} custom-call(bf16[16,1280]{1,0:T(8,128)(2,1)S(1)} %get-tuple-element.44.left_ref, bf16[16,1024]{1,0:T(8,128)(2,1)S(1)} %get-tuple-element.45.right_ref), custom_call_target="tpu_custom_call" | custom-call | flops 1000000000 | bytes 73728 | tf_op jit(solution)/shard_map/pallas_call | solution.py:264
  39.7 0.0 collective-permute-done.3
  39.7 0.0 collective-permute-done.1
  39.7 0.5 collective-permute-done.2
  40.2 1.5 %collective-permute-start.6 = (bf16[8,1408]{1,0:T(8,128)(2,1)S(1)}, bf16[8,1408]{1,0:T(8,128)(2,1)S(1)}, u32[]{:S(2)}, u32[]{:S(2)}) collective-permute-start(bf16[8,1408]{1,0:T(8,128)(2,1)S(1)} %add_convert_fusion.own_ref), channel_id=1, source_target_pairs={{0,24},{1,25},{2,26},{3,27},{4,28},{5,29},{6,30},{7,31},{8,16},{9,... | collective-permute-start | bytes 67592 | tf_op jit(solution)/shard_map/ppermute | solution.py:293
  41.7 0.7 %collective-permute-start.4 = (bf16[8,1408]{1,0:T(8,128)(2,1)S(1)}, bf16[8,1408]{1,0:T(8,128)(2,1)S(1)}, u32[]{:S(2)}, u32[]{:S(2)}) collective-permute-start(bf16[8,1408]{1,0:T(8,128)(2,1)S(1)} %add_convert_fusion.own_ref), channel_id=1, source_target_pairs={{0,16},{1,17},{2,18},{3,19},{4,20},{5,21},{6,22},{7,23},{8,24},{9,... | collective-permute-start | bytes 67592 | tf_op jit(solution)/shard_map/ppermute | solution.py:293
  42.3 2.3 %collective-permute-start.5 = (bf16[8,1408]{1,0:T(8,128)(2,1)S(1)}, bf16[8,1408]{1,0:T(8,128)(2,1)S(1)}, u32[]{:S(2)}, u32[]{:S(2)}) collective-permute-start(bf16[8,1408]{1,0:T(8,128)(2,1)S(1)} %add_convert_fusion.own_ref), channel_id=1, source_target_pairs={{0,8},{1,9},{2,10},{3,11},{4,12},{5,13},{6,14},{7,15},{8,0},{9,1},... | collective-permute-start | bytes 67592 | tf_op jit(solution)/shard_map/ppermute | solution.py:293
  44.7 1.9 %shard_map.114 = bf16[1,1024,1280]{2,1,0:T(8,128)(2,1)} custom-call(bf16[16,1024]{1,0:T(8,128)(2,1)S(1)} %get-tuple-element.47.left_ref, bf16[16,1280]{1,0:T(8,128)(2,1)S(1)} %get-tuple-element.48.right_ref), custom_call_target="tpu_custom_call" | custom-call | flops 1000000000 | bytes 73728 | tf_op jit(solution)/shard_map/pallas_call | solution.py:264
  46.6 0.0 collective-permute-done.4.other_ref
  46.6 0.0 collective-permute-done.5.refs_0_
  46.6 0.6 %shard_map.115 = (f32[8,1280]{1,0:T(8,128)}, f32[1,8]{1,0:T(1,128)}) custom-call(bf16[8,1408]{1,0:T(8,128)(2,1)S(1)} %add_convert_fusion.own_ref, bf16[8,1408]{1,0:T(8,128)(2,1)S(1)} %collective-permute-done.4.other_ref, bf16[8,1408]{1,0:T(8,128)(2,1)S(1)} %collective-permute-done.5.refs_0_, bf16[8,1408]{1,0:T(8,128)(2,1)S(1)} %collective-permute-done.6.refs_1_), custom_call_target="tpu_custom_call" | custom-call | flops 10000000 | bytes 90112 | tf_op jit(solution)/shard_map/pallas_call | solution.py:264
  (13 shorter events, 0.0 us)
Async XLA Ops:
  0.6 17.8 %copy-start = (bf16[1,1280,1024]{2,1,0:T(8,128)(2,1)S(1)}, bf16[1,1280,1024]{2,1,0:T(8,128)(2,1)}, u32[]{:S(2)}) copy-start(bf16[1,1280,1024]{2,1,0:T(8,128)(2,1)} %one_ref.1) | copy-start | bytes 7864324
  0.6 17.8 %copy-start.1 = (bf16[1,1024,1280]{2,1,0:T(8,128)(2,1)S(1)}, bf16[1,1024,1280]{2,1,0:T(8,128)(2,1)}, u32[]{:S(2)}) copy-start(bf16[1,1024,1280]{2,1,0:T(8,128)(2,1)} %two_ref.1) | copy-start | bytes 7864324
  18.5 13.5 %copy-start.2 = (bf16[1,128,1280]{2,1,0:T(8,128)(2,1)S(1)}, bf16[1,128,1280]{2,1,0:T(8,128)(2,1)}, u32[]{:S(2)}) copy-start(bf16[1,128,1280]{2,1,0:T(8,128)(2,1)} %tok_ref.3) | copy-start | bytes 983044
  18.5 13.5 %copy-start.3 = (bf16[1,128,1280]{2,1,0:T(8,128)(2,1)S(1)}, bf16[1,128,1280]{2,1,0:T(8,128)(2,1)}, u32[]{:S(2)}) copy-start(bf16[1,128,1280]{2,1,0:T(8,128)(2,1)} %grad_ref.1) | copy-start | bytes 983044
  18.5 13.5 %copy-start.4 = (bf16[1280,8]{0,1:T(8,128)(2,1)S(1)}, bf16[1280,8]{0,1:T(8,128)(2,1)}, u32[]{:S(2)}) copy-start(bf16[1280,8]{0,1:T(8,128)(2,1)} %param.8) | copy-start | bytes 61444
  18.5 13.5 %copy-start.5 = (f32[8]{0:T(128)S(1)}, f32[8]{0:T(128)}, u32[]{:S(2)}) copy-start(f32[8]{0:T(128)} %param.9) | copy-start | bytes 100
  32.6 1.7 %collective-permute-start = (f32[8,1408]{1,0:T(8,128)S(1)}, f32[8,1408]{1,0:T(8,128)S(1)}, u32[]{:S(2)}, u32[]{:S(2)}) collective-permute-start(f32[8,1408]{1,0:T(8,128)S(1)} %get-tuple-element.34), channel_id=1, source_target_pairs={{0,2},{1,3},{2,0},{3,1},{4,6},{5,7},{6,4},{7,5},{8,10},{9,11},{10,... | collective-permute-start | bytes 135176 | tf_op jit(solution)/shard_map/ppermute | solution.py:293
  34.3 5.4 %collective-permute-start.3 = (bf16[8,1408]{1,0:T(8,128)(2,1)S(1)}, bf16[8,1408]{1,0:T(8,128)(2,1)S(1)}, u32[]{:S(2)}, u32[]{:S(2)}) collective-permute-start(bf16[8,1408]{1,0:T(8,128)(2,1)S(1)} %add_convert_fusion.1), channel_id=1, source_target_pairs={{0,5},{1,4},{2,7},{3,6},{4,1},{5,0},{6,3},{7,2},{8,13},{9,12},{10,... | collective-permute-start | bytes 67592 | tf_op jit(solution)/shard_map/ppermute | solution.py:293
  35.0 4.7 %collective-permute-start.1 = (bf16[8,1408]{1,0:T(8,128)(2,1)S(1)}, bf16[8,1408]{1,0:T(8,128)(2,1)S(1)}, u32[]{:S(2)}, u32[]{:S(2)}) collective-permute-start(bf16[8,1408]{1,0:T(8,128)(2,1)S(1)} %add_convert_fusion.1), channel_id=1, source_target_pairs={{0,4},{1,5},{2,6},{3,7},{4,0},{5,1},{6,2},{7,3},{8,12},{9,13},{10,... | collective-permute-start | bytes 67592 | tf_op jit(solution)/shard_map/ppermute | solution.py:293
  36.4 3.8 %collective-permute-start.2 = (bf16[8,1408]{1,0:T(8,128)(2,1)S(1)}, bf16[8,1408]{1,0:T(8,128)(2,1)S(1)}, u32[]{:S(2)}, u32[]{:S(2)}) collective-permute-start(bf16[8,1408]{1,0:T(8,128)(2,1)S(1)} %add_convert_fusion.1), channel_id=1, source_target_pairs={{0,1},{1,0},{2,3},{3,2},{4,5},{5,4},{6,7},{7,6},{8,9},{9,8},{10,11... | collective-permute-start | bytes 67592 | tf_op jit(solution)/shard_map/ppermute | solution.py:293
  40.2 6.4 %collective-permute-start.6 = (bf16[8,1408]{1,0:T(8,128)(2,1)S(1)}, bf16[8,1408]{1,0:T(8,128)(2,1)S(1)}, u32[]{:S(2)}, u32[]{:S(2)}) collective-permute-start(bf16[8,1408]{1,0:T(8,128)(2,1)S(1)} %add_convert_fusion.own_ref), channel_id=1, source_target_pairs={{0,24},{1,25},{2,26},{3,27},{4,28},{5,29},{6,30},{7,31},{8,16},{9,... | collective-permute-start | bytes 67592 | tf_op jit(solution)/shard_map/ppermute | solution.py:293
  41.7 4.9 %collective-permute-start.4 = (bf16[8,1408]{1,0:T(8,128)(2,1)S(1)}, bf16[8,1408]{1,0:T(8,128)(2,1)S(1)}, u32[]{:S(2)}, u32[]{:S(2)}) collective-permute-start(bf16[8,1408]{1,0:T(8,128)(2,1)S(1)} %add_convert_fusion.own_ref), channel_id=1, source_target_pairs={{0,16},{1,17},{2,18},{3,19},{4,20},{5,21},{6,22},{7,23},{8,24},{9,... | collective-permute-start | bytes 67592 | tf_op jit(solution)/shard_map/ppermute | solution.py:293
  42.3 4.3 %collective-permute-start.5 = (bf16[8,1408]{1,0:T(8,128)(2,1)S(1)}, bf16[8,1408]{1,0:T(8,128)(2,1)S(1)}, u32[]{:S(2)}, u32[]{:S(2)}) collective-permute-start(bf16[8,1408]{1,0:T(8,128)(2,1)S(1)} %add_convert_fusion.own_ref), channel_id=1, source_target_pairs={{0,8},{1,9},{2,10},{3,11},{4,12},{5,13},{6,14},{7,15},{8,0},{9,1},... | collective-permute-start | bytes 67592 | tf_op jit(solution)/shard_map/ppermute | solution.py:293

commit v13 on v12

--- a/solution.py
+++ b/solution.py
@@ -243,11 +243,8 @@
     grads_ref[0] = (grads - column * tok_ref[0].astype(F32)).astype(BF)
 
 
-def last_kernel(own_ref, other_ref, *refs):
-    *more, router_ref, scale_ref = refs
-    sums = own_ref[...].astype(F32) + other_ref[...].astype(F32)
-    if more:
-        sums = sums + (more[0][...].astype(F32) + more[1][...].astype(F32))
+def last_kernel(mine_ref, other_ref, router_ref, scale_ref):
+    sums = mine_ref[...] + other_ref[...]
     experts, width = router_ref.shape
     router_ref[...] = sums[:, :width]
     eye = iota((experts, experts), 0) == iota((experts, experts), 1)
@@ -294,6 +291,8 @@
 
 
 def sum_everywhere(term, devices, beside):
+    masks = [1] + [1 << place for place in range(2, log2(devices))]
+    rounds = [masks[place : place + 2] for place in range(0, len(masks), 2)]
     done = []
 
     def together(value):
@@ -302,19 +301,17 @@
             done.append(ready)
         return value
 
-    term = term + together(pair(term, 2, devices))
-    masks = [1] + [1 << place for place in range(2, log2(devices))]
-    rounds = [masks[place : place + 2] for place in range(0, len(masks), 2)]
     for group in rounds:
-        if group is not rounds[0]:
-            term = (terms[0].astype(F32) + terms[1].astype(F32)) + (
-                terms[2].astype(F32) + terms[3].astype(F32)
-            )
         own = term.astype(BF)
         steps = [group[1], group[0], group[0] ^ group[1]] if len(group) == 2 else group
         terms = [own] + [pair(own, mask, devices) for mask in steps]
         terms[-1] = together(terms[-1])
-    return terms, done + beside[len(done) :]
+        terms = [value.astype(F32) for value in terms]
+        term = terms[0] + terms[1]
+        if len(terms) == 4:
+            term = term + (terms[2] + terms[3])
+    other = together(pair(term, 2, devices))
+    return term, other, done + beside[len(done) :]
 
 
 def shards(images, halves, tokens, grad_out, router, slot_scale, w_in, w_out):
@@ -357,11 +354,11 @@
         [(tokens.shape, BF), (tokens.shape, BF)],
         tokens, logit, ys, coef, mix, signal,
     )
-    terms, ((combined, grad_tokens), grad_w_in, grad_w_out) = sum_everywhere(
-        sums, devices, [(combined, grad_tokens), grad_w_in, grad_w_out]
+    mine, other, (grad_w_in, grad_w_out, (combined, grad_tokens)) = sum_everywhere(
+        sums, devices, [grad_w_in, grad_w_out, (combined, grad_tokens)]
     )
     grad_router, grad_scale = call(
-        last_kernel, [((experts, width), F32), ((1, experts), F32)], *terms
+        last_kernel, [((experts, width), F32), ((1, experts), F32)], mine, other
     )
     return (combined, grad_tokens, grad_router.T, grad_scale[0], grad_w_in, grad_w_out)
 

time: 47.4 us -> 47.5 us (level)
  waiting for transfers between devices: 0.49 us -> 1.03 us
  starting transfers between devices: 8.58 us -> 8.08 us
    ppermute x7, waiting for transfers between devices: 0.49 us -> 1.03 us  [pair(): return lax.ppermute(term, BOTH, [(d, d ^ mask) for d in range(devices)])]
    ppermute x7, starting transfers between devices: 8.58 us -> 8.08 us  [pair(): return lax.ppermute(term, BOTH, [(d, d ^ mask) for d in range(devices)])]
  transfers between devices with their start and end apart: 7 -> 7, of which waited for: 1 -> 2; matrix products, arithmetic and copies ran while one was open for 0% -> 0% of each run, Pallas kernels for 10% -> 10%
where the time goes in v13:
time: 47.5 us; the launch traced here: 47.3 us
  blocking collectives  26.8 us (56%)
  Pallas kernels  10.6 us (22%)
  starting transfers between devices  8.08 us (17%)
  waiting for transfers between devices  1.03 us (2%)
  between operations  0.77 us (2%)
    all_to_all x2, blocking collectives, exchange(): return lax.all_to_all(block, axes, split_axis=0, concat_axis=0, tiled=True)  26.8 us
    pallas_call x7, Pallas kernels, call(): pl.pallas_call(kernel, out_shape=[jax.ShapeDtypeStruct(shape, dtype) for...  10.6 us
    ppermute x7, starting transfers between devices, pair(): return lax.ppermute(term, BOTH, [(d, d ^ mask) for d in range(devices)])  8.08 us
    ppermute x7, waiting for transfers between devices, pair(): return lax.ppermute(term, BOTH, [(d, d ^ mask) for d in range(devices)])  1.03 us
  transfers between devices with their start and end apart: 7, of which 2 were waited for; matrix products, arithmetic and copies ran while one was open for 0% of the time, Pallas kernels for 10%

profile of v13, /device:TPU:0, one launch (start us, length us, event | category | flops | bytes accessed | tf_op | source)
XLA Modules:
  0.0 47.3 jit_solution(8397179406466769122)
XLA Ops:
  0.7 2.0 %shard_map.109 = (bf16[32,2,1408]{2,1,0:T(2,128)(2,1)S(1)}, f32[8,128]{1,0:T(8,128)S(1)}, f32[1,128]{1,0:T(1,128)S(1)}) custom-call(bf16[1,128,1280]{2,1,0:T(8,128)(2,1)} %tok_ref.3, bf16[1,128,1280]{2,1,0:T(8,128)(2,1)} %grad_ref.1, bf16[8,1280]{1,0:T(8,128)(2,1)} %bitcast.4, f32[1,8]{1,0:T(1,128)} %bitcast.6), custom_call_target="tpu_custom_call" | custom-call | flops 4000000000 | bytes 675872 | tf_op jit(solution)/shard_map/pallas_call | solution.py:261
  2.6 15.8 %all_to_all.10.got_ref = bf16[32,2,1408]{2,1,0:T(2,128)(2,1)S(1)} all-to-all(bf16[32,2,1408]{2,1,0:T(2,128)(2,1)S(1)} %get-tuple-element.30), channel_id=1, replica_groups=mesh['img'=16,'tok'=2] {'tok','img'}, dimensions={0} | all-to-all | bytes 360448 | tf_op jit(solution)/shard_map/all_to_all | solution.py:286
  18.5 0.0 copy-start.4
  18.5 0.0 copy-start.5
  18.5 2.6 %shard_map.110 = (bf16[32,2,1408]{2,1,0:T(2,128)(2,1)S(1)}, bf16[16,1280]{1,0:T(8,128)(2,1)S(1)}, bf16[16,1280]{1,0:T(8,128)(2,1)S(1)}, bf16[16,1024]{1,0:T(8,128)(2,1)S(1)}, bf16[16,1024]{1,0:T(8,128)(2,1)S(1)}) custom-call(bf16[32,2,1408]{2,1,0:T(2,128)(2,1)S(1)} %all_to_all.10.got_ref, bf16[1,1280,1024]{2,1,0:T(8,128)(2,1)S(1)} %copy-done, ...), custom_call_target="tpu_custom_call" | custom-call | flops 1000000000 | bytes 5423104 | tf_op jit(solution)/shard_map/pallas_call | solution.py:261
  21.1 10.9 %all_to_all.11.back_ref = bf16[32,2,1408]{2,1,0:T(2,128)(2,1)S(1)} all-to-all(bf16[32,2,1408]{2,1,0:T(2,128)(2,1)S(1)} %get-tuple-element.31), channel_id=1, replica_groups=mesh['img'=16,'tok'=2] {'tok','img'}, dimensions={0} | all-to-all | bytes 360448 | tf_op jit(solution)/shard_map/all_to_all | solution.py:286
  32.0 0.5 %shard_map.111 = (f32[8,1408]{1,0:T(8,128)S(1)}, bf16[8,1280]{1,0:T(8,128)(2,1)S(1)}, bf16[16,128]{1,0:T(8,128)(2,1)S(1)}, bf16[16,1280]{1,0:T(8,128)(2,1)S(1)}, f32[1,128]{1,0:T(1,128)S(1)}) custom-call(bf16[32,2,1408]{2,1,0:T(2,128)(2,1)S(1)} %all_to_all.11.back_ref, bf16[1,128,1280]{2,1,0:T(8,128)(2,1)S(1)} %copy-done.2, ...), custom_call_target="tpu_custom_call" | custom-call | flops 10000000 | bytes 860704 | tf_op jit(solution)/shard_map/pallas_call | solution.py:261
  32.6 1.2 %collective-permute-start.2 = (bf16[8,1408]{1,0:T(8,128)(2,1)S(1)}, bf16[8,1408]{1,0:T(8,128)(2,1)S(1)}, u32[]{:S(2)}, u32[]{:S(2)}) collective-permute-start(bf16[8,1408]{1,0:T(8,128)(2,1)S(1)} %convert_element_type.30), channel_id=1, source_target_pairs={{0,5},{1,4},{2,7},{3,6},{4,1},{5,0},{6,3},{7,2},{8,13},{9,12},{10,... | collective-permute-start | bytes 67592 | tf_op jit(solution)/shard_map/ppermute | solution.py:290
  33.7 1.4 %collective-permute-start = (bf16[8,1408]{1,0:T(8,128)(2,1)S(1)}, bf16[8,1408]{1,0:T(8,128)(2,1)S(1)}, u32[]{:S(2)}, u32[]{:S(2)}) collective-permute-start(bf16[8,1408]{1,0:T(8,128)(2,1)S(1)} %convert_element_type.30), channel_id=1, source_target_pairs={{0,4},{1,5},{2,6},{3,7},{4,0},{5,1},{6,2},{7,3},{8,12},{9,13},{10,... | collective-permute-start | bytes 67592 | tf_op jit(solution)/shard_map/ppermute | solution.py:290
  35.1 1.0 %collective-permute-start.1 = (bf16[8,1408]{1,0:T(8,128)(2,1)S(1)}, bf16[8,1408]{1,0:T(8,128)(2,1)S(1)}, u32[]{:S(2)}, u32[]{:S(2)}) collective-permute-start(bf16[8,1408]{1,0:T(8,128)(2,1)S(1)} %convert_element_type.30), channel_id=1, source_target_pairs={{0,1},{1,0},{2,3},{3,2},{4,5},{5,4},{6,7},{7,6},{8,9},{9,8},{10,11... | collective-permute-start | bytes 67592 | tf_op jit(solution)/shard_map/ppermute | solution.py:290
  36.1 1.8 %shard_map.112 = bf16[1,1280,1024]{2,1,0:T(8,128)(2,1)} custom-call(bf16[16,1280]{1,0:T(8,128)(2,1)S(1)} %get-tuple-element.35.left_ref, bf16[16,1024]{1,0:T(8,128)(2,1)S(1)} %get-tuple-element.36.right_ref), custom_call_target="tpu_custom_call" | custom-call | flops 1000000000 | bytes 73728 | tf_op jit(solution)/shard_map/pallas_call | solution.py:261
  38.0 0.0 collective-permute-done.2
  38.0 0.0 collective-permute-done
  38.0 0.9 %collective-permute-done.1 = bf16[8,1408]{1,0:T(8,128)(2,1)S(1)} collective-permute-done((bf16[8,1408]{1,0:T(8,128)(2,1)S(1)}, bf16[8,1408]{1,0:T(8,128)(2,1)S(1)}, u32[]{:S(2)}, u32[]{:S(2)}) %collective-permute-start.1) | collective-permute-done | bytes 22560 | tf_op jit(solution)/shard_map/ppermute | solution.py:290
  38.9 1.5 %collective-permute-start.5 = (bf16[8,1408]{1,0:T(8,128)(2,1)S(1)}, bf16[8,1408]{1,0:T(8,128)(2,1)S(1)}, u32[]{:S(2)}, u32[]{:S(2)}) collective-permute-start(bf16[8,1408]{1,0:T(8,128)(2,1)S(1)} %add_convert_fusion), channel_id=1, source_target_pairs={{0,24},{1,25},{2,26},{3,27},{4,28},{5,29},{6,30},{7,31},{8,16},{9,... | collective-permute-start | bytes 67592 | tf_op jit(solution)/shard_map/ppermute | solution.py:290
  40.4 0.7 %collective-permute-start.3 = (bf16[8,1408]{1,0:T(8,128)(2,1)S(1)}, bf16[8,1408]{1,0:T(8,128)(2,1)S(1)}, u32[]{:S(2)}, u32[]{:S(2)}) collective-permute-start(bf16[8,1408]{1,0:T(8,128)(2,1)S(1)} %add_convert_fusion), channel_id=1, source_target_pairs={{0,16},{1,17},{2,18},{3,19},{4,20},{5,21},{6,22},{7,23},{8,24},{9,... | collective-permute-start | bytes 67592 | tf_op jit(solution)/shard_map/ppermute | solution.py:290
  41.1 2.3 %collective-permute-start.4 = (bf16[8,1408]{1,0:T(8,128)(2,1)S(1)}, bf16[8,1408]{1,0:T(8,128)(2,1)S(1)}, u32[]{:S(2)}, u32[]{:S(2)}) collective-permute-start(bf16[8,1408]{1,0:T(8,128)(2,1)S(1)} %add_convert_fusion), channel_id=1, source_target_pairs={{0,8},{1,9},{2,10},{3,11},{4,12},{5,13},{6,14},{7,15},{8,0},{9,1},... | collective-permute-start | bytes 67592 | tf_op jit(solution)/shard_map/ppermute | solution.py:290
  43.4 1.9 %shard_map.113 = bf16[1,1024,1280]{2,1,0:T(8,128)(2,1)} custom-call(bf16[16,1024]{1,0:T(8,128)(2,1)S(1)} %get-tuple-element.38.left_ref, bf16[16,1280]{1,0:T(8,128)(2,1)S(1)} %get-tuple-element.39.right_ref), custom_call_target="tpu_custom_call" | custom-call | flops 1000000000 | bytes 73728 | tf_op jit(solution)/shard_map/pallas_call | solution.py:261
  45.3 0.0 collective-permute-done.5
  45.3 0.0 collective-permute-done.4
  45.4 0.1 collective-permute-start.6
  45.5 1.1 %shard_map.114 = (bf16[1,128,1280]{2,1,0:T(8,128)(2,1)}, bf16[1,128,1280]{2,1,0:T(8,128)(2,1)}) custom-call(bf16[1,128,1280]{2,1,0:T(8,128)(2,1)S(1)} %copy-done.2, f32[8,128]{1,0:T(8,128)S(1)} %get-tuple-element.32.logit_ref, bf16[8,1280]{1,0:T(8,128)(2,1)S(1)} %get-tuple-element.41.outs_ref, bf16[16,128]{1,0:T(8,128)(2,1)S(1)} %get-tuple-element.42.coef_ref, ...), custom_call_target="tpu_custom_call" | custom-call | flops 10000000 | bytes 397824 | tf_op jit(solution)/shard_map/pallas_call | solution.py:261
  46.6 0.1 collective-permute-done.6.other_ref
  46.7 0.6 %shard_map.115 = (f32[8,1280]{1,0:T(8,128)}, f32[1,8]{1,0:T(1,128)}) custom-call(f32[8,1408]{1,0:T(8,128)S(1)} %add_add_fusion.mine_ref, f32[8,1408]{1,0:T(8,128)S(1)} %collective-permute-done.6.other_ref), custom_call_target="tpu_custom_call" | custom-call | flops 10000000 | bytes 90112 | tf_op jit(solution)/shard_map/pallas_call | solution.py:261
  (14 shorter events, 0.1 us)
Async XLA Ops:
  0.6 17.8 %copy-start = (bf16[1,1280,1024]{2,1,0:T(8,128)(2,1)S(1)}, bf16[1,1280,1024]{2,1,0:T(8,128)(2,1)}, u32[]{:S(2)}) copy-start(bf16[1,1280,1024]{2,1,0:T(8,128)(2,1)} %one_ref.1) | copy-start | bytes 7864324
  0.6 17.8 %copy-start.1 = (bf16[1,1024,1280]{2,1,0:T(8,128)(2,1)S(1)}, bf16[1,1024,1280]{2,1,0:T(8,128)(2,1)}, u32[]{:S(2)}) copy-start(bf16[1,1024,1280]{2,1,0:T(8,128)(2,1)} %two_ref.1) | copy-start | bytes 7864324
  18.5 13.5 %copy-start.2 = (bf16[1,128,1280]{2,1,0:T(8,128)(2,1)S(1)}, bf16[1,128,1280]{2,1,0:T(8,128)(2,1)}, u32[]{:S(2)}) copy-start(bf16[1,128,1280]{2,1,0:T(8,128)(2,1)} %tok_ref.3) | copy-start | bytes 983044
  18.5 13.5 %copy-start.3 = (bf16[1,128,1280]{2,1,0:T(8,128)(2,1)S(1)}, bf16[1,128,1280]{2,1,0:T(8,128)(2,1)}, u32[]{:S(2)}) copy-start(bf16[1,128,1280]{2,1,0:T(8,128)(2,1)} %grad_ref.1) | copy-start | bytes 983044
  18.5 13.5 %copy-start.4 = (bf16[1280,8]{0,1:T(8,128)(2,1)S(1)}, bf16[1280,8]{0,1:T(8,128)(2,1)}, u32[]{:S(2)}) copy-start(bf16[1280,8]{0,1:T(8,128)(2,1)} %param.8) | copy-start | bytes 61444
  18.5 13.5 %copy-start.5 = (f32[8]{0:T(128)S(1)}, f32[8]{0:T(128)}, u32[]{:S(2)}) copy-start(f32[8]{0:T(128)} %param.9) | copy-start | bytes 100
  32.6 5.4 %collective-permute-start.2 = (bf16[8,1408]{1,0:T(8,128)(2,1)S(1)}, bf16[8,1408]{1,0:T(8,128)(2,1)S(1)}, u32[]{:S(2)}, u32[]{:S(2)}) collective-permute-start(bf16[8,1408]{1,0:T(8,128)(2,1)S(1)} %convert_element_type.30), channel_id=1, source_target_pairs={{0,5},{1,4},{2,7},{3,6},{4,1},{5,0},{6,3},{7,2},{8,13},{9,12},{10,... | collective-permute-start | bytes 67592 | tf_op jit(solution)/shard_map/ppermute | solution.py:290
  33.7 4.3 %collective-permute-start = (bf16[8,1408]{1,0:T(8,128)(2,1)S(1)}, bf16[8,1408]{1,0:T(8,128)(2,1)S(1)}, u32[]{:S(2)}, u32[]{:S(2)}) collective-permute-start(bf16[8,1408]{1,0:T(8,128)(2,1)S(1)} %convert_element_type.30), channel_id=1, source_target_pairs={{0,4},{1,5},{2,6},{3,7},{4,0},{5,1},{6,2},{7,3},{8,12},{9,13},{10,... | collective-permute-start | bytes 67592 | tf_op jit(solution)/shard_map/ppermute | solution.py:290
  35.1 3.8 %collective-permute-start.1 = (bf16[8,1408]{1,0:T(8,128)(2,1)S(1)}, bf16[8,1408]{1,0:T(8,128)(2,1)S(1)}, u32[]{:S(2)}, u32[]{:S(2)}) collective-permute-start(bf16[8,1408]{1,0:T(8,128)(2,1)S(1)} %convert_element_type.30), channel_id=1, source_target_pairs={{0,1},{1,0},{2,3},{3,2},{4,5},{5,4},{6,7},{7,6},{8,9},{9,8},{10,11... | collective-permute-start | bytes 67592 | tf_op jit(solution)/shard_map/ppermute | solution.py:290
  38.9 6.4 %collective-permute-start.5 = (bf16[8,1408]{1,0:T(8,128)(2,1)S(1)}, bf16[8,1408]{1,0:T(8,128)(2,1)S(1)}, u32[]{:S(2)}, u32[]{:S(2)}) collective-permute-start(bf16[8,1408]{1,0:T(8,128)(2,1)S(1)} %add_convert_fusion), channel_id=1, source_target_pairs={{0,24},{1,25},{2,26},{3,27},{4,28},{5,29},{6,30},{7,31},{8,16},{9,... | collective-permute-start | bytes 67592 | tf_op jit(solution)/shard_map/ppermute | solution.py:290
  40.4 4.9 %collective-permute-start.3 = (bf16[8,1408]{1,0:T(8,128)(2,1)S(1)}, bf16[8,1408]{1,0:T(8,128)(2,1)S(1)}, u32[]{:S(2)}, u32[]{:S(2)}) collective-permute-start(bf16[8,1408]{1,0:T(8,128)(2,1)S(1)} %add_convert_fusion), channel_id=1, source_target_pairs={{0,16},{1,17},{2,18},{3,19},{4,20},{5,21},{6,22},{7,23},{8,24},{9,... | collective-permute-start | bytes 67592 | tf_op jit(solution)/shard_map/ppermute | solution.py:290
  41.1 4.3 %collective-permute-start.4 = (bf16[8,1408]{1,0:T(8,128)(2,1)S(1)}, bf16[8,1408]{1,0:T(8,128)(2,1)S(1)}, u32[]{:S(2)}, u32[]{:S(2)}) collective-permute-start(bf16[8,1408]{1,0:T(8,128)(2,1)S(1)} %add_convert_fusion), channel_id=1, source_target_pairs={{0,8},{1,9},{2,10},{3,11},{4,12},{5,13},{6,14},{7,15},{8,0},{9,1},... | collective-permute-start | bytes 67592 | tf_op jit(solution)/shard_map/ppermute | solution.py:290
  45.4 1.3 %collective-permute-start.6 = (f32[8,1408]{1,0:T(8,128)S(1)}, f32[8,1408]{1,0:T(8,128)S(1)}, u32[]{:S(2)}, u32[]{:S(2)}) collective-permute-start(f32[8,1408]{1,0:T(8,128)S(1)} %add_add_fusion.mine_ref), channel_id=1, source_target_pairs={{0,2},{1,3},{2,0},{3,1},{4,6},{5,7},{6,4},{7,5},{8,10},{9,11},{10,... | collective-permute-start | bytes 135176 | tf_op jit(solution)/shard_map/ppermute | solution.py:290

commit v14 on v13

--- a/solution.py
+++ b/solution.py
@@ -234,9 +234,12 @@
     signal_ref[...] = inv_x * inv_x * jnp.sum(product, 0, keepdims=True)
 
 
-def tail_kernel(tok_ref, logit_ref, outs_ref, coef_ref, mix_ref, signal_ref, combined_ref, grads_ref):
+def combined_kernel(logit_ref, outs_ref, combined_ref):
     _, comb = softmax(logit_ref[...])
     combined_ref[0] = dot(comb.astype(BF), outs_ref[...], ((0,), (0,))).astype(BF)
+
+
+def tail_kernel(tok_ref, coef_ref, mix_ref, signal_ref, grads_ref):
     signal = signal_ref[...]
     column = jnp.transpose(jnp.broadcast_to(signal, (LANES, signal.shape[1])))[:, :1]
     grads = dot(coef_ref[...], mix_ref[...], ((0,), (0,)))
@@ -349,13 +352,10 @@
          ((2 * experts, width), BF), ((1, tok_rows), F32)],
         back, tokens, grad_out, logit, inv_x, router_t, scale_row,
     )
-    combined, grad_tokens = call(
-        tail_kernel,
-        [(tokens.shape, BF), (tokens.shape, BF)],
-        tokens, logit, ys, coef, mix, signal,
-    )
-    mine, other, (grad_w_in, grad_w_out, (combined, grad_tokens)) = sum_everywhere(
-        sums, devices, [grad_w_in, grad_w_out, (combined, grad_tokens)]
+    (combined,) = call(combined_kernel, [(tokens.shape, BF)], logit, ys)
+    (grad_tokens,) = call(tail_kernel, [(tokens.shape, BF)], tokens, coef, mix, signal)
+    mine, other, ((grad_w_in, combined), grad_w_out, grad_tokens) = sum_everywhere(
+        sums, devices, [(grad_w_in, combined), grad_w_out, grad_tokens]
     )
     grad_router, grad_scale = call(
         last_kernel, [((experts, width), F32), ((1, experts), F32)], mine, other

time: 47.5 us -> 47.8 us (level)
  Pallas kernels: 10.6 us -> 11.5 us
  waiting for transfers between devices: 1.03 us -> 0.48 us
    pallas_call x7 -> x8, Pallas kernels: 10.6 us -> 11.5 us  [call(): pl.pallas_call(kernel, out_shape=[jax.ShapeDtypeStruct(shape, dtype) for...]
    ppermute x7, waiting for transfers between devices: 1.03 us -> 0.48 us  [pair(): return lax.ppermute(term, BOTH, [(d, d ^ mask) for d in range(devices)])]
  transfers between devices with their start and end apart: 7 -> 7, of which waited for: 2 -> 2; matrix products, arithmetic and copies ran while one was open for 0% -> 0% of each run, Pallas kernels for 10% -> 12%
where the time goes in v14:
time: 47.8 us; the launch traced here: 47.6 us
  blocking collectives  26.8 us (56%)
  Pallas kernels  11.5 us (24%)
  starting transfers between devices  8.08 us (17%)
  between operations  0.75 us (2%)
  waiting for transfers between devices  0.48 us (1%)
    all_to_all x2, blocking collectives, exchange(): return lax.all_to_all(block, axes, split_axis=0, concat_axis=0, tiled=True)  26.8 us
    pallas_call x8, Pallas kernels, call(): pl.pallas_call(kernel, out_shape=[jax.ShapeDtypeStruct(shape, dtype) for...  11.5 us
    ppermute x7, starting transfers between devices, pair(): return lax.ppermute(term, BOTH, [(d, d ^ mask) for d in range(devices)])  8.08 us
  transfers between devices with their start and end apart: 7, of which 2 were waited for; matrix products, arithmetic and copies ran while one was open for 0% of the time, Pallas kernels for 12%

profile of v14, /device:TPU:0, one launch (start us, length us, event | category | flops | bytes accessed | tf_op | source)
XLA Modules:
  0.0 47.6 jit_solution(15362539304048065980)
XLA Ops:
  0.7 2.0 %shard_map.109 = (bf16[32,2,1408]{2,1,0:T(2,128)(2,1)S(1)}, f32[8,128]{1,0:T(8,128)S(1)}, f32[1,128]{1,0:T(1,128)S(1)}) custom-call(bf16[1,128,1280]{2,1,0:T(8,128)(2,1)} %tok_ref.3, bf16[1,128,1280]{2,1,0:T(8,128)(2,1)} %grad_ref.1, bf16[8,1280]{1,0:T(8,128)(2,1)} %bitcast.4, f32[1,8]{1,0:T(1,128)} %bitcast.6), custom_call_target="tpu_custom_call" | custom-call | flops 4000000000 | bytes 675872 | tf_op jit(solution)/shard_map/pallas_call | solution.py:264
  2.6 15.8 %all_to_all.10.got_ref = bf16[32,2,1408]{2,1,0:T(2,128)(2,1)S(1)} all-to-all(bf16[32,2,1408]{2,1,0:T(2,128)(2,1)S(1)} %get-tuple-element.28), channel_id=1, replica_groups=mesh['img'=16,'tok'=2] {'tok','img'}, dimensions={0} | all-to-all | bytes 360448 | tf_op jit(solution)/shard_map/all_to_all | solution.py:289
  18.5 0.0 copy-start.4
  18.5 0.0 copy-start.5
  18.5 2.6 %shard_map.110 = (bf16[32,2,1408]{2,1,0:T(2,128)(2,1)S(1)}, bf16[16,1280]{1,0:T(8,128)(2,1)S(1)}, bf16[16,1280]{1,0:T(8,128)(2,1)S(1)}, bf16[16,1024]{1,0:T(8,128)(2,1)S(1)}, bf16[16,1024]{1,0:T(8,128)(2,1)S(1)}) custom-call(bf16[32,2,1408]{2,1,0:T(2,128)(2,1)S(1)} %all_to_all.10.got_ref, bf16[1,1280,1024]{2,1,0:T(8,128)(2,1)S(1)} %copy-done, ...), custom_call_target="tpu_custom_call" | custom-call | flops 1000000000 | bytes 5423104 | tf_op jit(solution)/shard_map/pallas_call | solution.py:264
  21.1 10.9 %all_to_all.11.back_ref = bf16[32,2,1408]{2,1,0:T(2,128)(2,1)S(1)} all-to-all(bf16[32,2,1408]{2,1,0:T(2,128)(2,1)S(1)} %get-tuple-element.29), channel_id=1, replica_groups=mesh['img'=16,'tok'=2] {'tok','img'}, dimensions={0} | all-to-all | bytes 360448 | tf_op jit(solution)/shard_map/all_to_all | solution.py:289
  32.0 0.5 %shard_map.111 = (f32[8,1408]{1,0:T(8,128)S(1)}, bf16[8,1280]{1,0:T(8,128)(2,1)S(1)}, bf16[16,128]{1,0:T(8,128)(2,1)S(1)}, bf16[16,1280]{1,0:T(8,128)(2,1)S(1)}, f32[1,128]{1,0:T(1,128)S(1)}) custom-call(bf16[32,2,1408]{2,1,0:T(2,128)(2,1)S(1)} %all_to_all.11.back_ref, bf16[1,128,1280]{2,1,0:T(8,128)(2,1)S(1)} %copy-done.2, ...), custom_call_target="tpu_custom_call" | custom-call | flops 10000000 | bytes 860704 | tf_op jit(solution)/shard_map/pallas_call | solution.py:264
  32.6 1.2 %collective-permute-start = (bf16[8,1408]{1,0:T(8,128)(2,1)S(1)}, bf16[8,1408]{1,0:T(8,128)(2,1)S(1)}, u32[]{:S(2)}, u32[]{:S(2)}) collective-permute-start(bf16[8,1408]{1,0:T(8,128)(2,1)S(1)} %convert_element_type.30), channel_id=1, source_target_pairs={{0,5},{1,4},{2,7},{3,6},{4,1},{5,0},{6,3},{7,2},{8,13},{9,12},{10,... | collective-permute-start | bytes 67592 | tf_op jit(solution)/shard_map/ppermute | solution.py:293
  33.7 1.4 %collective-permute-start.1 = (bf16[8,1408]{1,0:T(8,128)(2,1)S(1)}, bf16[8,1408]{1,0:T(8,128)(2,1)S(1)}, u32[]{:S(2)}, u32[]{:S(2)}) collective-permute-start(bf16[8,1408]{1,0:T(8,128)(2,1)S(1)} %convert_element_type.30), channel_id=1, source_target_pairs={{0,4},{1,5},{2,6},{3,7},{4,0},{5,1},{6,2},{7,3},{8,12},{9,13},{10,... | collective-permute-start | bytes 67592 | tf_op jit(solution)/shard_map/ppermute | solution.py:293
  35.1 1.0 %collective-permute-start.2 = (bf16[8,1408]{1,0:T(8,128)(2,1)S(1)}, bf16[8,1408]{1,0:T(8,128)(2,1)S(1)}, u32[]{:S(2)}, u32[]{:S(2)}) collective-permute-start(bf16[8,1408]{1,0:T(8,128)(2,1)S(1)} %convert_element_type.30), channel_id=1, source_target_pairs={{0,1},{1,0},{2,3},{3,2},{4,5},{5,4},{6,7},{7,6},{8,9},{9,8},{10,11... | collective-permute-start | bytes 67592 | tf_op jit(solution)/shard_map/ppermute | solution.py:293
  36.1 1.8 %shard_map.112 = bf16[1,1280,1024]{2,1,0:T(8,128)(2,1)} custom-call(bf16[16,1280]{1,0:T(8,128)(2,1)S(1)} %get-tuple-element.33.left_ref, bf16[16,1024]{1,0:T(8,128)(2,1)S(1)} %get-tuple-element.34.right_ref), custom_call_target="tpu_custom_call" | custom-call | flops 1000000000 | bytes 73728 | tf_op jit(solution)/shard_map/pallas_call | solution.py:264
  38.0 1.0 %shard_map.113 = bf16[1,128,1280]{2,1,0:T(8,128)(2,1)} custom-call(f32[8,128]{1,0:T(8,128)S(1)} %get-tuple-element.30.logit_ref, bf16[8,1280]{1,0:T(8,128)(2,1)S(1)} %get-tuple-element.35.outs_ref), custom_call_target="tpu_custom_call" | custom-call | flops 10000000 | bytes 24576 | tf_op jit(solution)/shard_map/pallas_call | solution.py:264
  39.0 0.0 collective-permute-done
  39.0 1.9 %collective-permute-start.5 = (bf16[8,1408]{1,0:T(8,128)(2,1)S(1)}, bf16[8,1408]{1,0:T(8,128)(2,1)S(1)}, u32[]{:S(2)}, u32[]{:S(2)}) collective-permute-start(bf16[8,1408]{1,0:T(8,128)(2,1)S(1)} %add_convert_fusion), channel_id=1, source_target_pairs={{0,24},{1,25},{2,26},{3,27},{4,28},{5,29},{6,30},{7,31},{8,16},{9,... | collective-permute-start | bytes 67592 | tf_op jit(solution)/shard_map/ppermute | solution.py:293
  41.0 0.1 collective-permute-start.3
  41.1 2.4 %collective-permute-start.4 = (bf16[8,1408]{1,0:T(8,128)(2,1)S(1)}, bf16[8,1408]{1,0:T(8,128)(2,1)S(1)}, u32[]{:S(2)}, u32[]{:S(2)}) collective-permute-start(bf16[8,1408]{1,0:T(8,128)(2,1)S(1)} %add_convert_fusion), channel_id=1, source_target_pairs={{0,8},{1,9},{2,10},{3,11},{4,12},{5,13},{6,14},{7,15},{8,0},{9,1},... | collective-permute-start | bytes 67592 | tf_op jit(solution)/shard_map/ppermute | solution.py:293
  43.5 1.9 %shard_map.114 = bf16[1,1024,1280]{2,1,0:T(8,128)(2,1)} custom-call(bf16[16,1024]{1,0:T(8,128)(2,1)S(1)} %get-tuple-element.38.left_ref, bf16[16,1280]{1,0:T(8,128)(2,1)S(1)} %get-tuple-element.39.right_ref), custom_call_target="tpu_custom_call" | custom-call | flops 1000000000 | bytes 73728 | tf_op jit(solution)/shard_map/pallas_call | solution.py:264
  45.4 0.0 collective-permute-done.5
  45.4 0.3 collective-permute-done.3
  45.7 0.0 collective-permute-done.4
  45.7 0.1 collective-permute-start.6
  45.8 1.0 %shard_map.115 = bf16[1,128,1280]{2,1,0:T(8,128)(2,1)} custom-call(bf16[1,128,1280]{2,1,0:T(8,128)(2,1)S(1)} %copy-done.2, bf16[16,128]{1,0:T(8,128)(2,1)S(1)} %get-tuple-element.41.coef_ref, bf16[16,1280]{1,0:T(8,128)(2,1)S(1)} %get-tuple-element.42.mix_ref, f32[1,128]{1,0:T(1,128)S(1)} %get-tuple-element.43.signal_ref), custom_call_target="tpu_custom_call" | custom-call | flops 10000000 | bytes 373248 | tf_op jit(solution)/shard_map/pallas_call | solution.py:264
  46.8 0.2 collective-permute-done.6.other_ref
  47.0 0.6 %shard_map.116 = (f32[8,1280]{1,0:T(8,128)}, f32[1,8]{1,0:T(1,128)}) custom-call(f32[8,1408]{1,0:T(8,128)S(1)} %add_add_fusion.mine_ref, f32[8,1408]{1,0:T(8,128)S(1)} %collective-permute-done.6.other_ref), custom_call_target="tpu_custom_call" | custom-call | flops 10000000 | bytes 90112 | tf_op jit(solution)/shard_map/pallas_call | solution.py:264
  (15 shorter events, 0.1 us)
Async XLA Ops:
  0.6 17.8 %copy-start = (bf16[1,1280,1024]{2,1,0:T(8,128)(2,1)S(1)}, bf16[1,1280,1024]{2,1,0:T(8,128)(2,1)}, u32[]{:S(2)}) copy-start(bf16[1,1280,1024]{2,1,0:T(8,128)(2,1)} %one_ref.1) | copy-start | bytes 7864324
  0.6 17.8 %copy-start.1 = (bf16[1,1024,1280]{2,1,0:T(8,128)(2,1)S(1)}, bf16[1,1024,1280]{2,1,0:T(8,128)(2,1)}, u32[]{:S(2)}) copy-start(bf16[1,1024,1280]{2,1,0:T(8,128)(2,1)} %two_ref.1) | copy-start | bytes 7864324
  18.5 13.5 %copy-start.2 = (bf16[1,128,1280]{2,1,0:T(8,128)(2,1)S(1)}, bf16[1,128,1280]{2,1,0:T(8,128)(2,1)}, u32[]{:S(2)}) copy-start(bf16[1,128,1280]{2,1,0:T(8,128)(2,1)} %tok_ref.3) | copy-start | bytes 983044
  18.5 13.5 %copy-start.3 = (bf16[1,128,1280]{2,1,0:T(8,128)(2,1)S(1)}, bf16[1,128,1280]{2,1,0:T(8,128)(2,1)}, u32[]{:S(2)}) copy-start(bf16[1,128,1280]{2,1,0:T(8,128)(2,1)} %grad_ref.1) | copy-start | bytes 983044
  18.5 13.5 %copy-start.4 = (bf16[1280,8]{0,1:T(8,128)(2,1)S(1)}, bf16[1280,8]{0,1:T(8,128)(2,1)}, u32[]{:S(2)}) copy-start(bf16[1280,8]{0,1:T(8,128)(2,1)} %param.8) | copy-start | bytes 61444
  18.5 13.5 %copy-start.5 = (f32[8]{0:T(128)S(1)}, f32[8]{0:T(128)}, u32[]{:S(2)}) copy-start(f32[8]{0:T(128)} %param.9) | copy-start | bytes 100
  32.6 6.4 %collective-permute-start = (bf16[8,1408]{1,0:T(8,128)(2,1)S(1)}, bf16[8,1408]{1,0:T(8,128)(2,1)S(1)}, u32[]{:S(2)}, u32[]{:S(2)}) collective-permute-start(bf16[8,1408]{1,0:T(8,128)(2,1)S(1)} %convert_element_type.30), channel_id=1, source_target_pairs={{0,5},{1,4},{2,7},{3,6},{4,1},{5,0},{6,3},{7,2},{8,13},{9,12},{10,... | collective-permute-start | bytes 67592 | tf_op jit(solution)/shard_map/ppermute | solution.py:293
  33.7 5.3 %collective-permute-start.1 = (bf16[8,1408]{1,0:T(8,128)(2,1)S(1)}, bf16[8,1408]{1,0:T(8,128)(2,1)S(1)}, u32[]{:S(2)}, u32[]{:S(2)}) collective-permute-start(bf16[8,1408]{1,0:T(8,128)(2,1)S(1)} %convert_element_type.30), channel_id=1, source_target_pairs={{0,4},{1,5},{2,6},{3,7},{4,0},{5,1},{6,2},{7,3},{8,12},{9,13},{10,... | collective-permute-start | bytes 67592 | tf_op jit(solution)/shard_map/ppermute | solution.py:293
  35.1 3.9 %collective-permute-start.2 = (bf16[8,1408]{1,0:T(8,128)(2,1)S(1)}, bf16[8,1408]{1,0:T(8,128)(2,1)S(1)}, u32[]{:S(2)}, u32[]{:S(2)}) collective-permute-start(bf16[8,1408]{1,0:T(8,128)(2,1)S(1)} %convert_element_type.30), channel_id=1, source_target_pairs={{0,1},{1,0},{2,3},{3,2},{4,5},{5,4},{6,7},{7,6},{8,9},{9,8},{10,11... | collective-permute-start | bytes 67592 | tf_op jit(solution)/shard_map/ppermute | solution.py:293
  39.0 6.4 %collective-permute-start.5 = (bf16[8,1408]{1,0:T(8,128)(2,1)S(1)}, bf16[8,1408]{1,0:T(8,128)(2,1)S(1)}, u32[]{:S(2)}, u32[]{:S(2)}) collective-permute-start(bf16[8,1408]{1,0:T(8,128)(2,1)S(1)} %add_convert_fusion), channel_id=1, source_target_pairs={{0,24},{1,25},{2,26},{3,27},{4,28},{5,29},{6,30},{7,31},{8,16},{9,... | collective-permute-start | bytes 67592 | tf_op jit(solution)/shard_map/ppermute | solution.py:293
  41.0 4.7 %collective-permute-start.3 = (bf16[8,1408]{1,0:T(8,128)(2,1)S(1)}, bf16[8,1408]{1,0:T(8,128)(2,1)S(1)}, u32[]{:S(2)}, u32[]{:S(2)}) collective-permute-start(bf16[8,1408]{1,0:T(8,128)(2,1)S(1)} %add_convert_fusion), channel_id=1, source_target_pairs={{0,16},{1,17},{2,18},{3,19},{4,20},{5,21},{6,22},{7,23},{8,24},{9,... | collective-permute-start | bytes 67592 | tf_op jit(solution)/shard_map/ppermute | solution.py:293
  41.1 4.6 %collective-permute-start.4 = (bf16[8,1408]{1,0:T(8,128)(2,1)S(1)}, bf16[8,1408]{1,0:T(8,128)(2,1)S(1)}, u32[]{:S(2)}, u32[]{:S(2)}) collective-permute-start(bf16[8,1408]{1,0:T(8,128)(2,1)S(1)} %add_convert_fusion), channel_id=1, source_target_pairs={{0,8},{1,9},{2,10},{3,11},{4,12},{5,13},{6,14},{7,15},{8,0},{9,1},... | collective-permute-start | bytes 67592 | tf_op jit(solution)/shard_map/ppermute | solution.py:293
  45.7 1.3 %collective-permute-start.6 = (f32[8,1408]{1,0:T(8,128)S(1)}, f32[8,1408]{1,0:T(8,128)S(1)}, u32[]{:S(2)}, u32[]{:S(2)}) collective-permute-start(f32[8,1408]{1,0:T(8,128)S(1)} %add_add_fusion.mine_ref), channel_id=1, source_target_pairs={{0,2},{1,3},{2,0},{3,1},{4,6},{5,7},{6,4},{7,5},{8,10},{9,11},{10,... | collective-permute-start | bytes 135176 | tf_op jit(solution)/shard_map/ppermute | solution.py:293
